TPU v7x, 32 devices: a whole 2x2x4 slice. The times are simulated.
32 devices in a mesh: groups: 2 (over y), rows: 4 (over z), samples: 4 (over x, core).
Axes of the slice: x: 2, y: 2, z: 4, core: 2. Of those that a mesh axis runs over, the one named last changes fastest.
Arguments:
- ancestor: float32 [4096, 512], P(('groups', 'rows'), 'samples'), parts along dimension 0, may hold values from -6 to 6
- panels: float32 [2, 2, 1024, 256], P(None, None, 'rows', 'samples'), may hold values from -0.1875 to 0.1875
- row_map: int32 [2, 1024], P(None, 'rows'), may hold values from 0 to 511
- offsets: int32 [2], replicated, may hold values from 0 to 1536
- noise: float32 [4096, 512], P('groups', 'samples'), parts along dimension 0, may hold values from -6 to 6
- inverse: float32 [2, 2, 256, 256], P(None, None, 'rows'), as said below
- inner_link: float32 [2, 256, 256], P(None, 'rows'), may hold values from -0.375 to 0.375
- cross_link: float32 [2, 2, 256, 256], P(None, None, 'rows'), may hold values from -0.25 to 0.25
Outputs:
- solved: float32 [2, 2, 256, 1024], P(None, None, 'rows', ('groups', 'samples')), parts along dimension 3
There are 2 independent parts, one for each index of `groups`. A program takes and returns all parts, laid end to end along the dimension named above; an argument that names none is the same for every part. Nothing has to cross between parts.
Inputs may be any that keep to these rules, and one draw needn't show every extreme that they name: inverse[p, b] is upper triangular: entry (i, j) is zero for j < i, and its diagonal is positive.
All inputs are finite; a program needn't handle non-finite values.
Results may differ from a plain program's by a relative error of at most 0.0003.
Values sent between devices are 32-bit elements; how exact they have to be, the bound alone decides.
No kernel may reach another device: no remote copies, remote signals or barrier semaphores. Data moves between devices by JAX's collectives and lax.ppermute only.
A program may use at most 64 MiB of HBM per device.

v0:
```python
import jax
import jax.numpy as jnp
from jax import lax
from jax.sharding import PartitionSpec as P


def product(left, right):
    return jnp.dot(left, right, precision=lax.Precision.HIGHEST, preferred_element_type=jnp.float32)


def column_terms(local_panel, front_rows):
    return product(lax.all_gather(local_panel, "samples", axis=1, tiled=True).T, front_rows)


def apply_inverse(target, partial_value, inverse_rows):
    rows_here = inverse_rows.shape[0]
    share = lax.psum_scatter(partial_value, "rows", scatter_dimension=0, tiled=True)
    first_own = lax.axis_index("rows") * rows_here
    residue = lax.dynamic_slice_in_dim(target, first_own, rows_here, 0) - share
    return product(inverse_rows, lax.all_gather(residue, "rows", axis=0, tiled=True))


def local(ancestor, panels, row_map, offsets, noise, inverse, inner_link, cross_link):
    block_rows = inverse.shape[3]
    solved = [[None, None], [None, None]]
    for which_panel in (1, 0):
        front_rows = jnp.take(ancestor, row_map[which_panel], axis=0)
        window = lax.dynamic_slice_in_dim(noise, offsets[which_panel], 2 * block_rows, 0)
        for which_block in (1, 0):
            partial_value = column_terms(panels[which_panel, which_block], front_rows)
            if which_block == 0:
                partial_value = partial_value + product(
                    inner_link[which_panel].T, solved[which_panel][1]
                )
            if which_panel == 0:
                for earlier in (0, 1):
                    partial_value = partial_value + product(
                        cross_link[which_block, earlier].T, solved[1][earlier]
                    )
            target = window[which_block * block_rows : (which_block + 1) * block_rows]
            solved[which_panel][which_block] = apply_inverse(
                target, partial_value, inverse[which_panel, which_block]
            )
    return jnp.stack([jnp.stack(solved[0]), jnp.stack(solved[1])])


def solution(mesh):
    placed = (
        P(("groups", "rows"), "samples"),
        P(None, None, "rows", "samples"),
        P(None, "rows"),
        P(),
        P("groups", "samples"),
        P(None, None, "rows", None),
        P(None, "rows", None),
        P(None, None, "rows", None),
    )
    return jax.shard_map(
        local,
        mesh=mesh,
        in_specs=placed,
        out_specs=P(None, None, "rows", ("groups", "samples")),
        check_vma=False,
    )
```

profile of v0, /device:TPU:0, one launch (start us, length us, event | category | flops | bytes accessed | tf_op | source)
XLA Modules:
  0.0 160.8 jit_solution(15474961298306131321)
XLA Ops:
  6.5 0.8 fusion.56
  7.3 1.0 fusion.55
  8.3 7.2 %all-gather.3 = f32[1,1,256,256]{2,3,1,0:T(8,128)S(1)} all-gather(f32[1,1,256,64]{2,3,1,0:T(8,128)S(1)} %get-tuple-element.8), channel_id=5, replica_groups=mesh['groups'=2,'rows'=4,'samples'=4] {'samples'}, dimensions={3}, use_global_device_ids=true | all-gather | bytes 327680 | tf_op jit(solution)/shard_map/all_gather | solution.py:12
  15.5 0.7 gather_fusion.1
  16.2 1.1 convolution_bitcast_fusion
  17.4 0.6 copy-done.4
  18.0 0.6 fusion.57
  18.6 5.9 %all-gather.2 = f32[1,1,256,256]{2,3,1,0:T(8,128)S(1)} all-gather(f32[1,1,256,64]{2,3,1,0:T(8,128)S(1)} %get-tuple-element.9), channel_id=4, replica_groups=mesh['groups'=2,'rows'=4,'samples'=4] {'samples'}, dimensions={3}, use_global_device_ids=true | all-gather | bytes 327680 | tf_op jit(solution)/shard_map/all_gather | solution.py:12
  24.5 6.0 %all-gather.1 = f32[1,1,256,256]{2,3,1,0:T(8,128)S(1)} all-gather(f32[1,1,256,64]{2,3,1,0:T(8,128)S(1)} %get-tuple-element.7), channel_id=3, replica_groups=mesh['groups'=2,'rows'=4,'samples'=4] {'samples'}, dimensions={3}, use_global_device_ids=true | all-gather | bytes 327680 | tf_op jit(solution)/shard_map/all_gather | solution.py:12
  32.4 5.7 %reduce-scatter.5.cloned.1.call-done = f32[64,128]{1,0:T(8,128)} async-done(((f32[256,128]{1,0:T(8,128)}), f32[64,128]{1,0:T(8,128)}) %reduce-scatter.5.cloned.1.call-update) | async-done | bytes 32784 | tf_op jit(solution)/shard_map/reduce_scatter | solution.py:17
  38.0 0.8 dynamic-slice_subtract_fusion
  38.8 13.4 %all_gather.28 = f32[256,128]{1,0:T(8,128)S(1)} all-gather(f32[64,128]{1,0:T(8,128)S(1)} %dynamic-slice_subtract_fusion), channel_id=1, replica_groups=mesh['groups'=2,'rows'=4,'samples'=4] {'rows'}, dimensions={0}, use_global_device_ids=true | all-gather | bytes 163840 | tf_op jit(solution)/shard_map/all_gather | solution.py:20
  52.4 0.7 copy-done.3
  53.5 1.1 fusion
  54.7 5.8 %all-gather = f32[1,1,256,256]{2,3,1,0:T(8,128)S(1)} all-gather(f32[1,1,256,64]{2,3,1,0:T(8,128)S(1)} %get-tuple-element.6), channel_id=2, replica_groups=mesh['groups'=2,'rows'=4,'samples'=4] {'samples'}, dimensions={3}, use_global_device_ids=true | all-gather | bytes 327680 | tf_op jit(solution)/shard_map/all_gather | solution.py:12
  61.7 0.7 gather_fusion
  63.1 0.4 fusion.23
  63.5 8.7 %reduce-scatter.7.cloned.1.call-done = f32[64,128]{1,0:T(8,128)} async-done(((f32[256,128]{1,0:T(8,128)}), f32[64,128]{1,0:T(8,128)}) %reduce-scatter.7.cloned.1.call-update) | async-done | bytes 32784 | tf_op jit(solution)/shard_map/reduce_scatter | solution.py:17
  72.2 0.8 dynamic-slice_subtract_fusion.1
  73.0 13.4 %all_gather.29 = f32[256,128]{1,0:T(8,128)S(1)} all-gather(f32[64,128]{1,0:T(8,128)S(1)} %dynamic-slice_subtract_fusion.1), channel_id=1, replica_groups=mesh['groups'=2,'rows'=4,'samples'=4] {'rows'}, dimensions={0}, use_global_device_ids=true | all-gather | bytes 163840 | tf_op jit(solution)/shard_map/all_gather | solution.py:20
  86.6 0.4 fusion.25
  87.0 1.1 fusion.2
  88.2 0.4 fusion.15
  88.6 0.4 fusion.17
  89.0 16.7 %reduce-scatter.9.cloned.1.call-done = f32[64,128]{1,0:T(8,128)} async-done(((f32[256,128]{1,0:T(8,128)}), f32[64,128]{1,0:T(8,128)}) %reduce-scatter.9.cloned.1.call-update) | async-done | bytes 32784 | tf_op jit(solution)/shard_map/reduce_scatter | solution.py:17
  105.7 0.8 dynamic-slice_subtract_fusion.2
  106.5 13.4 %all_gather.30 = f32[256,128]{1,0:T(8,128)S(1)} all-gather(f32[64,128]{1,0:T(8,128)S(1)} %dynamic-slice_subtract_fusion.2), channel_id=1, replica_groups=mesh['groups'=2,'rows'=4,'samples'=4] {'rows'}, dimensions={0}, use_global_device_ids=true | all-gather | bytes 163840 | tf_op jit(solution)/shard_map/all_gather | solution.py:20
  120.5 1.1 fusion.5
  121.7 17.5 %reduce-scatter.11.cloned.1.call-done = f32[64,128]{1,0:T(8,128)} async-done(((f32[256,128]{1,0:T(8,128)}), f32[64,128]{1,0:T(8,128)}) %reduce-scatter.11.cloned.1.call-update) | async-done | bytes 32784 | tf_op jit(solution)/shard_map/reduce_scatter | solution.py:17
  139.2 0.8 dynamic-slice_subtract_fusion.3
  140.0 13.4 %all_gather.31 = f32[256,128]{1,0:T(8,128)S(1)} all-gather(f32[64,128]{1,0:T(8,128)S(1)} %dynamic-slice_subtract_fusion.3), channel_id=1, replica_groups=mesh['groups'=2,'rows'=4,'samples'=4] {'rows'}, dimensions={0}, use_global_device_ids=true | all-gather | bytes 163840 | tf_op jit(solution)/shard_map/all_gather | solution.py:20
  153.6 0.7 pad_maximum_fusion
  (29 shorter events, 1.9 us)
Async XLA Ops:
  6.5 9.0 %copy-start = (f32[512,128]{1,0:T(8,128)S(1)}, f32[512,128]{1,0:T(8,128)}, u32[]{:S(2)}) copy-start(f32[512,128]{1,0:T(8,128)} %param.10) | copy-start | bytes 786436
  6.5 31.5 %reduce-scatter.5.cloned.1.call-start = ((), (), s32[]{:S(2)}) async-start(), calls=%async_computation.4 | async-start | bytes 163840 | tf_op jit(solution)/shard_map/reduce_scatter | solution.py:17
  17.3 0.7 copy-start.4
  17.4 54.9 %reduce-scatter.7.cloned.1.call-start = ((), (), s32[]{:S(2)}) async-start(), calls=%async_computation.5 | async-start | bytes 163840 | tf_op jit(solution)/shard_map/reduce_scatter | solution.py:17
  24.5 27.8 %copy-start.2 = (f32[2,2,64,256]{3,2,1,0:T(8,128)S(1)}, f32[2,2,64,256]{3,2,1,0:T(8,128)}, u32[]{:S(2)}) copy-start(f32[2,2,64,256]{3,2,1,0:T(8,128)} %param.15) | copy-start | bytes 786436
  52.2 0.9 copy-start.3
  54.6 51.0 %reduce-scatter.9.cloned.1.call-start = ((), (), s32[]{:S(2)}) async-start(), calls=%async_computation.6 | async-start | bytes 163840 | tf_op jit(solution)/shard_map/reduce_scatter | solution.py:17
  61.7 1.4 copy-start.1
  88.1 51.1 %reduce-scatter.11.cloned.1.call-start = ((), (), s32[]{:S(2)}) async-start(), calls=%async_computation.7 | async-start | bytes 163840 | tf_op jit(solution)/shard_map/reduce_scatter | solution.py:17
Sparse Core Ops, SparseCore 0:
  17.5 20.5 reduce-scatter.4
  54.8 17.3 reduce-scatter.6
  88.3 17.3 reduce-scatter.8
  121.8 17.3 reduce-scatter.10
where the time goes:
time: 161 us
  blocking collectives  78.3 us (49%)
  waiting for transfers between devices  48.7 us (30%)
  between operations  17.1 us (11%)
  matrix products  7.65 us (5%)
  local copies, waits for them, and re-layouts  5.06 us (3%)
  other arithmetic  3.89 us (2%)
    all_gather x4, blocking collectives, apply_inverse(): lax.all_gather(residue, 'rows', axis=0, tiled=True)  53.5 us
    reduce_scatter x4, waiting for transfers between devices, apply_inverse(): lax.psum_scatter(partial_value, 'rows', scatter_dimension=0, tiled=True)  48.6 us
    all_gather x4, blocking collectives, column_terms(): lax.all_gather(local_panel, 'samples', axis=1, tiled=True)  24.8 us
    dot_general x14, matrix products, product(): jnp.dot(left, right, precision=lax.Precision.HIGHEST, preferred_element_t...  7.65 us
  transfers between devices with their start and end apart: 4, of which 4 were waited for; matrix products, arithmetic and copies ran while one was open for 2% of the time, Pallas kernels for 0%

commit v1 on v0

v1 whole, which is shorter than its diff:
```python
import functools

import jax
import jax.numpy as jnp
from jax import lax
from jax.experimental import pallas as pl
from jax.experimental.pallas import tpu as pltpu
from jax.sharding import PartitionSpec as P

F32 = jnp.float32
HIGHEST = lax.Precision.HIGHEST
VMEM = pl.BlockSpec(memory_space=pltpu.VMEM)
SMEM = pl.BlockSpec(memory_space=pltpu.SMEM)


def product(left, right):
    return jnp.dot(left, right, precision=HIGHEST, preferred_element_type=F32)


def product_t(left, right):
    return lax.dot_general(
        left, right, (((1,), (1,)), ((), ())), precision=HIGHEST, preferred_element_type=F32
    )


def apply_inverse(target, partial_value, inverse_rows):
    rows_here = inverse_rows.shape[0]
    share = lax.psum_scatter(partial_value, "rows", scatter_dimension=0, tiled=True)
    first_own = lax.axis_index("rows") * rows_here
    residue = lax.dynamic_slice_in_dim(target, first_own, rows_here, 0) - share
    return product(inverse_rows, lax.all_gather(residue, "rows", axis=0, tiled=True))


def general(ancestor, panels, row_map, offsets, noise, inverse, inner_link, cross_link):
    block_rows = inverse.shape[3]
    solved = [[None, None], [None, None]]
    for p in (1, 0):
        front_rows = jnp.take(ancestor, row_map[p], axis=0)
        window = lax.dynamic_slice_in_dim(noise, offsets[p], 2 * block_rows, 0)
        for b in (1, 0):
            whole = lax.all_gather(panels[p, b], "samples", axis=1, tiled=True)
            partial_value = product(whole.T, front_rows)
            if b == 0:
                partial_value = partial_value + product(inner_link[p].T, solved[p][1])
            if p == 0:
                for earlier in (0, 1):
                    partial_value = partial_value + product(
                        cross_link[b, earlier].T, solved[1][earlier]
                    )
            target = window[b * block_rows : (b + 1) * block_rows]
            solved[p][b] = apply_inverse(target, partial_value, inverse[p, b])
    return jnp.stack([jnp.stack(solved[0]), jnp.stack(solved[1])])


def exchange(array, axis, mask, size):
    return lax.ppermute(array, axis, [(i, i ^ mask) for i in range(size)])


def pack_kernel(pos_ref, panels_ref, inv_ref, inner_ref, cross_ref, packed_ref, share_ref):
    for p in range(2):
        packed_ref[p] = jnp.concatenate([panels_ref[p, 0], panels_ref[p, 1]], axis=-1)
    share_ref[0:4] = inv_ref[...]
    share_ref[4:6] = inner_ref[...]
    share_ref[6:10] = cross_ref[...]


def pack(pos, panels, inverse, inner, cross, parts):
    k_rows, cols = panels.shape[2:]
    rows_here, block = inverse.shape[1:]
    piece = rows_here // parts

    def rows_of(count):
        return pl.BlockSpec((count, piece, block), lambda i, pos: (0, pos[3], 0))

    return pl.pallas_call(
        pack_kernel,
        out_shape=(
            jax.ShapeDtypeStruct((2, k_rows, 2 * cols), F32),
            jax.ShapeDtypeStruct((10, piece, block), F32),
        ),
        grid_spec=pltpu.PrefetchScalarGridSpec(
            num_scalar_prefetch=1,
            grid=(1,),
            in_specs=[
                pl.BlockSpec(panels.shape, lambda i, pos: (0, 0, 0, 0)),
                rows_of(4),
                rows_of(2),
                rows_of(4),
            ],
            out_specs=[
                pl.BlockSpec((2, k_rows, 2 * cols), lambda i, pos: (0, 0, 0)),
                pl.BlockSpec((10, piece, block), lambda i, pos: (0, 0, 0)),
            ],
        ),
        name="pack",
    )(pos, panels, inverse, inner, cross)


def terms(pos_ref, front_t, packed, out_refs, hold):
    row = pos_ref[0]
    ranks, quarter = hold.shape[0], hold.shape[1]
    width = packed[0].shape[2]
    for p in range(2):
        both = jnp.concatenate([ref[p] for ref in packed], axis=-1)
        value = product(front_t[p], both)
        hold[...] = value.reshape(ranks, quarter, value.shape[1])
        for k, out in enumerate(out_refs):
            piece = hold[row ^ k]
            for group in range(len(packed)):
                out[group, p] = piece[:, group * width : (group + 1) * width]


def first_terms_kernel(pos_ref, map_ref, ancestor_ref, own_ref, other_ref, front_ref, *rest):
    out_refs, (front, hold) = rest[:-2], rest[-2:]
    k_rows = front.shape[1]
    step = 8
    for p in range(2):

        def body(i, carry):
            base = pl.multiple_of(i * step, step)
            rows = [ancestor_ref[pl.ds(map_ref[p, base + j], 1), :] for j in range(step)]
            front[p, pl.ds(base, step), :] = jnp.concatenate(rows, axis=0)
            return carry

        lax.fori_loop(0, k_rows // step, body, 0, unroll=4)
    for p in range(2):
        front_ref[p] = front[p].T
    terms(pos_ref, front_ref, (own_ref, other_ref), out_refs, hold)


def first_terms(pos, row_map, ancestor, own, other, ranks):
    k_rows, width = own.shape[1:]
    cols_here = ancestor.shape[1]
    quarter = cols_here // ranks
    out = jax.ShapeDtypeStruct((2, 2, quarter, width), F32)
    return pl.pallas_call(
        first_terms_kernel,
        out_shape=(jax.ShapeDtypeStruct((2, cols_here, k_rows), F32),) + (out,) * ranks,
        in_specs=[SMEM, SMEM, VMEM, VMEM, VMEM],
        out_specs=(VMEM,) * (ranks + 1),
        scratch_shapes=[
            pltpu.VMEM((2, k_rows, cols_here), F32),
            pltpu.VMEM((ranks, quarter, 2 * width), F32),
        ],
        name="first_terms",
    )(pos, row_map, ancestor, own, other)


def second_terms_kernel(pos_ref, front_ref, left_ref, right_ref, *rest):
    out_refs, hold = rest[:-1], rest[-1]
    terms(pos_ref, front_ref, (left_ref, right_ref), out_refs, hold)


def second_terms(pos, front_t, left, right, ranks):
    width = left.shape[2]
    quarter = front_t.shape[1] // ranks
    out = jax.ShapeDtypeStruct((2, 2, quarter, width), F32)
    return pl.pallas_call(
        second_terms_kernel,
        out_shape=(out,) * ranks,
        in_specs=[SMEM, VMEM, VMEM, VMEM],
        out_specs=(VMEM,) * ranks,
        scratch_shapes=[pltpu.VMEM((ranks, quarter, 2 * width), F32)],
        name="second_terms",
    )(pos, front_t, left, right)


def target_kernel(pos_ref, one_ref, two_ref, out_ref, hold):
    ranks, quarter = hold.shape[0], hold.shape[1]
    for p, ref in enumerate((one_ref, two_ref)):
        turned = ref[...].T
        hold[...] = turned.reshape(ranks, quarter, turned.shape[1])
        out_ref[p] = hold[pos_ref[0]]


def targets(pos, windows, ranks):
    rows, cols_here = windows[0].shape
    quarter = cols_here // ranks
    return pl.pallas_call(
        target_kernel,
        out_shape=jax.ShapeDtypeStruct((2, quarter, rows), F32),
        in_specs=[SMEM, VMEM, VMEM],
        out_specs=VMEM,
        scratch_shapes=[pltpu.VMEM((ranks, quarter, rows), F32)],
        name="targets",
    )(pos, *windows)


def solve_kernel(ranks, samples, masks, *refs):
    refs = list(refs)
    pos_ref, target_ref = refs[:2]
    first = refs[2 : 2 + ranks]
    second = refs[2 + ranks : 2 + 2 * ranks]
    at = 2 + 2 * ranks
    inv_ref, inner_ref, cross_ref = refs[at : at + 3]
    at += 3
    shares = refs[at : at + len(masks)]
    at += len(masks)
    outs = refs[at : at + ranks]
    sums, mats, ordered = refs[at + ranks :]

    row, sample, group = pos_ref[0], pos_ref[1], pos_ref[2]
    rows_here, block = inv_ref.shape[1:]
    piece = shares[0].shape[2]
    own = pl.ds(pl.multiple_of(row * rows_here, rows_here), rows_here)
    mats[0:4, own, :] = inv_ref[...]
    mats[4:6, own, :] = inner_ref[...]
    mats[6:10, own, :] = cross_ref[...]
    for (group_mask, sample_mask), ref in zip(masks, shares):
        part = (group ^ group_mask) * samples + (sample ^ sample_mask)
        for k in range(1, ranks):
            start = (row ^ k) * rows_here + part * piece
            mats[:, pl.ds(pl.multiple_of(start, piece), piece), :] = ref[k - 1]

    half = samples // 2
    for stage, pieces in ((0, first), (1, second)):
        for position in range(half):
            total = pieces[0][position]
            for ref in pieces[1:]:
                total = total + ref[position]
            sums[sample ^ (stage * half + position)] = total
    cols = block // samples
    rest = [[None, None], [None, None]]
    for p in range(2):
        for b in range(2):
            value = jnp.concatenate(
                [sums[s, p, :, b * cols : (b + 1) * cols] for s in range(samples)], axis=-1
            )
            rest[p][b] = target_ref[p, :, b * block : (b + 1) * block] - value

    x11 = product_t(rest[1][1], mats[3])
    x10 = product_t(rest[1][0] - product(x11, mats[5]), mats[2])
    x01 = product_t(
        rest[0][1] - product(x11, mats[9]) - product(x10, mats[8]), mats[1]
    )
    x00 = product_t(
        rest[0][0] - product(x11, mats[7]) - product(x10, mats[6]) - product(x01, mats[4]),
        mats[0],
    )
    for j in range(ranks):
        ordered[j] = jnp.concatenate(
            [x[:, j * rows_here : (j + 1) * rows_here] for x in (x00, x01, x10, x11)], axis=-1
        )
    for k, out in enumerate(outs):
        out[...] = ordered[row ^ k]


def solve(pos, target, first, second, inverse, inner, cross, masks, shares, samples):
    ranks = len(first)
    quarter = target.shape[1]
    rows_here, block = inverse.shape[1:]
    out = jax.ShapeDtypeStruct((quarter, 4 * rows_here), F32)
    return pl.pallas_call(
        functools.partial(solve_kernel, ranks, samples, masks),
        out_shape=(out,) * ranks,
        in_specs=[SMEM] + [VMEM] * (1 + 2 * ranks + 3 + len(shares)),
        out_specs=(VMEM,) * ranks,
        scratch_shapes=[
            pltpu.VMEM((samples, 2, quarter, 2 * block // samples), F32),
            pltpu.VMEM((10, block, block), F32),
            pltpu.VMEM((ranks, quarter, 4 * rows_here), F32),
        ],
        name="solve",
    )(pos, target, *first, *second, inverse, inner, cross, *shares)


def place_kernel(ranks, *refs):
    pos_ref, pieces, out_ref, hold = refs[0], refs[1 : 1 + ranks], refs[1 + ranks], refs[2 + ranks]
    for k, ref in enumerate(pieces):
        hold[pos_ref[0] ^ k] = ref[...]
    quarter, width = hold.shape[1:]
    turned = hold[...].reshape(ranks * quarter, width).T
    rows_here = out_ref.shape[2]
    for p in range(2):
        for b in range(2):
            start = (2 * p + b) * rows_here
            out_ref[p, b] = turned[start : start + rows_here]


def place(pos, pieces):
    ranks = len(pieces)
    quarter, width = pieces[0].shape
    return pl.pallas_call(
        functools.partial(place_kernel, ranks),
        out_shape=jax.ShapeDtypeStruct((2, 2, width // 4, ranks * quarter), F32),
        in_specs=[SMEM] + [VMEM] * ranks,
        out_specs=VMEM,
        scratch_shapes=[pltpu.VMEM((ranks, quarter, width), F32)],
        name="place",
    )(pos, *pieces)


def paired(groups, ranks, samples):
    def local(ancestor, panels, row_map, offsets, noise, inverse, inner_link, cross_link):
        row, sample, group = (lax.axis_index(a) for a in ("rows", "samples", "groups"))
        pos = jnp.stack([row, sample, group, group * samples + sample]).astype(jnp.int32)
        block = inverse.shape[3]
        inverse = inverse.reshape((4,) + inverse.shape[2:])
        cross = cross_link.reshape((4,) + cross_link.shape[2:])

        own, share = pack(pos, panels, inverse, inner_link, cross, groups * samples)
        far = exchange(own, "samples", 2, samples)
        near = exchange(own, "samples", 1, samples)
        got = [exchange(share, "rows", k, ranks) for k in range(1, ranks)]
        windows = [lax.dynamic_slice_in_dim(noise, offsets[p], 2 * block, 0) for p in range(2)]

        front_t, *first = first_terms(pos, row_map, ancestor, own, near, ranks)
        first = [first[0]] + [exchange(first[k], "rows", k, ranks) for k in range(1, ranks)]
        far_near = exchange(far, "samples", 1, samples)
        second = second_terms(pos, front_t, far, far_near, ranks)
        second = [second[0]] + [exchange(second[k], "rows", k, ranks) for k in range(1, ranks)]
        target = targets(pos, windows, ranks)

        here = jnp.stack(got)
        over_x = exchange(here, "samples", 2, samples)
        over_y = exchange(here, "groups", 1, groups)
        over_xy = exchange(over_x, "groups", 1, groups)
        masks = [(0, 0), (0, 2), (1, 0), (1, 2)]
        shares = [here, over_x, over_y, over_xy]
        shares = shares + [exchange(a, "samples", 1, samples) for a in shares]
        masks = masks + [(g, s ^ 1) for g, s in masks]

        pieces = solve(
            pos, target, first, second, inverse, inner_link, cross, tuple(masks), shares, samples
        )
        pieces = [pieces[0]] + [exchange(pieces[k], "rows", k, ranks) for k in range(1, ranks)]
        return place(pos, pieces)

    return local


def solution(mesh):
    groups, ranks, samples = (mesh.shape[a] for a in ("groups", "rows", "samples"))
    placed = (
        P(("groups", "rows"), "samples"),
        P(None, None, "rows", "samples"),
        P(None, "rows"),
        P(),
        P("groups", "samples"),
        P(None, None, "rows", None),
        P(None, "rows", None),
        P(None, None, "rows", None),
    )

    def whole(*arrays):
        block, columns = arrays[5].shape[3], arrays[0].shape[1]
        fits = (
            groups == 2
            and samples == 4
            and ranks in (2, 4)
            and block % (ranks * groups * samples * 8) == 0
            and columns % (samples * ranks * 8) == 0
        )
        return jax.shard_map(
            paired(groups, ranks, samples) if fits else general,
            mesh=mesh,
            in_specs=placed,
            out_specs=P(None, None, "rows", ("groups", "samples")),
            check_vma=False,
        )(*arrays)

    return whole
```

time: 161 us -> 72.4 us (0.45)
  blocking collectives: 78.3 us -> 0 us
  waiting for transfers between devices: 48.7 us -> 16.8 us
  starting transfers between devices: 0.13 us -> 27.6 us
  Pallas kernels: 0 us -> 17.4 us
  between operations: 17.1 us -> 4.16 us
  matrix products: 7.65 us -> 0 us
  other arithmetic: 3.89 us -> 0.67 us
    all_gather x8 -> x0, blocking collectives: 78.3 us -> none  [the longest x4 53.5 us: apply_inverse(): lax.all_gather(residue, 'rows', axis=0, tiled=True)]
    reduce_scatter x4 -> x0, waiting for transfers between devices: 48.6 us -> none  [apply_inverse(): lax.psum_scatter(partial_value, 'rows', scatter_dimension=0, tiled=True)]
    ppermute x0 -> x22, starting transfers between devices: none -> 27.6 us  [exchange(): return lax.ppermute(array, axis, [(i, i ^ mask) for i in range(size)])]
    pallas_call x0 -> x6, Pallas kernels: none -> 17.4 us  [the longest x1 5.52 us: solve(): pl.pallas_call(functools.partial(solve_kernel, ranks, samples, masks), ou...]
    ppermute x0 -> x22, waiting for transfers between devices: none -> 16.8 us  [exchange(): return lax.ppermute(array, axis, [(i, i ^ mask) for i in range(size)])]
    dot_general x14 -> x0, matrix products: 7.65 us -> none  [product(): jnp.dot(left, right, precision=lax.Precision.HIGHEST, preferred_element_t...]
    sub x4 -> x0, other arithmetic: 3.18 us -> none  [apply_inverse(): residue = lax.dynamic_slice_in_dim(target, first_own, rows_here, 0) - share]
    unnamed x10 -> x45, local copies, waits for them, and re-layouts: 1.28 us -> 3.94 us
  transfers between devices with their start and end apart: 4 -> 22, of which waited for: 4 -> 9; matrix products, arithmetic and copies ran while one was open for 2% -> 2% of each run, Pallas kernels for 0% -> 11%
where the time goes in v1:
time: 72.4 us; the launch traced here: 72 us
  starting transfers between devices  27.6 us (38%)
  Pallas kernels  17.4 us (24%)
  waiting for transfers between devices  16.8 us (23%)
  local copies, waits for them, and re-layouts  5.39 us (7%)
  between operations  4.16 us (6%)
    ppermute x22, starting transfers between devices, exchange(): return lax.ppermute(array, axis, [(i, i ^ mask) for i in range(size)])  27.6 us
    ppermute x22, waiting for transfers between devices, exchange(): return lax.ppermute(array, axis, [(i, i ^ mask) for i in range(size)])  16.8 us
    pallas_call x1, Pallas kernels, solve(): pl.pallas_call(functools.partial(solve_kernel, ranks, samples, masks), ou...  5.52 us
    unnamed x45, local copies, waits for them, and re-layouts  3.94 us
    pallas_call x1, Pallas kernels, first_terms(): pl.pallas_call(first_terms_kernel, out_shape=(jax.ShapeDtypeStruct((2, co...  3.37 us
    pallas_call x1, Pallas kernels, pack(): pl.pallas_call(pack_kernel, out_shape=(jax.ShapeDtypeStruct((2, k_rows, 2...  2.71 us
    pallas_call x1, Pallas kernels, second_terms(): pl.pallas_call(second_terms_kernel, out_shape=(out,) * ranks, in_specs=[S...  2.3 us
    pallas_call x1, Pallas kernels, targets(): pl.pallas_call(target_kernel, out_shape=jax.ShapeDtypeStruct((2, quarter,...  1.9 us
  transfers between devices with their start and end apart: 22, of which 9 were waited for; matrix products, arithmetic and copies ran while one was open for 2% of the time, Pallas kernels for 11%

profile of v1, /device:TPU:0, one launch (start us, length us, event | category | flops | bytes accessed | tf_op | source)
XLA Modules:
  0.0 72.0 jit_solution(15282396022596984695)
XLA Ops:
  0.0 2.0 %copy.9.panels_ref = f32[2,2,256,64]{3,2,1,0:T(8,128)} copy(f32[2,2,256,64]{2,3,1,0:T(8,128)} %param.9) | data formatting | bytes 524288 | tf_op args[1]
  2.0 0.6 pad_add_fusion.pos_ref.refs_0_
  2.6 2.7 %pack.1 = (f32[2,256,128]{2,1,0:T(8,128)}, f32[10,8,256]{2,1,0:T(8,128)}) custom-call(s32[4]{0:T(128)} %pad_add_fusion.pos_ref.refs_0_, f32[2,2,256,64]{3,2,1,0:T(8,128)} %copy.9.panels_ref, f32[4,64,256]{2,1,0:T(8,128)} %bitcast.11, f32[2,64,256]{2,1,0:T(8,128)} %refs_11_.1, f32[4,64,256]{2,1,0:T(8,128)} %bitcast.13), custom_call_target="tpu_custom_call" | custom-call | tf_op jit(solution)/shard_map/pack/pallas_call | solution.py:75
  5.3 5.0 %collective-permute-start.11 = (f32[10,8,256]{2,1,0:T(8,128)}, f32[10,8,256]{2,1,0:T(8,128)S(1)}, u32[]{:S(2)}, u32[]{:S(2)}) collective-permute-start(f32[10,8,256]{2,1,0:T(8,128)} %get-tuple-element.30), channel_id=1, source_target_pairs={{0,12},{4,8},{8,4},{12,0},{1,13},{5,9},{9,5},{13,1},{2,14},{6,10},... | collective-permute-start | bytes 245768 | tf_op jit(solution)/shard_map/ppermute | solution.py:56
  10.4 0.6 collective-permute-start.9
  11.0 1.6 %collective-permute-start.4 = (f32[2,256,128]{2,1,0:T(8,128)}, f32[2,256,128]{2,1,0:T(8,128)S(1)}, u32[]{:S(2)}, u32[]{:S(2)}) collective-permute-start(f32[2,256,128]{2,1,0:T(8,128)} %get-tuple-element.20.own_ref), channel_id=1, source_target_pairs={{0,2},{1,3},{2,0},{3,1},{4,6},{5,7},{6,4},{7,5},{8,10},{9,11},{10,... | collective-permute-start | bytes 786440 | tf_op jit(solution)/shard_map/ppermute | solution.py:56
  12.7 1.0 %collective-permute-done.11 = f32[10,8,256]{2,1,0:T(8,128)S(1)} collective-permute-done((f32[10,8,256]{2,1,0:T(8,128)}, f32[10,8,256]{2,1,0:T(8,128)S(1)}, u32[]{:S(2)}, u32[]{:S(2)}) %collective-permute-start.11) | collective-permute-done | bytes 81952 | tf_op jit(solution)/shard_map/ppermute | solution.py:56
  13.6 3.8 %collective-permute-done.10 = f32[10,8,256]{2,1,0:T(8,128)S(1)} collective-permute-done((f32[10,8,256]{2,1,0:T(8,128)}, f32[10,8,256]{2,1,0:T(8,128)S(1)}, u32[]{:S(2)}, u32[]{:S(2)}) %collective-permute-start.10) | collective-permute-done | bytes 81952 | tf_op jit(solution)/shard_map/ppermute | solution.py:56
  17.5 1.6 %collective-permute-start.12 = (f32[3,10,8,256]{3,2,1,0:T(8,128)S(1)}, f32[3,10,8,256]{3,2,1,0:T(8,128)S(1)}, u32[]{:S(2)}, u32[]{:S(2)}) collective-permute-start(f32[3,10,8,256]{3,2,1,0:T(8,128)S(1)} %pad_maximum_fusion.refs_13_), channel_id=1, source_target_pairs={{0,2},{1,3},{2,0},{3,1},{4,6},{5,7},{6,4},{7,5},{8,10},{9,11},{10,... | collective-permute-start | bytes 737288 | tf_op jit(solution)/shard_map/ppermute | solution.py:56
  19.6 1.5 %collective-permute-start.13 = (f32[3,10,8,256]{3,2,1,0:T(8,128)S(1)}, f32[3,10,8,256]{3,2,1,0:T(8,128)S(1)}, u32[]{:S(2)}, u32[]{:S(2)}) collective-permute-start(f32[3,10,8,256]{3,2,1,0:T(8,128)S(1)} %pad_maximum_fusion.refs_13_), channel_id=1, source_target_pairs={{0,16},{16,0},{1,17},{17,1},{2,18},{18,2},{3,19},{19,3},{4,20},{20... | collective-permute-start | bytes 737288 | tf_op jit(solution)/shard_map/ppermute | solution.py:56
  21.1 3.6 %collective-permute-done.12.refs_14_ = f32[3,10,8,256]{3,2,1,0:T(8,128)S(1)} collective-permute-done((f32[3,10,8,256]{3,2,1,0:T(8,128)S(1)}, f32[3,10,8,256]{3,2,1,0:T(8,128)S(1)}, u32[]{:S(2)}, u32[]{:S(2)}) %collective-permute-start.12) | collective-permute-done | bytes 245792 | tf_op jit(solution)/shard_map/ppermute | solution.py:56
  24.7 1.7 %collective-permute-start.14 = (f32[3,10,8,256]{3,2,1,0:T(8,128)S(1)}, f32[3,10,8,256]{3,2,1,0:T(8,128)S(1)}, u32[]{:S(2)}, u32[]{:S(2)}) collective-permute-start(f32[3,10,8,256]{3,2,1,0:T(8,128)S(1)} %collective-permute-done.12.refs_14_), channel_id=1, source_target_pairs={{0,16},{16,0},{1,17},{17,1},{2,18},{18,2},{3,19},{19,3},{4,20},{20... | collective-permute-start | bytes 737288 | tf_op jit(solution)/shard_map/ppermute | solution.py:56
  26.4 0.7 copy-done.5
  27.1 3.4 %first_terms.1 = (f32[2,128,256]{2,1,0:T(8,128)}, f32[2,2,32,128]{3,2,1,0:T(8,128)}, f32[2,2,32,128]{3,2,1,0:T(8,128)}, f32[2,2,32,128]{3,2,1,0:T(8,128)}, f32[2,2,32,128]{3,2,1,0:T(8,128)}) custom-call(s32[4]{0:T(128)} %pad_add_fusion.pos_ref.refs_0_, s32[2,256]{1,0:T(2,128)} %map_ref.1, f32[512,128]{1,0:T(8,128)} %ancestor_ref.1, ...), custom_call_target="tpu_custom_call" | custom-call | tf_op jit(solution)/shard_map/first_terms/pallas_call | solution.py:136
  31.0 2.6 %collective-permute-start.2 = (f32[2,2,32,128]{3,2,1,0:T(8,128)}, f32[2,2,32,128]{3,2,1,0:T(8,128)S(1)}, u32[]{:S(2)}, u32[]{:S(2)}) collective-permute-start(f32[2,2,32,128]{3,2,1,0:T(8,128)} %get-tuple-element.23), channel_id=1, source_target_pairs={{0,8},{4,12},{8,0},{12,4},{1,9},{5,13},{9,1},{13,5},{2,10},{6,14},... | collective-permute-start | bytes 196616 | tf_op jit(solution)/shard_map/ppermute | solution.py:56
  33.6 1.3 %collective-permute-done.1.refs_3_ = f32[2,2,32,128]{3,2,1,0:T(8,128)S(1)} collective-permute-done((f32[2,2,32,128]{3,2,1,0:T(8,128)}, f32[2,2,32,128]{3,2,1,0:T(8,128)S(1)}, u32[]{:S(2)}, u32[]{:S(2)}) %collective-permute-start.1) | collective-permute-done | bytes 65568 | tf_op jit(solution)/shard_map/ppermute | solution.py:56
  35.0 1.4 %collective-permute-done.2.refs_4_ = f32[2,2,32,128]{3,2,1,0:T(8,128)S(1)} collective-permute-done((f32[2,2,32,128]{3,2,1,0:T(8,128)}, f32[2,2,32,128]{3,2,1,0:T(8,128)S(1)}, u32[]{:S(2)}, u32[]{:S(2)}) %collective-permute-start.2) | collective-permute-done | bytes 65568 | tf_op jit(solution)/shard_map/ppermute | solution.py:56
  37.0 2.4 %collective-permute-start.3 = (f32[2,2,32,128]{3,2,1,0:T(8,128)}, f32[2,2,32,128]{3,2,1,0:T(8,128)S(1)}, u32[]{:S(2)}, u32[]{:S(2)}) collective-permute-start(f32[2,2,32,128]{3,2,1,0:T(8,128)} %get-tuple-element.24), channel_id=1, source_target_pairs={{0,12},{4,8},{8,4},{12,0},{1,13},{5,9},{9,5},{13,1},{2,14},{6,10},... | collective-permute-start | bytes 196616 | tf_op jit(solution)/shard_map/ppermute | solution.py:56
  43.9 2.3 %second_terms.1 = (f32[2,2,32,128]{3,2,1,0:T(8,128)}, f32[2,2,32,128]{3,2,1,0:T(8,128)}, f32[2,2,32,128]{3,2,1,0:T(8,128)}, f32[2,2,32,128]{3,2,1,0:T(8,128)}) custom-call(s32[4]{0:T(128)} %pad_add_fusion.pos_ref.refs_0_, f32[2,128,256]{2,1,0:T(8,128)} %get-tuple-element.25.front_ref, f32[2,256,128]{2,1,0:T(8,128)} %copy-done.2, f32[2,256,128]{2,1,0:T(8,128)} %copy-done.3), custom_call_target="tpu_custom_call" | custom-call | tf_op jit(solution)/shard_map/second_terms/pallas_call | solution.py:158
  46.3 0.9 %collective-permute-start.6 = (f32[2,2,32,128]{3,2,1,0:T(8,128)}, f32[2,2,32,128]{3,2,1,0:T(8,128)S(1)}, u32[]{:S(2)}, u32[]{:S(2)}) collective-permute-start(f32[2,2,32,128]{3,2,1,0:T(8,128)} %get-tuple-element.27), channel_id=1, source_target_pairs={{0,4},{4,0},{8,12},{12,8},{1,5},{5,1},{9,13},{13,9},{2,6},{6,2},{1... | collective-permute-start | bytes 196616 | tf_op jit(solution)/shard_map/ppermute | solution.py:56
  47.2 1.2 %collective-permute-start.7 = (f32[2,2,32,128]{3,2,1,0:T(8,128)}, f32[2,2,32,128]{3,2,1,0:T(8,128)S(1)}, u32[]{:S(2)}, u32[]{:S(2)}) collective-permute-start(f32[2,2,32,128]{3,2,1,0:T(8,128)} %get-tuple-element.28), channel_id=1, source_target_pairs={{0,8},{4,12},{8,0},{12,4},{1,9},{5,13},{9,1},{13,5},{2,10},{6,14},... | collective-permute-start | bytes 196616 | tf_op jit(solution)/shard_map/ppermute | solution.py:56
  48.4 2.4 %collective-permute-start.8 = (f32[2,2,32,128]{3,2,1,0:T(8,128)}, f32[2,2,32,128]{3,2,1,0:T(8,128)S(1)}, u32[]{:S(2)}, u32[]{:S(2)}) collective-permute-start(f32[2,2,32,128]{3,2,1,0:T(8,128)} %get-tuple-element.29), channel_id=1, source_target_pairs={{0,12},{4,8},{8,4},{12,0},{1,13},{5,9},{9,5},{13,1},{2,14},{6,10},... | collective-permute-start | bytes 196616 | tf_op jit(solution)/shard_map/ppermute | solution.py:56
  50.7 0.9 %constant_dynamic-slice_fusion = (f32[512,128]{1,0:T(8,128)}, f32[512,128]{1,0:T(8,128)}) fusion(f32[2048,128]{1,0:T(8,128)S(1)} %copy-done.1, s32[]{:T(128)S(6)} %select_n.7, s32[]{:T(128)S(6)} %select_n.6), kind=kLoop, calls=%fused_computation.2 | loop fusion | bytes 1048584 | tf_op jit(solution)/shard_map/dynamic_slice | solution.py:305
  51.6 1.9 %targets.1.refs_1_ = f32[2,32,512]{2,1,0:T(8,128)} custom-call(s32[4]{0:T(128)} %pad_add_fusion.pos_ref.refs_0_, f32[512,128]{1,0:T(8,128)} %get-tuple-element.36.one_ref, f32[512,128]{1,0:T(8,128)} %get-tuple-element.35.two_ref), custom_call_target="tpu_custom_call" | custom-call | tf_op jit(solution)/shard_map/targets/pallas_call | solution.py:179
  53.5 2.1 %collective-permute-done.7.refs_8_ = f32[2,2,32,128]{3,2,1,0:T(8,128)S(1)} collective-permute-done((f32[2,2,32,128]{3,2,1,0:T(8,128)}, f32[2,2,32,128]{3,2,1,0:T(8,128)S(1)}, u32[]{:S(2)}, u32[]{:S(2)}) %collective-permute-start.7) | collective-permute-done | bytes 65568 | tf_op jit(solution)/shard_map/ppermute | solution.py:56
  56.3 5.5 %solve.1 = (f32[32,256]{1,0:T(8,128)}, f32[32,256]{1,0:T(8,128)}, f32[32,256]{1,0:T(8,128)}, f32[32,256]{1,0:T(8,128)}) custom-call(s32[4]{0:T(128)} %pad_add_fusion.pos_ref.refs_0_, f32[2,32,512]{2,1,0:T(8,128)} %targets.1.refs_1_, f32[2,2,32,128]{3,2,1,0:T(8,128)} %get-tuple-element.21.refs_2_, f32[2,2,32,128]{3,2,1,0:T(8,128)} %copy-done.12, ...), custom_call_target="tpu_custom_call" | custom-call | tf_op jit(solution)/shard_map/solve/pallas_call | solution.py:253
  61.9 1.3 %collective-permute-start.19 = (f32[32,256]{1,0:T(8,128)}, f32[32,256]{1,0:T(8,128)S(1)}, u32[]{:S(2)}, u32[]{:S(2)}) collective-permute-start(f32[32,256]{1,0:T(8,128)} %get-tuple-element.32), channel_id=1, source_target_pairs={{0,4},{4,0},{8,12},{12,8},{1,5},{5,1},{9,13},{13,9},{2,6},{6,2},{1... | collective-permute-start | bytes 98312 | tf_op jit(solution)/shard_map/ppermute | solution.py:56
  63.2 0.7 %collective-permute-start.20 = (f32[32,256]{1,0:T(8,128)}, f32[32,256]{1,0:T(8,128)S(1)}, u32[]{:S(2)}, u32[]{:S(2)}) collective-permute-start(f32[32,256]{1,0:T(8,128)} %get-tuple-element.33), channel_id=1, source_target_pairs={{0,8},{4,12},{8,0},{12,4},{1,9},{5,13},{9,1},{13,5},{2,10},{6,14},... | collective-permute-start | bytes 98312 | tf_op jit(solution)/shard_map/ppermute | solution.py:56
  63.9 2.4 %collective-permute-start.21 = (f32[32,256]{1,0:T(8,128)}, f32[32,256]{1,0:T(8,128)S(1)}, u32[]{:S(2)}, u32[]{:S(2)}) collective-permute-start(f32[32,256]{1,0:T(8,128)} %get-tuple-element.34), channel_id=1, source_target_pairs={{0,12},{4,8},{8,4},{12,0},{1,13},{5,9},{9,5},{13,1},{2,14},{6,10},... | collective-permute-start | bytes 98312 | tf_op jit(solution)/shard_map/ppermute | solution.py:56
  66.4 2.1 %collective-permute-done.20.refs_3_ = f32[32,256]{1,0:T(8,128)S(1)} collective-permute-done((f32[32,256]{1,0:T(8,128)}, f32[32,256]{1,0:T(8,128)S(1)}, u32[]{:S(2)}, u32[]{:S(2)}) %collective-permute-start.20) | collective-permute-done | bytes 32800 | tf_op jit(solution)/shard_map/ppermute | solution.py:56
  68.5 1.3 %collective-permute-done.21.refs_4_ = f32[32,256]{1,0:T(8,128)S(1)} collective-permute-done((f32[32,256]{1,0:T(8,128)}, f32[32,256]{1,0:T(8,128)S(1)}, u32[]{:S(2)}, u32[]{:S(2)}) %collective-permute-start.21) | collective-permute-done | bytes 32800 | tf_op jit(solution)/shard_map/ppermute | solution.py:56
  70.4 1.6 %place.1 = f32[2,2,64,128]{3,2,1,0:T(8,128)} custom-call(s32[4]{0:T(128)} %pad_add_fusion.pos_ref.refs_0_, f32[32,256]{1,0:T(8,128)} %get-tuple-element.31.refs_1_, f32[32,256]{1,0:T(8,128)} %copy-done.18, f32[32,256]{1,0:T(8,128)} %copy-done.19, f32[32,256]{1,0:T(8,128)} %copy-done.20), custom_call_target="tpu_custom_call" | custom-call | tf_op jit(solution)/shard_map/place/pallas_call | solution.py:283
  (67 shorter events, 3.6 us)
Async XLA Ops:
  2.6 36.7 %copy-start.21 = (s32[2]{0:T(128)S(1)}, s32[2]{0:T(128)}, u32[]{:S(2)}) copy-start(s32[2]{0:T(128)} %param.11) | copy-start | bytes 28
  5.3 13.7 %copy-start.4 = (f32[2,256,128]{2,1,0:T(8,128)S(1)}, f32[2,256,128]{2,1,0:T(8,128)}, u32[]{:S(2)}) copy-start(f32[2,256,128]{2,1,0:T(8,128)} %get-tuple-element.20.own_ref) | copy-start | bytes 786436
  5.3 8.3 %collective-permute-start.11 = (f32[10,8,256]{2,1,0:T(8,128)}, f32[10,8,256]{2,1,0:T(8,128)S(1)}, u32[]{:S(2)}, u32[]{:S(2)}) collective-permute-start(f32[10,8,256]{2,1,0:T(8,128)} %get-tuple-element.30), channel_id=1, source_target_pairs={{0,12},{4,8},{8,4},{12,0},{1,13},{5,9},{9,5},{13,1},{2,14},{6,10},... | collective-permute-start | bytes 245768 | tf_op jit(solution)/shard_map/ppermute | solution.py:56
  10.4 7.1 %collective-permute-start.10 = (f32[10,8,256]{2,1,0:T(8,128)}, f32[10,8,256]{2,1,0:T(8,128)S(1)}, u32[]{:S(2)}, u32[]{:S(2)}) collective-permute-start(f32[10,8,256]{2,1,0:T(8,128)} %get-tuple-element.30), channel_id=1, source_target_pairs={{0,8},{4,12},{8,0},{12,4},{1,9},{5,13},{9,1},{13,5},{2,10},{6,14},... | collective-permute-start | bytes 245768 | tf_op jit(solution)/shard_map/ppermute | solution.py:56
  10.4 7.1 %collective-permute-start.9 = (f32[10,8,256]{2,1,0:T(8,128)}, f32[10,8,256]{2,1,0:T(8,128)S(1)}, u32[]{:S(2)}, u32[]{:S(2)}) collective-permute-start(f32[10,8,256]{2,1,0:T(8,128)} %get-tuple-element.30), channel_id=1, source_target_pairs={{0,4},{4,0},{8,12},{12,8},{1,5},{5,1},{9,13},{13,9},{2,6},{6,2},{1... | collective-permute-start | bytes 245768 | tf_op jit(solution)/shard_map/ppermute | solution.py:56
  11.0 8.0 %collective-permute-start.4 = (f32[2,256,128]{2,1,0:T(8,128)}, f32[2,256,128]{2,1,0:T(8,128)S(1)}, u32[]{:S(2)}, u32[]{:S(2)}) collective-permute-start(f32[2,256,128]{2,1,0:T(8,128)} %get-tuple-element.20.own_ref), channel_id=1, source_target_pairs={{0,2},{1,3},{2,0},{3,1},{4,6},{5,7},{6,4},{7,5},{8,10},{9,11},{10,... | collective-permute-start | bytes 786440 | tf_op jit(solution)/shard_map/ppermute | solution.py:56
  17.5 33.3 %copy-start.1 = (f32[2048,128]{1,0:T(8,128)S(1)}, f32[2048,128]{1,0:T(8,128)}, u32[]{:S(2)}) copy-start(f32[2048,128]{1,0:T(8,128)} %param.12) | copy-start | bytes 3145732
  17.5 17.5 %copy-start = (f32[3,10,8,256]{3,2,1,0:T(8,128)}, f32[3,10,8,256]{3,2,1,0:T(8,128)S(1)}, u32[]{:S(2)}) copy-start(f32[3,10,8,256]{3,2,1,0:T(8,128)S(1)} %pad_maximum_fusion.refs_13_) | copy-start | bytes 737284
  17.5 7.2 %collective-permute-start.12 = (f32[3,10,8,256]{3,2,1,0:T(8,128)S(1)}, f32[3,10,8,256]{3,2,1,0:T(8,128)S(1)}, u32[]{:S(2)}, u32[]{:S(2)}) collective-permute-start(f32[3,10,8,256]{3,2,1,0:T(8,128)S(1)} %pad_maximum_fusion.refs_13_), channel_id=1, source_target_pairs={{0,2},{1,3},{2,0},{3,1},{4,6},{5,7},{6,4},{7,5},{8,10},{9,11},{10,... | collective-permute-start | bytes 737288 | tf_op jit(solution)/shard_map/ppermute | solution.py:56
  19.0 7.3 %collective-permute-start = (f32[2,256,128]{2,1,0:T(8,128)S(1)}, f32[2,256,128]{2,1,0:T(8,128)S(1)}, u32[]{:S(2)}, u32[]{:S(2)}) collective-permute-start(f32[2,256,128]{2,1,0:T(8,128)S(1)} %copy-done.4), channel_id=1, source_target_pairs={{0,1},{1,0},{2,3},{3,2},{4,5},{5,4},{6,7},{7,6},{8,9},{9,8},{10,11... | collective-permute-start | bytes 786440 | tf_op jit(solution)/shard_map/ppermute | solution.py:56
  19.1 11.4 %copy-start.2 = (f32[2,256,128]{2,1,0:T(8,128)}, f32[2,256,128]{2,1,0:T(8,128)S(1)}, u32[]{:S(2)}) copy-start(f32[2,256,128]{2,1,0:T(8,128)S(1)} %collective-permute-done.4.left_ref) | copy-start | bytes 786436
  19.1 17.9 %collective-permute-start.5 = (f32[2,256,128]{2,1,0:T(8,128)S(1)}, f32[2,256,128]{2,1,0:T(8,128)S(1)}, u32[]{:S(2)}, u32[]{:S(2)}) collective-permute-start(f32[2,256,128]{2,1,0:T(8,128)S(1)} %collective-permute-done.4.left_ref), channel_id=1, source_target_pairs={{0,1},{1,0},{2,3},{3,2},{4,5},{5,4},{6,7},{7,6},{8,9},{9,8},{10,11... | collective-permute-start | bytes 786440 | tf_op jit(solution)/shard_map/ppermute | solution.py:56
  19.6 16.8 %collective-permute-start.13 = (f32[3,10,8,256]{3,2,1,0:T(8,128)S(1)}, f32[3,10,8,256]{3,2,1,0:T(8,128)S(1)}, u32[]{:S(2)}, u32[]{:S(2)}) collective-permute-start(f32[3,10,8,256]{3,2,1,0:T(8,128)S(1)} %pad_maximum_fusion.refs_13_), channel_id=1, source_target_pairs={{0,16},{16,0},{1,17},{17,1},{2,18},{18,2},{3,19},{19,3},{4,20},{20... | collective-permute-start | bytes 737288 | tf_op jit(solution)/shard_map/ppermute | solution.py:56
  24.7 21.5 %copy-start.6 = (f32[3,10,8,256]{3,2,1,0:T(8,128)}, f32[3,10,8,256]{3,2,1,0:T(8,128)S(1)}, u32[]{:S(2)}) copy-start(f32[3,10,8,256]{3,2,1,0:T(8,128)S(1)} %collective-permute-done.12.refs_14_) | copy-start | bytes 737284
  24.7 12.2 %collective-permute-start.14 = (f32[3,10,8,256]{3,2,1,0:T(8,128)S(1)}, f32[3,10,8,256]{3,2,1,0:T(8,128)S(1)}, u32[]{:S(2)}, u32[]{:S(2)}) collective-permute-start(f32[3,10,8,256]{3,2,1,0:T(8,128)S(1)} %collective-permute-done.12.refs_14_), channel_id=1, source_target_pairs={{0,16},{16,0},{1,17},{17,1},{2,18},{18,2},{3,19},{19,3},{4,20},{20... | collective-permute-start | bytes 737288 | tf_op jit(solution)/shard_map/ppermute | solution.py:56
  30.5 4.5 %collective-permute-start.1 = (f32[2,2,32,128]{3,2,1,0:T(8,128)}, f32[2,2,32,128]{3,2,1,0:T(8,128)S(1)}, u32[]{:S(2)}, u32[]{:S(2)}) collective-permute-start(f32[2,2,32,128]{3,2,1,0:T(8,128)} %get-tuple-element.22), channel_id=1, source_target_pairs={{0,4},{4,0},{8,12},{12,8},{1,5},{5,1},{9,13},{13,9},{2,6},{6,2},{1... | collective-permute-start | bytes 196616 | tf_op jit(solution)/shard_map/ppermute | solution.py:56
  31.0 5.4 %collective-permute-start.2 = (f32[2,2,32,128]{3,2,1,0:T(8,128)}, f32[2,2,32,128]{3,2,1,0:T(8,128)S(1)}, u32[]{:S(2)}, u32[]{:S(2)}) collective-permute-start(f32[2,2,32,128]{3,2,1,0:T(8,128)} %get-tuple-element.23), channel_id=1, source_target_pairs={{0,8},{4,12},{8,0},{12,4},{1,9},{5,13},{9,1},{13,5},{2,10},{6,14},... | collective-permute-start | bytes 196616 | tf_op jit(solution)/shard_map/ppermute | solution.py:56
  34.9 11.3 %copy-start.12 = (f32[2,2,32,128]{3,2,1,0:T(8,128)}, f32[2,2,32,128]{3,2,1,0:T(8,128)S(1)}, u32[]{:S(2)}) copy-start(f32[2,2,32,128]{3,2,1,0:T(8,128)S(1)} %collective-permute-done.1.refs_3_) | copy-start | bytes 196612
  34.9 12.2 %collective-permute-start.15 = (f32[3,10,8,256]{3,2,1,0:T(8,128)S(1)}, f32[3,10,8,256]{3,2,1,0:T(8,128)S(1)}, u32[]{:S(2)}, u32[]{:S(2)}) collective-permute-start(f32[3,10,8,256]{3,2,1,0:T(8,128)S(1)} %pad_maximum_fusion.refs_13_), channel_id=1, source_target_pairs={{0,1},{1,0},{2,3},{3,2},{4,5},{5,4},{6,7},{7,6},{8,9},{9,8},{10,11... | collective-permute-start | bytes 737288 | tf_op jit(solution)/shard_map/ppermute | solution.py:56
  36.3 9.9 %copy-start.13 = (f32[2,2,32,128]{3,2,1,0:T(8,128)}, f32[2,2,32,128]{3,2,1,0:T(8,128)S(1)}, u32[]{:S(2)}) copy-start(f32[2,2,32,128]{3,2,1,0:T(8,128)S(1)} %collective-permute-done.2.refs_4_) | copy-start | bytes 196612
  36.4 12.0 %collective-permute-start.16 = (f32[3,10,8,256]{3,2,1,0:T(8,128)S(1)}, f32[3,10,8,256]{3,2,1,0:T(8,128)S(1)}, u32[]{:S(2)}, u32[]{:S(2)}) collective-permute-start(f32[3,10,8,256]{3,2,1,0:T(8,128)S(1)} %collective-permute-done.12.refs_14_), channel_id=1, source_target_pairs={{0,1},{1,0},{2,3},{3,2},{4,5},{5,4},{6,7},{7,6},{8,9},{9,8},{10,11... | collective-permute-start | bytes 737288 | tf_op jit(solution)/shard_map/ppermute | solution.py:56
  36.4 15.2 %copy-start.7 = (f32[3,10,8,256]{3,2,1,0:T(8,128)}, f32[3,10,8,256]{3,2,1,0:T(8,128)S(1)}, u32[]{:S(2)}) copy-start(f32[3,10,8,256]{3,2,1,0:T(8,128)S(1)} %collective-permute-done.13.refs_15_) | copy-start | bytes 737284
  36.4 17.2 %collective-permute-start.17 = (f32[3,10,8,256]{3,2,1,0:T(8,128)S(1)}, f32[3,10,8,256]{3,2,1,0:T(8,128)S(1)}, u32[]{:S(2)}, u32[]{:S(2)}) collective-permute-start(f32[3,10,8,256]{3,2,1,0:T(8,128)S(1)} %collective-permute-done.13.refs_15_), channel_id=1, source_target_pairs={{0,1},{1,0},{2,3},{3,2},{4,5},{5,4},{6,7},{7,6},{8,9},{9,8},{10,11... | collective-permute-start | bytes 737288 | tf_op jit(solution)/shard_map/ppermute | solution.py:56
  36.9 14.7 %copy-start.8 = (f32[3,10,8,256]{3,2,1,0:T(8,128)}, f32[3,10,8,256]{3,2,1,0:T(8,128)S(1)}, u32[]{:S(2)}) copy-start(f32[3,10,8,256]{3,2,1,0:T(8,128)S(1)} %collective-permute-done.14.refs_16_) | copy-start | bytes 737284
  36.9 18.8 %collective-permute-start.18 = (f32[3,10,8,256]{3,2,1,0:T(8,128)S(1)}, f32[3,10,8,256]{3,2,1,0:T(8,128)}, u32[]{:S(2)}, u32[]{:S(2)}) collective-permute-start(f32[3,10,8,256]{3,2,1,0:T(8,128)S(1)} %collective-permute-done.14.refs_16_), channel_id=1, source_target_pairs={{0,1},{1,0},{2,3},{3,2},{4,5},{5,4},{6,7},{7,6},{8,9},{9,8},{10,11... | collective-permute-start | bytes 737288 | tf_op jit(solution)/shard_map/ppermute | solution.py:56
  37.0 9.3 %collective-permute-start.3 = (f32[2,2,32,128]{3,2,1,0:T(8,128)}, f32[2,2,32,128]{3,2,1,0:T(8,128)S(1)}, u32[]{:S(2)}, u32[]{:S(2)}) collective-permute-start(f32[2,2,32,128]{3,2,1,0:T(8,128)} %get-tuple-element.24), channel_id=1, source_target_pairs={{0,12},{4,8},{8,4},{12,0},{1,13},{5,9},{9,5},{13,1},{2,14},{6,10},... | collective-permute-start | bytes 196616 | tf_op jit(solution)/shard_map/ppermute | solution.py:56
  46.3 7.3 %collective-permute-start.6 = (f32[2,2,32,128]{3,2,1,0:T(8,128)}, f32[2,2,32,128]{3,2,1,0:T(8,128)S(1)}, u32[]{:S(2)}, u32[]{:S(2)}) collective-permute-start(f32[2,2,32,128]{3,2,1,0:T(8,128)} %get-tuple-element.27), channel_id=1, source_target_pairs={{0,4},{4,0},{8,12},{12,8},{1,5},{5,1},{9,13},{13,9},{2,6},{6,2},{1... | collective-permute-start | bytes 196616 | tf_op jit(solution)/shard_map/ppermute | solution.py:56
  47.2 8.5 %collective-permute-start.7 = (f32[2,2,32,128]{3,2,1,0:T(8,128)}, f32[2,2,32,128]{3,2,1,0:T(8,128)S(1)}, u32[]{:S(2)}, u32[]{:S(2)}) collective-permute-start(f32[2,2,32,128]{3,2,1,0:T(8,128)} %get-tuple-element.28), channel_id=1, source_target_pairs={{0,8},{4,12},{8,0},{12,4},{1,9},{5,13},{9,1},{13,5},{2,10},{6,14},... | collective-permute-start | bytes 196616 | tf_op jit(solution)/shard_map/ppermute | solution.py:56
  48.4 7.3 %collective-permute-start.8 = (f32[2,2,32,128]{3,2,1,0:T(8,128)}, f32[2,2,32,128]{3,2,1,0:T(8,128)S(1)}, u32[]{:S(2)}, u32[]{:S(2)}) collective-permute-start(f32[2,2,32,128]{3,2,1,0:T(8,128)} %get-tuple-element.29), channel_id=1, source_target_pairs={{0,12},{4,8},{8,4},{12,0},{1,13},{5,9},{9,5},{13,1},{2,14},{6,10},... | collective-permute-start | bytes 196616 | tf_op jit(solution)/shard_map/ppermute | solution.py:56
  61.9 4.5 %collective-permute-start.19 = (f32[32,256]{1,0:T(8,128)}, f32[32,256]{1,0:T(8,128)S(1)}, u32[]{:S(2)}, u32[]{:S(2)}) collective-permute-start(f32[32,256]{1,0:T(8,128)} %get-tuple-element.32), channel_id=1, source_target_pairs={{0,4},{4,0},{8,12},{12,8},{1,5},{5,1},{9,13},{13,9},{2,6},{6,2},{1... | collective-permute-start | bytes 98312 | tf_op jit(solution)/shard_map/ppermute | solution.py:56
  63.2 5.4 %collective-permute-start.20 = (f32[32,256]{1,0:T(8,128)}, f32[32,256]{1,0:T(8,128)S(1)}, u32[]{:S(2)}, u32[]{:S(2)}) collective-permute-start(f32[32,256]{1,0:T(8,128)} %get-tuple-element.33), channel_id=1, source_target_pairs={{0,8},{4,12},{8,0},{12,4},{1,9},{5,13},{9,1},{13,5},{2,10},{6,14},... | collective-permute-start | bytes 98312 | tf_op jit(solution)/shard_map/ppermute | solution.py:56
  63.9 5.9 %collective-permute-start.21 = (f32[32,256]{1,0:T(8,128)}, f32[32,256]{1,0:T(8,128)S(1)}, u32[]{:S(2)}, u32[]{:S(2)}) collective-permute-start(f32[32,256]{1,0:T(8,128)} %get-tuple-element.34), channel_id=1, source_target_pairs={{0,12},{4,8},{8,4},{12,0},{1,13},{5,9},{9,5},{13,1},{2,14},{6,10},... | collective-permute-start | bytes 98312 | tf_op jit(solution)/shard_map/ppermute | solution.py:56
  (12 other events, 31.6 us)

commit v2 on v1

v2 whole, which is shorter than its diff:
```python
import functools

import jax
import jax.numpy as jnp
from jax import lax
from jax.experimental import pallas as pl
from jax.experimental.pallas import tpu as pltpu
from jax.sharding import PartitionSpec as P

F32 = jnp.float32
HIGHEST = lax.Precision.HIGHEST
B16 = jnp.bfloat16
VMEM = pl.BlockSpec(memory_space=pltpu.VMEM)
SMEM = pl.BlockSpec(memory_space=pltpu.SMEM)
ANY = pl.BlockSpec(memory_space=pl.ANY)


def product(left, right):
    return jnp.dot(left, right, precision=HIGHEST, preferred_element_type=F32)


def apply_inverse(target, partial_value, inverse_rows):
    rows_here = inverse_rows.shape[0]
    share = lax.psum_scatter(partial_value, "rows", scatter_dimension=0, tiled=True)
    first_own = lax.axis_index("rows") * rows_here
    residue = lax.dynamic_slice_in_dim(target, first_own, rows_here, 0) - share
    return product(inverse_rows, lax.all_gather(residue, "rows", axis=0, tiled=True))


def general(ancestor, panels, row_map, offsets, noise, inverse, inner_link, cross_link):
    block_rows = inverse.shape[3]
    solved = [[None, None], [None, None]]
    for p in (1, 0):
        front_rows = jnp.take(ancestor, row_map[p], axis=0)
        window = lax.dynamic_slice_in_dim(noise, offsets[p], 2 * block_rows, 0)
        for b in (1, 0):
            whole = lax.all_gather(panels[p, b], "samples", axis=1, tiled=True)
            partial_value = product(whole.T, front_rows)
            if b == 0:
                partial_value = partial_value + product(inner_link[p].T, solved[p][1])
            if p == 0:
                for earlier in (0, 1):
                    partial_value = partial_value + product(
                        cross_link[b, earlier].T, solved[1][earlier]
                    )
            target = window[b * block_rows : (b + 1) * block_rows]
            solved[p][b] = apply_inverse(target, partial_value, inverse[p, b])
    return jnp.stack([jnp.stack(solved[0]), jnp.stack(solved[1])])


def exchange(array, axis, mask, size):
    return lax.ppermute(array, axis, [(i, i ^ mask) for i in range(size)])


def near_core(array):
    return pltpu.with_memory_space_constraint(array, pltpu.VMEM)


def params():
    return pltpu.CompilerParams(vmem_limit_bytes=16 * 2**20)


def cost(flops, moved):
    return pl.CostEstimate(flops=flops, bytes_accessed=moved, transcendentals=0)


def halves(value):
    high = value.astype(B16)
    return high, (value - high.astype(F32)).astype(B16)


def dot_t(left, right):
    return lax.dot_general(left, right, (((1,), (1,)), ((), ())), preferred_element_type=F32)


def dot_n(left, right):
    return lax.dot_general(left, right, (((1,), (0,)), ((), ())), preferred_element_type=F32)


def stacked(dot, left, high, low):
    rows = left.shape[0]
    left_high, left_low = halves(left)
    value = dot(jnp.concatenate([left_high, left_low], axis=0), high)
    return value[:rows] + value[rows:] + dot(left_high, low)


def share_kernel(parts, samples, inv_ref, inner_ref, cross_ref, share_ref, sems):
    piece = share_ref.shape[1]
    part = lax.axis_index("groups") * samples + lax.axis_index("samples")
    rows = pl.ds(pl.multiple_of(part * piece, piece), piece)
    copies = []
    at = 0
    for i, ref in enumerate((inv_ref, inner_ref, cross_ref)):
        count = ref.shape[0]
        copies.append(
            pltpu.make_async_copy(
                ref.at[:, rows, :], share_ref.at[at : at + count], sems.at[i]
            )
        )
        at += count
    for copy in copies:
        copy.start()
    for copy in copies:
        copy.wait()


def own_share(inverse, inner, cross, groups, samples):
    parts = groups * samples
    rows_here, block = inverse.shape[1:]
    return pl.pallas_call(
        functools.partial(share_kernel, parts, samples),
        out_shape=pltpu.VMEM((10, rows_here // parts, block), F32),
        in_specs=[ANY] * 3,
        out_specs=VMEM,
        scratch_shapes=[pltpu.SemaphoreType.DMA((3,))],
        compiler_params=params(),
        name="own_share",
    )(inverse, inner, cross)


def front_kernel(map_ref, ancestor_ref, high_ref, low_ref, front):
    k_rows = front.shape[1]
    step = 8
    for p in range(2):

        def body(i, carry):
            base = pl.multiple_of(i * step, step)
            rows = [ancestor_ref[pl.ds(map_ref[p, base + j], 1), :] for j in range(step)]
            front[p, pl.ds(base, step), :] = jnp.concatenate(rows, axis=0)
            return carry

        lax.fori_loop(0, k_rows // step, body, 0, unroll=8)
        high_ref[p], low_ref[p] = halves(front[p].T)


def front_rows(row_map, ancestor):
    k_rows, cols_here = row_map.shape[1], ancestor.shape[1]
    out = pltpu.VMEM((2, cols_here, k_rows), B16)
    return pl.pallas_call(
        front_kernel,
        out_shape=(out, out),
        in_specs=[SMEM, VMEM],
        out_specs=(VMEM, VMEM),
        scratch_shapes=[pltpu.VMEM((2, k_rows, cols_here), F32)],
        cost_estimate=cost(2**22, 2**20),
        compiler_params=params(),
        name="front_rows",
    )(row_map, near_core(ancestor))


def terms_kernel(high_ref, low_ref, one_ref, two_ref, *rest):
    out_refs, hold = rest[:-1], rest[-1]
    row = lax.axis_index("rows")
    ranks, quarter = hold.shape[0], hold.shape[1]
    width = one_ref.shape[1]
    for p in range(2):
        high, low = halves(jnp.concatenate([one_ref[p], two_ref[p]], axis=0))
        value = dot_t(high_ref[p], high) + (dot_t(high_ref[p], low) + dot_t(low_ref[p], high))
        hold[...] = value.reshape(ranks, quarter, value.shape[1])
        for k, out in enumerate(out_refs):
            piece = hold[row ^ k]
            for group in range(2):
                out[group, p] = piece[:, group * width : (group + 1) * width]


def terms(front, one, two, ranks):
    width = one.shape[1]
    quarter = front[0].shape[1] // ranks
    out = pltpu.VMEM((2, 2, quarter, width), F32)
    return pl.pallas_call(
        terms_kernel,
        out_shape=(out,) * ranks,
        in_specs=[VMEM] * 4,
        out_specs=(VMEM,) * ranks,
        scratch_shapes=[pltpu.VMEM((ranks, quarter, 2 * width), F32)],
        cost_estimate=cost(2**26, 2**20),
        compiler_params=params(),
        name="terms",
    )(*front, near_core(one), near_core(two))


def target_kernel(off_ref, noise_ref, out_ref, window, hold, sems):
    ranks, quarter, rows = hold.shape
    span = window.shape[1]
    copies, shifts = [], []
    for p in range(2):
        offset = jnp.clip(off_ref[p], 0, noise_ref.shape[0] - rows)
        start = jnp.minimum((offset // 8) * 8, noise_ref.shape[0] - span)
        shifts.append(offset - start)
        copies.append(
            pltpu.make_async_copy(
                noise_ref.at[pl.ds(pl.multiple_of(start, 8), span), :], window.at[p], sems.at[p]
            )
        )
    for copy in copies:
        copy.start()
    for p in range(2):
        copies[p].wait()
        turned = window[p, pl.ds(shifts[p], rows), :].T
        hold[...] = turned.reshape(ranks, quarter, rows)
        out_ref[p] = hold[lax.axis_index("rows")]


def targets(offsets, noise, rows, ranks):
    cols_here = noise.shape[1]
    quarter = cols_here // ranks
    return pl.pallas_call(
        target_kernel,
        out_shape=pltpu.VMEM((2, quarter, rows), F32),
        in_specs=[SMEM, ANY],
        out_specs=VMEM,
        scratch_shapes=[
            pltpu.VMEM((2, rows + 8, cols_here), F32),
            pltpu.VMEM((ranks, quarter, rows), F32),
            pltpu.SemaphoreType.DMA((2,)),
        ],
        cost_estimate=cost(2**22, 2**20),
        compiler_params=params(),
        name="targets",
    )(offsets, noise)


def assemble_kernel(ranks, samples, masks, inv_ref, inner_ref, cross_ref, *rest):
    shares, (high_ref, low_ref, mats) = rest[: len(masks)], rest[len(masks) :]
    row, sample, group = (lax.axis_index(a) for a in ("rows", "samples", "groups"))
    rows_here = inv_ref.shape[1]
    piece = shares[0].shape[2]
    own = pl.ds(pl.multiple_of(row * rows_here, rows_here), rows_here)
    mats[0:4, own, :] = inv_ref[...]
    mats[4:6, own, :] = inner_ref[...]
    mats[6:10, own, :] = cross_ref[...]
    for (group_mask, sample_mask), ref in zip(masks, shares):
        part = (group ^ group_mask) * samples + (sample ^ sample_mask)
        for k in range(1, ranks):
            start = (row ^ k) * rows_here + part * piece
            mats[:, pl.ds(pl.multiple_of(start, piece), piece), :] = ref[k - 1]
    for m in range(10):
        high_ref[m], low_ref[m] = halves(mats[m])


def assemble(inverse, inner, cross, masks, shares, ranks, samples):
    block = inverse.shape[2]
    out = pltpu.VMEM((10, block, block), B16)
    return pl.pallas_call(
        functools.partial(assemble_kernel, ranks, samples, masks),
        out_shape=(out, out),
        in_specs=[VMEM] * (3 + len(shares)),
        out_specs=(VMEM, VMEM),
        scratch_shapes=[pltpu.VMEM((10, block, block), F32)],
        cost_estimate=cost(2**22, 2**22),
        compiler_params=params(),
        name="assemble",
    )(*(near_core(a) for a in (inverse, inner, cross, *shares)))


def solve_kernel(ranks, samples, target_ref, high_ref, low_ref, *refs):
    first, second = refs[:ranks], refs[ranks : 2 * ranks]
    outs, (sums, ordered) = refs[2 * ranks : 3 * ranks], refs[3 * ranks :]
    row, sample = lax.axis_index("rows"), lax.axis_index("samples")
    block = high_ref.shape[1]
    rows_here = block // ranks
    half = samples // 2
    for stage, pieces in ((0, first), (1, second)):
        for position in range(half):
            total = pieces[0][position]
            for ref in pieces[1:]:
                total = total + ref[position]
            sums[sample ^ (stage * half + position)] = total
    cols = block // samples
    rest = [[None, None], [None, None]]
    for p in range(2):
        for b in range(2):
            value = jnp.concatenate(
                [sums[s, p, :, b * cols : (b + 1) * cols] for s in range(samples)], axis=-1
            )
            rest[p][b] = target_ref[p, :, b * block : (b + 1) * block] - value

    def apply(value, m):
        return stacked(dot_t, value, high_ref[m], low_ref[m])

    def link(value, m):
        return stacked(dot_n, value, high_ref[m], low_ref[m])

    x11 = apply(rest[1][1], 3)
    x10 = apply(rest[1][0] - link(x11, 5), 2)
    x01 = apply(rest[0][1] - link(x11, 9) - link(x10, 8), 1)
    x00 = apply(rest[0][0] - link(x11, 7) - link(x10, 6) - link(x01, 4), 0)
    for j in range(ranks):
        ordered[j] = jnp.concatenate(
            [x[:, j * rows_here : (j + 1) * rows_here] for x in (x00, x01, x10, x11)], axis=-1
        )
    for k, out in enumerate(outs):
        out[...] = ordered[row ^ k]


def solve(target, mats, first, second, samples):
    ranks = len(first)
    quarter = target.shape[1]
    block = mats[0].shape[1]
    out = pltpu.VMEM((quarter, 4 * block // ranks), F32)
    return pl.pallas_call(
        functools.partial(solve_kernel, ranks, samples),
        out_shape=(out,) * ranks,
        in_specs=[VMEM] * (3 + 2 * ranks),
        out_specs=(VMEM,) * ranks,
        scratch_shapes=[
            pltpu.VMEM((samples, 2, quarter, 2 * block // samples), F32),
            pltpu.VMEM((ranks, quarter, 4 * block // ranks), F32),
        ],
        cost_estimate=cost(2**26, 2**21),
        compiler_params=params(),
        name="solve",
    )(*(near_core(a) for a in (target, *mats, *first, *second)))


def place_kernel(ranks, *refs):
    pieces, out_ref, hold = refs[:ranks], refs[ranks], refs[ranks + 1]
    for k, ref in enumerate(pieces):
        hold[lax.axis_index("rows") ^ k] = ref[...]
    quarter, width = hold.shape[1:]
    turned = hold[...].reshape(ranks * quarter, width).T
    rows_here = out_ref.shape[2]
    for p in range(2):
        for b in range(2):
            start = (2 * p + b) * rows_here
            out_ref[p, b] = turned[start : start + rows_here]


def place(pieces):
    ranks = len(pieces)
    quarter, width = pieces[0].shape
    return pl.pallas_call(
        functools.partial(place_kernel, ranks),
        out_shape=jax.ShapeDtypeStruct((2, 2, width // 4, ranks * quarter), F32),
        in_specs=[VMEM] * ranks,
        out_specs=VMEM,
        scratch_shapes=[pltpu.VMEM((ranks, quarter, width), F32)],
        compiler_params=params(),
        name="place",
    )(*(near_core(a) for a in pieces))


def paired(groups, ranks, samples):
    def over_rows(pieces):
        return [pieces[0]] + [exchange(pieces[k], "rows", k, ranks) for k in range(1, ranks)]

    def local(ancestor, panels, row_map, offsets, noise, inverse, inner_link, cross_link):
        block = inverse.shape[3]
        inverse = inverse.reshape((4,) + inverse.shape[2:])
        cross = cross_link.reshape((4,) + cross_link.shape[2:])
        own = jnp.swapaxes(panels, 2, 3)
        own = own.reshape((2, 2 * own.shape[2], own.shape[3]))

        share = own_share(inverse, inner_link, cross, groups, samples)
        far = exchange(own, "samples", 2, samples)
        near = exchange(own, "samples", 1, samples)
        got = [exchange(share, "rows", k, ranks) for k in range(1, ranks)]
        front = front_rows(row_map, ancestor)
        target = targets(offsets, noise, 2 * block, ranks)

        first = over_rows(terms(front, own, near, ranks))
        far_near = exchange(far, "samples", 1, samples)
        second = over_rows(terms(front, far, far_near, ranks))

        here = jnp.stack(got)
        over_x = exchange(here, "samples", 2, samples)
        over_y = exchange(here, "groups", 1, groups)
        over_xy = exchange(over_x, "groups", 1, groups)
        masks = [(0, 0), (0, 2), (1, 0), (1, 2)]
        shares = [here, over_x, over_y, over_xy]
        shares = shares + [exchange(a, "samples", 1, samples) for a in shares]
        masks = masks + [(g, s ^ 1) for g, s in masks]
        mats = assemble(inverse, inner_link, cross, tuple(masks), shares, ranks, samples)

        return place(over_rows(solve(target, mats, first, second, samples)))

    return local


def solution(mesh):
    groups, ranks, samples = (mesh.shape[a] for a in ("groups", "rows", "samples"))
    placed = (
        P(("groups", "rows"), "samples"),
        P(None, None, "rows", "samples"),
        P(None, "rows"),
        P(),
        P("groups", "samples"),
        P(None, None, "rows", None),
        P(None, "rows", None),
        P(None, None, "rows", None),
    )

    def whole(*arrays):
        block, columns = arrays[5].shape[3], arrays[0].shape[1]
        fits = (
            groups == 2
            and samples == 4
            and ranks in (2, 4)
            and block % (ranks * groups * samples * 8) == 0
            and columns % (samples * ranks * 8) == 0
        )
        return jax.shard_map(
            paired(groups, ranks, samples) if fits else general,
            mesh=mesh,
            in_specs=placed,
            out_specs=P(None, None, "rows", ("groups", "samples")),
            check_vma=False,
        )(*arrays)

    return whole
```

time: 72.4 us -> 61 us (0.84)
  Pallas kernels: 17.4 us -> 6.52 us
  waiting for transfers between devices: 16.8 us -> 24.2 us
  between operations: 4.16 us -> 0.19 us
  local copies, waits for them, and re-layouts: 5.39 us -> 3.52 us
  starting transfers between devices: 27.6 us -> 26.3 us
    pallas_call x5 -> x7, Pallas kernels: 15.8 us -> 5.75 us  [the longest x1 1.83 us: front_rows(): pl.pallas_call(front_kernel, out_shape=(out, out), in_specs=[SMEM, VMEM],...]
    ppermute x22, waiting for transfers between devices: 16.8 us -> 24.2 us  [exchange(): return lax.ppermute(array, axis, [(i, i ^ mask) for i in range(size)])]
    ppermute x22, starting transfers between devices: 27.6 us -> 26.3 us  [exchange(): return lax.ppermute(array, axis, [(i, i ^ mask) for i in range(size)])]
    dynamic_slice x1 -> x0, local copies, waits for them, and re-layouts: 0.85 us -> none  [local(): lax.dynamic_slice_in_dim(noise, offsets[p], 2 * block, 0)]
    pallas_call x1, Pallas kernels: 1.58 us -> 0.77 us  [place(): pl.pallas_call(functools.partial(place_kernel, ranks), out_shape=jax.Shap...]
    unnamed x45 -> x22, local copies, waits for them, and re-layouts: 3.94 us -> 3.52 us
  transfers between devices with their start and end apart: 22 -> 22, of which waited for: 9 -> 8; matrix products, arithmetic and copies ran while one was open for 2% -> 0% of each run, Pallas kernels for 11% -> 7%
where the time goes in v2:
time: 61 us; the launch traced here: 60.8 us
  starting transfers between devices  26.3 us (43%)
  waiting for transfers between devices  24.2 us (40%)
  Pallas kernels  6.52 us (11%)
  local copies, waits for them, and re-layouts  3.52 us (6%)
    ppermute x22, starting transfers between devices, exchange(): return lax.ppermute(array, axis, [(i, i ^ mask) for i in range(size)])  26.3 us
    ppermute x22, waiting for transfers between devices, exchange(): return lax.ppermute(array, axis, [(i, i ^ mask) for i in range(size)])  24.2 us
    unnamed x22, local copies, waits for them, and re-layouts  3.52 us
    pallas_call x1, Pallas kernels, front_rows(): pl.pallas_call(front_kernel, out_shape=(out, out), in_specs=[SMEM, VMEM],...  1.83 us
    pallas_call x1, Pallas kernels, solve(): pl.pallas_call(functools.partial(solve_kernel, ranks, samples), out_shape...  1.36 us
  transfers between devices with their start and end apart: 22, of which 8 were waited for; matrix products, arithmetic and copies ran while one was open for 0% of the time, Pallas kernels for 7%

profile of v2, /device:TPU:0, one launch (start us, length us, event | category | flops | bytes accessed | tf_op | source)
XLA Modules:
  0.0 60.8 jit_solution(2610655245556628895)
XLA Ops:
  0.0 0.9 %copy-done = f32[2,2,64,256]{3,2,1,0:T(8,128)S(1)} copy-done((f32[2,2,64,256]{3,2,1,0:T(8,128)S(1)}, f32[2,2,64,256]{3,2,1,0:T(8,128)}, u32[]{:S(2)}) %copy-start) | copy-done | bytes 262168
  1.0 0.9 %copy-done.2 = f32[2,2,64,256]{3,2,1,0:T(8,128)S(1)} copy-done((f32[2,2,64,256]{3,2,1,0:T(8,128)S(1)}, f32[2,2,64,256]{3,2,1,0:T(8,128)}, u32[]{:S(2)}) %copy-start.2) | copy-done | bytes 262168
  1.9 0.9 %copy-done.5 = f32[2,64,256]{2,1,0:T(8,128)S(1)} copy-done((f32[2,64,256]{2,1,0:T(8,128)S(1)}, f32[2,64,256]{2,1,0:T(8,128)}, u32[]{:S(2)}) %copy-start.5) | copy-done | bytes 131096
  2.9 3.1 %collective-permute-start = (f32[10,8,256]{2,1,0:T(8,128)S(1)}, f32[10,8,256]{2,1,0:T(8,128)S(1)}, u32[]{:S(2)}, u32[]{:S(2)}) collective-permute-start(f32[10,8,256]{2,1,0:T(8,128)S(1)} %own_share.1), channel_id=1, source_target_pairs={{0,4},{4,0},{8,12},{12,8},{1,5},{5,1},{9,13},{13,9},{2,6},{6,2},{1... | collective-permute-start | bytes 245768 | tf_op jit(solution)/shard_map/ppermute | solution.py:52
  6.0 2.6 %collective-permute-start.1 = (f32[10,8,256]{2,1,0:T(8,128)S(1)}, f32[10,8,256]{2,1,0:T(8,128)S(1)}, u32[]{:S(2)}, u32[]{:S(2)}) collective-permute-start(f32[10,8,256]{2,1,0:T(8,128)S(1)} %own_share.1), channel_id=1, source_target_pairs={{0,8},{4,12},{8,0},{12,4},{1,9},{5,13},{9,1},{13,5},{2,10},{6,14},... | collective-permute-start | bytes 245768 | tf_op jit(solution)/shard_map/ppermute | solution.py:52
  8.6 6.6 %collective-permute-done.1 = f32[10,8,256]{2,1,0:T(8,128)S(1)} collective-permute-done((f32[10,8,256]{2,1,0:T(8,128)S(1)}, f32[10,8,256]{2,1,0:T(8,128)S(1)}, u32[]{:S(2)}, u32[]{:S(2)}) %collective-permute-start.1) | collective-permute-done | bytes 81952 | tf_op jit(solution)/shard_map/ppermute | solution.py:52
  15.2 1.6 %collective-permute-start.3 = (f32[3,10,8,256]{3,2,1,0:T(8,128)S(1)}, f32[3,10,8,256]{3,2,1,0:T(8,128)S(1)}, u32[]{:S(2)}, u32[]{:S(2)}) collective-permute-start(f32[3,10,8,256]{3,2,1,0:T(8,128)S(1)} %pad_maximum_fusion.rest_0_), channel_id=1, source_target_pairs={{0,2},{1,3},{2,0},{3,1},{4,6},{5,7},{6,4},{7,5},{8,10},{9,11},{10,... | collective-permute-start | bytes 737288 | tf_op jit(solution)/shard_map/ppermute | solution.py:52
  16.8 0.5 collective-permute-start.14
  17.3 1.5 %collective-permute-start.4 = (f32[3,10,8,256]{3,2,1,0:T(8,128)S(1)}, f32[3,10,8,256]{3,2,1,0:T(8,128)S(1)}, u32[]{:S(2)}, u32[]{:S(2)}) collective-permute-start(f32[3,10,8,256]{3,2,1,0:T(8,128)S(1)} %pad_maximum_fusion.rest_0_), channel_id=1, source_target_pairs={{0,16},{16,0},{1,17},{17,1},{2,18},{18,2},{3,19},{19,3},{4,20},{20... | collective-permute-start | bytes 737288 | tf_op jit(solution)/shard_map/ppermute | solution.py:52
  18.8 5.0 %collective-permute-done.3.rest_1_ = f32[3,10,8,256]{3,2,1,0:T(8,128)S(1)} collective-permute-done((f32[3,10,8,256]{3,2,1,0:T(8,128)S(1)}, f32[3,10,8,256]{3,2,1,0:T(8,128)S(1)}, u32[]{:S(2)}, u32[]{:S(2)}) %collective-permute-start.3) | collective-permute-done | bytes 245792 | tf_op jit(solution)/shard_map/ppermute | solution.py:52
  23.8 1.5 %collective-permute-start.5 = (f32[3,10,8,256]{3,2,1,0:T(8,128)S(1)}, f32[3,10,8,256]{3,2,1,0:T(8,128)S(1)}, u32[]{:S(2)}, u32[]{:S(2)}) collective-permute-start(f32[3,10,8,256]{3,2,1,0:T(8,128)S(1)} %collective-permute-done.3.rest_1_), channel_id=1, source_target_pairs={{0,16},{16,0},{1,17},{17,1},{2,18},{18,2},{3,19},{19,3},{4,20},{20... | collective-permute-start | bytes 737288 | tf_op jit(solution)/shard_map/ppermute | solution.py:52
  25.3 1.3 %collective-permute-done.14.one_ref = f32[2,128,256]{2,1,0:T(8,128)S(1)} collective-permute-done((f32[2,128,256]{2,1,0:T(8,128)}, f32[2,128,256]{2,1,0:T(8,128)S(1)}, u32[]{:S(2)}, u32[]{:S(2)}) %collective-permute-start.14) | collective-permute-done | bytes 262176 | tf_op jit(solution)/shard_map/ppermute | solution.py:52
  27.7 3.3 %collective-permute-done.5.rest_3_ = f32[3,10,8,256]{3,2,1,0:T(8,128)S(1)} collective-permute-done((f32[3,10,8,256]{3,2,1,0:T(8,128)S(1)}, f32[3,10,8,256]{3,2,1,0:T(8,128)S(1)}, u32[]{:S(2)}, u32[]{:S(2)}) %collective-permute-start.5) | collective-permute-done | bytes 245792 | tf_op jit(solution)/shard_map/ppermute | solution.py:52
  30.9 0.7 %copy-done.9 = s32[2,256]{1,0:T(2,128)S(1)} copy-done((s32[2,256]{1,0:T(2,128)S(1)}, s32[2,256]{1,0:T(2,128)}, u32[]{:S(2)}) %copy-start.9) | copy-done | bytes 2072
  31.6 1.8 %front_rows.1 = (bf16[2,128,256]{2,1,0:T(8,128)(2,1)S(1)}, bf16[2,128,256]{2,1,0:T(8,128)(2,1)S(1)}) custom-call(s32[2,256]{1,0:T(2,128)S(1)} %copy-done.9, f32[512,128]{1,0:T(8,128)S(1)} %copy-done.8), custom_call_target="tpu_custom_call" | custom-call | flops 4194304 | bytes 1048576 | tf_op jit(solution)/shard_map/front_rows/pallas_call | solution.py:139
  33.9 1.5 %collective-permute-start.11 = (f32[2,2,32,128]{3,2,1,0:T(8,128)S(1)}, f32[2,2,32,128]{3,2,1,0:T(8,128)S(1)}, u32[]{:S(2)}, u32[]{:S(2)}) collective-permute-start(f32[2,2,32,128]{3,2,1,0:T(8,128)S(1)} %get-tuple-element.26), channel_id=1, source_target_pairs={{0,4},{4,0},{8,12},{12,8},{1,5},{5,1},{9,13},{13,9},{2,6},{6,2},{1... | collective-permute-start | bytes 196616 | tf_op jit(solution)/shard_map/ppermute | solution.py:52
  35.9 1.7 %collective-permute-start.12 = (f32[2,2,32,128]{3,2,1,0:T(8,128)S(1)}, f32[2,2,32,128]{3,2,1,0:T(8,128)S(1)}, u32[]{:S(2)}, u32[]{:S(2)}) collective-permute-start(f32[2,2,32,128]{3,2,1,0:T(8,128)S(1)} %get-tuple-element.27), channel_id=1, source_target_pairs={{0,8},{4,12},{8,0},{12,4},{1,9},{5,13},{9,1},{13,5},{2,10},{6,14},... | collective-permute-start | bytes 196616 | tf_op jit(solution)/shard_map/ppermute | solution.py:52
  37.6 1.0 %collective-permute-done.11.refs_1_ = f32[2,2,32,128]{3,2,1,0:T(8,128)S(1)} collective-permute-done((f32[2,2,32,128]{3,2,1,0:T(8,128)S(1)}, f32[2,2,32,128]{3,2,1,0:T(8,128)S(1)}, u32[]{:S(2)}, u32[]{:S(2)}) %collective-permute-start.11) | collective-permute-done | bytes 65568 | tf_op jit(solution)/shard_map/ppermute | solution.py:52
  38.5 2.5 %collective-permute-start.13 = (f32[2,2,32,128]{3,2,1,0:T(8,128)S(1)}, f32[2,2,32,128]{3,2,1,0:T(8,128)S(1)}, u32[]{:S(2)}, u32[]{:S(2)}) collective-permute-start(f32[2,2,32,128]{3,2,1,0:T(8,128)S(1)} %get-tuple-element.28), channel_id=1, source_target_pairs={{0,12},{4,8},{8,4},{12,0},{1,13},{5,9},{9,5},{13,1},{2,14},{6,10},... | collective-permute-start | bytes 196616 | tf_op jit(solution)/shard_map/ppermute | solution.py:52
  41.0 0.9 %collective-permute-start.16 = (f32[2,2,32,128]{3,2,1,0:T(8,128)S(1)}, f32[2,2,32,128]{3,2,1,0:T(8,128)S(1)}, u32[]{:S(2)}, u32[]{:S(2)}) collective-permute-start(f32[2,2,32,128]{3,2,1,0:T(8,128)S(1)} %get-tuple-element.30), channel_id=1, source_target_pairs={{0,4},{4,0},{8,12},{12,8},{1,5},{5,1},{9,13},{13,9},{2,6},{6,2},{1... | collective-permute-start | bytes 196616 | tf_op jit(solution)/shard_map/ppermute | solution.py:52
  41.9 1.0 %collective-permute-start.17 = (f32[2,2,32,128]{3,2,1,0:T(8,128)S(1)}, f32[2,2,32,128]{3,2,1,0:T(8,128)S(1)}, u32[]{:S(2)}, u32[]{:S(2)}) collective-permute-start(f32[2,2,32,128]{3,2,1,0:T(8,128)S(1)} %get-tuple-element.31), channel_id=1, source_target_pairs={{0,8},{4,12},{8,0},{12,4},{1,9},{5,13},{9,1},{13,5},{2,10},{6,14},... | collective-permute-start | bytes 196616 | tf_op jit(solution)/shard_map/ppermute | solution.py:52
  42.9 2.5 %collective-permute-start.18 = (f32[2,2,32,128]{3,2,1,0:T(8,128)S(1)}, f32[2,2,32,128]{3,2,1,0:T(8,128)S(1)}, u32[]{:S(2)}, u32[]{:S(2)}) collective-permute-start(f32[2,2,32,128]{3,2,1,0:T(8,128)S(1)} %get-tuple-element.32), channel_id=1, source_target_pairs={{0,12},{4,8},{8,4},{12,0},{1,13},{5,9},{9,5},{13,1},{2,14},{6,10},... | collective-permute-start | bytes 196616 | tf_op jit(solution)/shard_map/ppermute | solution.py:52
  45.4 0.9 %targets.1.target_ref = f32[2,32,512]{2,1,0:T(8,128)S(1)} custom-call(s32[2]{0:T(128)S(1)} %copy-done.10, f32[2048,128]{1,0:T(8,128)S(1)} %copy-done.4), custom_call_target="tpu_custom_call" | custom-call | flops 4194304 | bytes 1048576 | tf_op jit(solution)/shard_map/targets/pallas_call | solution.py:207
  46.3 0.8 %assemble.1 = (bf16[10,256,256]{2,1,0:T(8,128)(2,1)S(1)}, bf16[10,256,256]{2,1,0:T(8,128)(2,1)S(1)}) custom-call(f32[4,64,256]{2,1,0:T(8,128)S(1)} %bitcast.9, f32[2,64,256]{2,1,0:T(8,128)S(1)} %copy-done.6, f32[4,64,256]{2,1,0:T(8,128)S(1)} %bitcast.11, f32[3,10,8,256]{3,2,1,0:T(8,128)S(1)} %pad_maximum_fusion.rest_0_, ...), custom_call_target="tpu_custom_call" | custom-call | flops 4194304 | bytes 4194304 | tf_op jit(solution)/shard_map/assemble/pallas_call | solution.py:244
  47.1 2.9 %collective-permute-done.17.refs_6_ = f32[2,2,32,128]{3,2,1,0:T(8,128)S(1)} collective-permute-done((f32[2,2,32,128]{3,2,1,0:T(8,128)S(1)}, f32[2,2,32,128]{3,2,1,0:T(8,128)S(1)}, u32[]{:S(2)}, u32[]{:S(2)}) %collective-permute-start.17) | collective-permute-done | bytes 65568 | tf_op jit(solution)/shard_map/ppermute | solution.py:52
  50.0 1.4 %solve.1 = (f32[32,256]{1,0:T(8,128)S(1)}, f32[32,256]{1,0:T(8,128)S(1)}, f32[32,256]{1,0:T(8,128)S(1)}, f32[32,256]{1,0:T(8,128)S(1)}) custom-call(f32[2,32,512]{2,1,0:T(8,128)S(1)} %targets.1.target_ref, bf16[10,256,256]{2,1,0:T(8,128)(2,1)S(1)} %get-tuple-element.21.high_ref, bf16[10,256,256]{2,1,0:T(8,128)(2,1)S(1)} %get-tuple-element.22.low_ref, ...), custom_call_target="tpu_custom_call" | custom-call | flops 67108864 | bytes 2097152 | tf_op jit(solution)/shard_map/solve/pallas_call | solution.py:301
  51.4 1.5 %collective-permute-start.19 = (f32[32,256]{1,0:T(8,128)S(1)}, f32[32,256]{1,0:T(8,128)S(1)}, u32[]{:S(2)}, u32[]{:S(2)}) collective-permute-start(f32[32,256]{1,0:T(8,128)S(1)} %get-tuple-element.34), channel_id=1, source_target_pairs={{0,4},{4,0},{8,12},{12,8},{1,5},{5,1},{9,13},{13,9},{2,6},{6,2},{1... | collective-permute-start | bytes 98312 | tf_op jit(solution)/shard_map/ppermute | solution.py:52
  52.9 1.4 %collective-permute-start.20 = (f32[32,256]{1,0:T(8,128)S(1)}, f32[32,256]{1,0:T(8,128)S(1)}, u32[]{:S(2)}, u32[]{:S(2)}) collective-permute-start(f32[32,256]{1,0:T(8,128)S(1)} %get-tuple-element.35), channel_id=1, source_target_pairs={{0,8},{4,12},{8,0},{12,4},{1,9},{5,13},{9,1},{13,5},{2,10},{6,14},... | collective-permute-start | bytes 98312 | tf_op jit(solution)/shard_map/ppermute | solution.py:52
  54.3 1.5 %collective-permute-start.21 = (f32[32,256]{1,0:T(8,128)S(1)}, f32[32,256]{1,0:T(8,128)S(1)}, u32[]{:S(2)}, u32[]{:S(2)}) collective-permute-start(f32[32,256]{1,0:T(8,128)S(1)} %get-tuple-element.36), channel_id=1, source_target_pairs={{0,12},{4,8},{8,4},{12,0},{1,13},{5,9},{9,5},{13,1},{2,14},{6,10},... | collective-permute-start | bytes 98312 | tf_op jit(solution)/shard_map/ppermute | solution.py:52
  55.8 2.8 %collective-permute-done.20.refs_2_ = f32[32,256]{1,0:T(8,128)S(1)} collective-permute-done((f32[32,256]{1,0:T(8,128)S(1)}, f32[32,256]{1,0:T(8,128)S(1)}, u32[]{:S(2)}, u32[]{:S(2)}) %collective-permute-start.20) | collective-permute-done | bytes 32800 | tf_op jit(solution)/shard_map/ppermute | solution.py:52
  58.6 1.4 %collective-permute-done.21.refs_3_ = f32[32,256]{1,0:T(8,128)S(1)} collective-permute-done((f32[32,256]{1,0:T(8,128)S(1)}, f32[32,256]{1,0:T(8,128)S(1)}, u32[]{:S(2)}, u32[]{:S(2)}) %collective-permute-start.21) | collective-permute-done | bytes 32800 | tf_op jit(solution)/shard_map/ppermute | solution.py:52
  60.0 0.8 %place.1 = f32[2,2,64,128]{3,2,1,0:T(8,128)} custom-call(f32[32,256]{1,0:T(8,128)S(1)} %get-tuple-element.33.refs_0_, f32[32,256]{1,0:T(8,128)S(1)} %collective-permute-done.19.refs_1_, f32[32,256]{1,0:T(8,128)S(1)} %collective-permute-done.20.refs_2_, f32[32,256]{1,0:T(8,128)S(1)} %collective-permute-done.21.refs_3_), custom_call_target="tpu_custom_call" | custom-call | tf_op jit(solution)/shard_map/place/pallas_call | solution.py:332
  (43 shorter events, 2.0 us)
Async XLA Ops:
  0.0 0.9 %copy-start = (f32[2,2,64,256]{3,2,1,0:T(8,128)S(1)}, f32[2,2,64,256]{3,2,1,0:T(8,128)}, u32[]{:S(2)}) copy-start(f32[2,2,64,256]{3,2,1,0:T(8,128)} %param.13) | copy-start | bytes 786436
  1.0 0.9 %copy-start.2 = (f32[2,2,64,256]{3,2,1,0:T(8,128)S(1)}, f32[2,2,64,256]{3,2,1,0:T(8,128)}, u32[]{:S(2)}) copy-start(f32[2,2,64,256]{3,2,1,0:T(8,128)} %param.15) | copy-start | bytes 786436
  1.9 0.9 %copy-start.5 = (f32[2,64,256]{2,1,0:T(8,128)S(1)}, f32[2,64,256]{2,1,0:T(8,128)}, u32[]{:S(2)}) copy-start(f32[2,64,256]{2,1,0:T(8,128)} %inner_ref.3) | copy-start | bytes 393220
  2.8 28.1 %copy-start.8 = (f32[512,128]{1,0:T(8,128)S(1)}, f32[512,128]{1,0:T(8,128)}, u32[]{:S(2)}) copy-start(f32[512,128]{1,0:T(8,128)} %ancestor_ref.1) | copy-start | bytes 786436
  2.8 30.6 %copy-start.7 = (f32[2,2,256,64]{2,3,1,0:T(8,128)S(1)}, f32[2,2,256,64]{2,3,1,0:T(8,128)}, u32[]{:S(2)}) copy-start(f32[2,2,256,64]{2,3,1,0:T(8,128)} %param.9) | copy-start | bytes 786436
  2.8 42.6 %copy-start.10 = (s32[2]{0:T(128)S(1)}, s32[2]{0:T(128)}, u32[]{:S(2)}) copy-start(s32[2]{0:T(128)} %off_ref.1) | copy-start | bytes 28
  2.9 42.5 %copy-start.4 = (f32[2048,128]{1,0:T(8,128)S(1)}, f32[2048,128]{1,0:T(8,128)}, u32[]{:S(2)}) copy-start(f32[2048,128]{1,0:T(8,128)} %noise_ref.1) | copy-start | bytes 3145732
  2.9 5.7 %collective-permute-start = (f32[10,8,256]{2,1,0:T(8,128)S(1)}, f32[10,8,256]{2,1,0:T(8,128)S(1)}, u32[]{:S(2)}, u32[]{:S(2)}) collective-permute-start(f32[10,8,256]{2,1,0:T(8,128)S(1)} %own_share.1), channel_id=1, source_target_pairs={{0,4},{4,0},{8,12},{12,8},{1,5},{5,1},{9,13},{13,9},{2,6},{6,2},{1... | collective-permute-start | bytes 245768 | tf_op jit(solution)/shard_map/ppermute | solution.py:52
  6.0 9.2 %collective-permute-start.1 = (f32[10,8,256]{2,1,0:T(8,128)S(1)}, f32[10,8,256]{2,1,0:T(8,128)S(1)}, u32[]{:S(2)}, u32[]{:S(2)}) collective-permute-start(f32[10,8,256]{2,1,0:T(8,128)S(1)} %own_share.1), channel_id=1, source_target_pairs={{0,8},{4,12},{8,0},{12,4},{1,9},{5,13},{9,1},{13,5},{2,10},{6,14},... | collective-permute-start | bytes 245768 | tf_op jit(solution)/shard_map/ppermute | solution.py:52
  8.6 6.6 %collective-permute-start.2 = (f32[10,8,256]{2,1,0:T(8,128)S(1)}, f32[10,8,256]{2,1,0:T(8,128)S(1)}, u32[]{:S(2)}, u32[]{:S(2)}) collective-permute-start(f32[10,8,256]{2,1,0:T(8,128)S(1)} %own_share.1), channel_id=1, source_target_pairs={{0,12},{4,8},{8,4},{12,0},{1,13},{5,9},{9,5},{13,1},{2,14},{6,10},... | collective-permute-start | bytes 245768 | tf_op jit(solution)/shard_map/ppermute | solution.py:52
  15.2 8.6 %collective-permute-start.3 = (f32[3,10,8,256]{3,2,1,0:T(8,128)S(1)}, f32[3,10,8,256]{3,2,1,0:T(8,128)S(1)}, u32[]{:S(2)}, u32[]{:S(2)}) collective-permute-start(f32[3,10,8,256]{3,2,1,0:T(8,128)S(1)} %pad_maximum_fusion.rest_0_), channel_id=1, source_target_pairs={{0,2},{1,3},{2,0},{3,1},{4,6},{5,7},{6,4},{7,5},{8,10},{9,11},{10,... | collective-permute-start | bytes 737288 | tf_op jit(solution)/shard_map/ppermute | solution.py:52
  16.8 9.9 %collective-permute-start.14 = (f32[2,128,256]{2,1,0:T(8,128)}, f32[2,128,256]{2,1,0:T(8,128)S(1)}, u32[]{:S(2)}, u32[]{:S(2)}) collective-permute-start(f32[2,128,256]{2,1,0:T(8,128)} %bitcast.12), channel_id=1, source_target_pairs={{0,2},{1,3},{2,0},{3,1},{4,6},{5,7},{6,4},{7,5},{8,10},{9,11},{10,... | collective-permute-start | bytes 786440 | tf_op jit(solution)/shard_map/ppermute | solution.py:52
  17.3 9.9 %collective-permute-start.10 = (f32[2,128,256]{2,1,0:T(8,128)}, f32[2,128,256]{2,1,0:T(8,128)S(1)}, u32[]{:S(2)}, u32[]{:S(2)}) collective-permute-start(f32[2,128,256]{2,1,0:T(8,128)} %bitcast.13), channel_id=1, source_target_pairs={{0,1},{1,0},{2,3},{3,2},{4,5},{5,4},{6,7},{7,6},{8,9},{9,8},{10,11... | collective-permute-start | bytes 786440 | tf_op jit(solution)/shard_map/ppermute | solution.py:52
  17.3 9.9 %collective-permute-start.4 = (f32[3,10,8,256]{3,2,1,0:T(8,128)S(1)}, f32[3,10,8,256]{3,2,1,0:T(8,128)S(1)}, u32[]{:S(2)}, u32[]{:S(2)}) collective-permute-start(f32[3,10,8,256]{3,2,1,0:T(8,128)S(1)} %pad_maximum_fusion.rest_0_), channel_id=1, source_target_pairs={{0,16},{16,0},{1,17},{17,1},{2,18},{18,2},{3,19},{19,3},{4,20},{20... | collective-permute-start | bytes 737288 | tf_op jit(solution)/shard_map/ppermute | solution.py:52
  23.8 7.1 %collective-permute-start.5 = (f32[3,10,8,256]{3,2,1,0:T(8,128)S(1)}, f32[3,10,8,256]{3,2,1,0:T(8,128)S(1)}, u32[]{:S(2)}, u32[]{:S(2)}) collective-permute-start(f32[3,10,8,256]{3,2,1,0:T(8,128)S(1)} %collective-permute-done.3.rest_1_), channel_id=1, source_target_pairs={{0,16},{16,0},{1,17},{17,1},{2,18},{18,2},{3,19},{19,3},{4,20},{20... | collective-permute-start | bytes 737288 | tf_op jit(solution)/shard_map/ppermute | solution.py:52
  26.6 7.3 %collective-permute-start.15 = (f32[2,128,256]{2,1,0:T(8,128)S(1)}, f32[2,128,256]{2,1,0:T(8,128)S(1)}, u32[]{:S(2)}, u32[]{:S(2)}) collective-permute-start(f32[2,128,256]{2,1,0:T(8,128)S(1)} %collective-permute-done.14.one_ref), channel_id=1, source_target_pairs={{0,1},{1,0},{2,3},{3,2},{4,5},{5,4},{6,7},{7,6},{8,9},{9,8},{10,11... | collective-permute-start | bytes 786440 | tf_op jit(solution)/shard_map/ppermute | solution.py:52
  26.6 9.2 %collective-permute-start.6 = (f32[3,10,8,256]{3,2,1,0:T(8,128)S(1)}, f32[3,10,8,256]{3,2,1,0:T(8,128)S(1)}, u32[]{:S(2)}, u32[]{:S(2)}) collective-permute-start(f32[3,10,8,256]{3,2,1,0:T(8,128)S(1)} %pad_maximum_fusion.rest_0_), channel_id=1, source_target_pairs={{0,1},{1,0},{2,3},{3,2},{4,5},{5,4},{6,7},{7,6},{8,9},{9,8},{10,11... | collective-permute-start | bytes 737288 | tf_op jit(solution)/shard_map/ppermute | solution.py:52
  27.1 13.8 %collective-permute-start.7 = (f32[3,10,8,256]{3,2,1,0:T(8,128)S(1)}, f32[3,10,8,256]{3,2,1,0:T(8,128)S(1)}, u32[]{:S(2)}, u32[]{:S(2)}) collective-permute-start(f32[3,10,8,256]{3,2,1,0:T(8,128)S(1)} %collective-permute-done.3.rest_1_), channel_id=1, source_target_pairs={{0,1},{1,0},{2,3},{3,2},{4,5},{5,4},{6,7},{7,6},{8,9},{9,8},{10,11... | collective-permute-start | bytes 737288 | tf_op jit(solution)/shard_map/ppermute | solution.py:52
  27.2 14.8 %collective-permute-start.8 = (f32[3,10,8,256]{3,2,1,0:T(8,128)S(1)}, f32[3,10,8,256]{3,2,1,0:T(8,128)S(1)}, u32[]{:S(2)}, u32[]{:S(2)}) collective-permute-start(f32[3,10,8,256]{3,2,1,0:T(8,128)S(1)} %collective-permute-done.4.rest_2_), channel_id=1, source_target_pairs={{0,1},{1,0},{2,3},{3,2},{4,5},{5,4},{6,7},{7,6},{8,9},{9,8},{10,11... | collective-permute-start | bytes 737288 | tf_op jit(solution)/shard_map/ppermute | solution.py:52
  30.9 12.0 %collective-permute-start.9 = (f32[3,10,8,256]{3,2,1,0:T(8,128)S(1)}, f32[3,10,8,256]{3,2,1,0:T(8,128)S(1)}, u32[]{:S(2)}, u32[]{:S(2)}) collective-permute-start(f32[3,10,8,256]{3,2,1,0:T(8,128)S(1)} %collective-permute-done.5.rest_3_), channel_id=1, source_target_pairs={{0,1},{1,0},{2,3},{3,2},{4,5},{5,4},{6,7},{7,6},{8,9},{9,8},{10,11... | collective-permute-start | bytes 737288 | tf_op jit(solution)/shard_map/ppermute | solution.py:52
  33.5 12.8 %copy-start.1 = (f32[2,2,64,256]{3,2,1,0:T(8,128)S(1)}, f32[2,2,64,256]{3,2,1,0:T(8,128)}, u32[]{:S(2)}) copy-start(f32[2,2,64,256]{3,2,1,0:T(8,128)} %param.13) | copy-start | bytes 786436
  33.5 12.8 %copy-start.3 = (f32[2,2,64,256]{3,2,1,0:T(8,128)S(1)}, f32[2,2,64,256]{3,2,1,0:T(8,128)}, u32[]{:S(2)}) copy-start(f32[2,2,64,256]{3,2,1,0:T(8,128)} %param.15) | copy-start | bytes 786436
  33.5 12.8 %copy-start.6 = (f32[2,64,256]{2,1,0:T(8,128)S(1)}, f32[2,64,256]{2,1,0:T(8,128)}, u32[]{:S(2)}) copy-start(f32[2,64,256]{2,1,0:T(8,128)} %inner_ref.3) | copy-start | bytes 393220
  33.9 4.6 %collective-permute-start.11 = (f32[2,2,32,128]{3,2,1,0:T(8,128)S(1)}, f32[2,2,32,128]{3,2,1,0:T(8,128)S(1)}, u32[]{:S(2)}, u32[]{:S(2)}) collective-permute-start(f32[2,2,32,128]{3,2,1,0:T(8,128)S(1)} %get-tuple-element.26), channel_id=1, source_target_pairs={{0,4},{4,0},{8,12},{12,8},{1,5},{5,1},{9,13},{13,9},{2,6},{6,2},{1... | collective-permute-start | bytes 196616 | tf_op jit(solution)/shard_map/ppermute | solution.py:52
  35.9 11.2 %collective-permute-start.12 = (f32[2,2,32,128]{3,2,1,0:T(8,128)S(1)}, f32[2,2,32,128]{3,2,1,0:T(8,128)S(1)}, u32[]{:S(2)}, u32[]{:S(2)}) collective-permute-start(f32[2,2,32,128]{3,2,1,0:T(8,128)S(1)} %get-tuple-element.27), channel_id=1, source_target_pairs={{0,8},{4,12},{8,0},{12,4},{1,9},{5,13},{9,1},{13,5},{2,10},{6,14},... | collective-permute-start | bytes 196616 | tf_op jit(solution)/shard_map/ppermute | solution.py:52
  38.5 8.6 %collective-permute-start.13 = (f32[2,2,32,128]{3,2,1,0:T(8,128)S(1)}, f32[2,2,32,128]{3,2,1,0:T(8,128)S(1)}, u32[]{:S(2)}, u32[]{:S(2)}) collective-permute-start(f32[2,2,32,128]{3,2,1,0:T(8,128)S(1)} %get-tuple-element.28), channel_id=1, source_target_pairs={{0,12},{4,8},{8,4},{12,0},{1,13},{5,9},{9,5},{13,1},{2,14},{6,10},... | collective-permute-start | bytes 196616 | tf_op jit(solution)/shard_map/ppermute | solution.py:52
  41.0 6.1 %collective-permute-start.16 = (f32[2,2,32,128]{3,2,1,0:T(8,128)S(1)}, f32[2,2,32,128]{3,2,1,0:T(8,128)S(1)}, u32[]{:S(2)}, u32[]{:S(2)}) collective-permute-start(f32[2,2,32,128]{3,2,1,0:T(8,128)S(1)} %get-tuple-element.30), channel_id=1, source_target_pairs={{0,4},{4,0},{8,12},{12,8},{1,5},{5,1},{9,13},{13,9},{2,6},{6,2},{1... | collective-permute-start | bytes 196616 | tf_op jit(solution)/shard_map/ppermute | solution.py:52
  41.9 8.1 %collective-permute-start.17 = (f32[2,2,32,128]{3,2,1,0:T(8,128)S(1)}, f32[2,2,32,128]{3,2,1,0:T(8,128)S(1)}, u32[]{:S(2)}, u32[]{:S(2)}) collective-permute-start(f32[2,2,32,128]{3,2,1,0:T(8,128)S(1)} %get-tuple-element.31), channel_id=1, source_target_pairs={{0,8},{4,12},{8,0},{12,4},{1,9},{5,13},{9,1},{13,5},{2,10},{6,14},... | collective-permute-start | bytes 196616 | tf_op jit(solution)/shard_map/ppermute | solution.py:52
  42.9 7.1 %collective-permute-start.18 = (f32[2,2,32,128]{3,2,1,0:T(8,128)S(1)}, f32[2,2,32,128]{3,2,1,0:T(8,128)S(1)}, u32[]{:S(2)}, u32[]{:S(2)}) collective-permute-start(f32[2,2,32,128]{3,2,1,0:T(8,128)S(1)} %get-tuple-element.32), channel_id=1, source_target_pairs={{0,12},{4,8},{8,4},{12,0},{1,13},{5,9},{9,5},{13,1},{2,14},{6,10},... | collective-permute-start | bytes 196616 | tf_op jit(solution)/shard_map/ppermute | solution.py:52
  51.4 4.5 %collective-permute-start.19 = (f32[32,256]{1,0:T(8,128)S(1)}, f32[32,256]{1,0:T(8,128)S(1)}, u32[]{:S(2)}, u32[]{:S(2)}) collective-permute-start(f32[32,256]{1,0:T(8,128)S(1)} %get-tuple-element.34), channel_id=1, source_target_pairs={{0,4},{4,0},{8,12},{12,8},{1,5},{5,1},{9,13},{13,9},{2,6},{6,2},{1... | collective-permute-start | bytes 98312 | tf_op jit(solution)/shard_map/ppermute | solution.py:52
  52.9 5.7 %collective-permute-start.20 = (f32[32,256]{1,0:T(8,128)S(1)}, f32[32,256]{1,0:T(8,128)S(1)}, u32[]{:S(2)}, u32[]{:S(2)}) collective-permute-start(f32[32,256]{1,0:T(8,128)S(1)} %get-tuple-element.35), channel_id=1, source_target_pairs={{0,8},{4,12},{8,0},{12,4},{1,9},{5,13},{9,1},{13,5},{2,10},{6,14},... | collective-permute-start | bytes 98312 | tf_op jit(solution)/shard_map/ppermute | solution.py:52
  54.3 5.7 %collective-permute-start.21 = (f32[32,256]{1,0:T(8,128)S(1)}, f32[32,256]{1,0:T(8,128)S(1)}, u32[]{:S(2)}, u32[]{:S(2)}) collective-permute-start(f32[32,256]{1,0:T(8,128)S(1)} %get-tuple-element.36), channel_id=1, source_target_pairs={{0,12},{4,8},{8,4},{12,0},{1,13},{5,9},{9,5},{13,1},{2,14},{6,10},... | collective-permute-start | bytes 98312 | tf_op jit(solution)/shard_map/ppermute | solution.py:52
  (1 other events, 0.7 us)

commit v3 on v2

--- a/solution.py
+++ b/solution.py
@@ -52,8 +52,21 @@
     return lax.ppermute(array, axis, [(i, i ^ mask) for i in range(size)])
 
 
+def with_after(kernel, count, after):
+    extra = len(after)
+
+    def body(*refs):
+        return kernel(*refs[:count], *refs[count + extra :])
+
+    return body
+
+
 def near_core(array):
     return pltpu.with_memory_space_constraint(array, pltpu.VMEM)
+
+
+def far_memory(array):
+    return pltpu.with_memory_space_constraint(array, pltpu.HBM)
 
 
 def params():
@@ -84,38 +97,38 @@
     return value[:rows] + value[rows:] + dot(left_high, low)
 
 
-def share_kernel(parts, samples, inv_ref, inner_ref, cross_ref, share_ref, sems):
+def share_kernel(samples, *refs):
+    sources, (share_ref, *fetched), sems = refs[:5], refs[5:8], refs[8]
+    inv_ref, inner_ref, cross_ref, *whole = sources
     piece = share_ref.shape[1]
     part = lax.axis_index("groups") * samples + lax.axis_index("samples")
     rows = pl.ds(pl.multiple_of(part * piece, piece), piece)
-    copies = []
-    at = 0
-    for i, ref in enumerate((inv_ref, inner_ref, cross_ref)):
-        count = ref.shape[0]
-        copies.append(
-            pltpu.make_async_copy(
-                ref.at[:, rows, :], share_ref.at[at : at + count], sems.at[i]
-            )
-        )
-        at += count
+    pairs, at = [], 0
+    for ref in (inv_ref, inner_ref, cross_ref):
+        pairs.append((ref.at[:, rows, :], share_ref.at[at : at + ref.shape[0]]))
+        at += ref.shape[0]
+    pairs += list(zip(whole, fetched))
+    copies = [pltpu.make_async_copy(*pair, sems.at[i]) for i, pair in enumerate(pairs)]
     for copy in copies:
         copy.start()
     for copy in copies:
         copy.wait()
 
 
-def own_share(inverse, inner, cross, groups, samples):
+def own_share(inverse, inner, cross, whole, groups, samples):
     parts = groups * samples
     rows_here, block = inverse.shape[1:]
     return pl.pallas_call(
-        functools.partial(share_kernel, parts, samples),
-        out_shape=pltpu.VMEM((10, rows_here // parts, block), F32),
-        in_specs=[ANY] * 3,
-        out_specs=VMEM,
-        scratch_shapes=[pltpu.SemaphoreType.DMA((3,))],
-        compiler_params=params(),
+        functools.partial(share_kernel, samples),
+        out_shape=(pltpu.VMEM((10, rows_here // parts, block), F32),)
+        + tuple(pltpu.VMEM(a.shape, a.dtype) for a in whole),
+        in_specs=[ANY] * (3 + len(whole)),
+        out_specs=(VMEM,) * (1 + len(whole)),
+        scratch_shapes=[pltpu.SemaphoreType.DMA((3 + len(whole),))],
+        compiler_params=params(),
+        cost_estimate=cost(1, 1),
         name="own_share",
-    )(inverse, inner, cross)
+    )(*(far_memory(a) for a in (inverse, inner, cross, *whole)))
 
 
 def front_kernel(map_ref, ancestor_ref, high_ref, low_ref, front):
@@ -142,41 +155,81 @@
         in_specs=[SMEM, VMEM],
         out_specs=(VMEM, VMEM),
         scratch_shapes=[pltpu.VMEM((2, k_rows, cols_here), F32)],
-        cost_estimate=cost(2**22, 2**20),
+        cost_estimate=cost(1, 1),
         compiler_params=params(),
         name="front_rows",
-    )(row_map, near_core(ancestor))
-
-
-def terms_kernel(high_ref, low_ref, one_ref, two_ref, *rest):
-    out_refs, hold = rest[:-1], rest[-1]
+    )(far_memory(row_map), near_core(ancestor))
+
+
+def gather_kernel(count, *refs):
+    pieces, out_ref = refs[:count], refs[-1]
+    at = 0
+    for ref in pieces:
+        out_ref[at : at + ref.shape[0]] = ref[...]
+        at += ref.shape[0]
+
+
+def gathered(pieces, after):
+    total = sum(piece.shape[0] for piece in pieces)
+    return pl.pallas_call(
+        functools.partial(gather_kernel, len(pieces)),
+        out_shape=pltpu.VMEM((total,) + pieces[0].shape[1:], F32),
+        in_specs=[VMEM] * (len(pieces) + len(after)),
+        out_specs=VMEM,
+        compiler_params=params(),
+        cost_estimate=cost(1, 1),
+        name="gathered",
+    )(*(near_core(a) for a in (*pieces, *after)))
+
+
+def terms_kernel(high_ref, low_ref, *refs):
+    group_refs, (keep_ref, send_ref, hold) = refs[:-3], refs[-3:]
     row = lax.axis_index("rows")
     ranks, quarter = hold.shape[0], hold.shape[1]
-    width = one_ref.shape[1]
-    for p in range(2):
-        high, low = halves(jnp.concatenate([one_ref[p], two_ref[p]], axis=0))
+    width = group_refs[0].shape[1]
+    for p in range(2):
+        high, low = halves(jnp.concatenate([ref[p] for ref in group_refs], axis=0))
         value = dot_t(high_ref[p], high) + (dot_t(high_ref[p], low) + dot_t(low_ref[p], high))
         hold[...] = value.reshape(ranks, quarter, value.shape[1])
-        for k, out in enumerate(out_refs):
-            piece = hold[row ^ k]
-            for group in range(2):
-                out[group, p] = piece[:, group * width : (group + 1) * width]
-
-
-def terms(front, one, two, ranks):
-    width = one.shape[1]
+        for i in range(ranks // 2):
+            for ref, mask in ((keep_ref, 3 * i), (send_ref, 3 * i ^ 1)):
+                piece = hold[row ^ mask]
+                for group in range(len(group_refs)):
+                    ref[i, group, p] = piece[:, group * width : (group + 1) * width]
+
+
+def terms(front, columns, ranks, after=()):
+    width = columns[0].shape[1]
     quarter = front[0].shape[1] // ranks
-    out = pltpu.VMEM((2, 2, quarter, width), F32)
-    return pl.pallas_call(
-        terms_kernel,
-        out_shape=(out,) * ranks,
-        in_specs=[VMEM] * 4,
-        out_specs=(VMEM,) * ranks,
-        scratch_shapes=[pltpu.VMEM((ranks, quarter, 2 * width), F32)],
-        cost_estimate=cost(2**26, 2**20),
-        compiler_params=params(),
+    out = pltpu.VMEM((ranks // 2, len(columns), 2, quarter, width), F32)
+    return pl.pallas_call(
+        with_after(terms_kernel, 2 + len(columns), after),
+        out_shape=(out, out),
+        in_specs=[VMEM] * (2 + len(columns) + len(after)),
+        out_specs=(VMEM,) * 2,
+        scratch_shapes=[pltpu.VMEM((ranks, quarter, len(columns) * width), F32)],
+        compiler_params=params(),
+        cost_estimate=cost(1, 1),
         name="terms",
-    )(*front, near_core(one), near_core(two))
+    )(*(near_core(a) for a in (*front, *columns, *after)))
+
+
+def fold_kernel(keep_ref, got_ref, own_ref, send_ref):
+    own_ref[...] = keep_ref[0] + got_ref[0]
+    send_ref[...] = keep_ref[1] + got_ref[1]
+
+
+def fold(keep, got, after=()):
+    out = pltpu.VMEM(keep.shape[1:], F32)
+    return pl.pallas_call(
+        with_after(fold_kernel, 2, after),
+        out_shape=(out, out),
+        in_specs=[VMEM] * (2 + len(after)),
+        out_specs=(VMEM,) * 2,
+        compiler_params=params(),
+        cost_estimate=cost(1, 1),
+        name="fold",
+    )(*(near_core(a) for a in (keep, got, *after)))
 
 
 def target_kernel(off_ref, noise_ref, out_ref, window, hold, sems):
@@ -201,23 +254,23 @@
         out_ref[p] = hold[lax.axis_index("rows")]
 
 
-def targets(offsets, noise, rows, ranks):
+def targets(offsets, noise, rows, ranks, after=()):
     cols_here = noise.shape[1]
     quarter = cols_here // ranks
     return pl.pallas_call(
-        target_kernel,
+        with_after(target_kernel, 2, after),
         out_shape=pltpu.VMEM((2, quarter, rows), F32),
-        in_specs=[SMEM, ANY],
+        in_specs=[SMEM, ANY] + [VMEM] * len(after),
         out_specs=VMEM,
         scratch_shapes=[
             pltpu.VMEM((2, rows + 8, cols_here), F32),
             pltpu.VMEM((ranks, quarter, rows), F32),
             pltpu.SemaphoreType.DMA((2,)),
         ],
-        cost_estimate=cost(2**22, 2**20),
+        cost_estimate=cost(1, 1),
         compiler_params=params(),
         name="targets",
-    )(offsets, noise)
+    )(offsets, far_memory(noise), *(near_core(a) for a in after))
 
 
 def assemble_kernel(ranks, samples, masks, inv_ref, inner_ref, cross_ref, *rest):
@@ -229,11 +282,12 @@
     mats[0:4, own, :] = inv_ref[...]
     mats[4:6, own, :] = inner_ref[...]
     mats[6:10, own, :] = cross_ref[...]
-    for (group_mask, sample_mask), ref in zip(masks, shares):
-        part = (group ^ group_mask) * samples + (sample ^ sample_mask)
-        for k in range(1, ranks):
-            start = (row ^ k) * rows_here + part * piece
-            mats[:, pl.ds(pl.multiple_of(start, piece), piece), :] = ref[k - 1]
+    for pair, ref in zip(masks, shares):
+        for j, (group_mask, sample_mask) in enumerate(pair):
+            part = (group ^ group_mask) * samples + (sample ^ sample_mask)
+            for i, k in enumerate((3, 1, 2)):
+                start = (row ^ k) * rows_here + part * piece
+                mats[:, pl.ds(pl.multiple_of(start, piece), piece), :] = ref[3 * j + i]
     for m in range(10):
         high_ref[m], low_ref[m] = halves(mats[m])
 
@@ -247,25 +301,19 @@
         in_specs=[VMEM] * (3 + len(shares)),
         out_specs=(VMEM, VMEM),
         scratch_shapes=[pltpu.VMEM((10, block, block), F32)],
-        cost_estimate=cost(2**22, 2**22),
+        cost_estimate=cost(1, 1),
         compiler_params=params(),
         name="assemble",
     )(*(near_core(a) for a in (inverse, inner, cross, *shares)))
 
 
 def solve_kernel(ranks, samples, target_ref, high_ref, low_ref, *refs):
-    first, second = refs[:ranks], refs[ranks : 2 * ranks]
-    outs, (sums, ordered) = refs[2 * ranks : 3 * ranks], refs[3 * ranks :]
+    (kept_ref, got_ref), outs, (sums, ordered) = refs[:2], refs[2 : 2 + ranks], refs[2 + ranks :]
     row, sample = lax.axis_index("rows"), lax.axis_index("samples")
     block = high_ref.shape[1]
     rows_here = block // ranks
-    half = samples // 2
-    for stage, pieces in ((0, first), (1, second)):
-        for position in range(half):
-            total = pieces[0][position]
-            for ref in pieces[1:]:
-                total = total + ref[position]
-            sums[sample ^ (stage * half + position)] = total
+    for i in range(samples):
+        sums[sample ^ i] = kept_ref[i] + got_ref[i]
     cols = block // samples
     rest = [[None, None], [None, None]]
     for p in range(2):
@@ -293,24 +341,23 @@
         out[...] = ordered[row ^ k]
 
 
-def solve(target, mats, first, second, samples):
-    ranks = len(first)
+def solve(target, mats, parts, ranks, samples):
     quarter = target.shape[1]
     block = mats[0].shape[1]
     out = pltpu.VMEM((quarter, 4 * block // ranks), F32)
     return pl.pallas_call(
         functools.partial(solve_kernel, ranks, samples),
         out_shape=(out,) * ranks,
-        in_specs=[VMEM] * (3 + 2 * ranks),
+        in_specs=[VMEM] * 5,
         out_specs=(VMEM,) * ranks,
         scratch_shapes=[
             pltpu.VMEM((samples, 2, quarter, 2 * block // samples), F32),
             pltpu.VMEM((ranks, quarter, 4 * block // ranks), F32),
         ],
-        cost_estimate=cost(2**26, 2**21),
+        cost_estimate=cost(1, 1),
         compiler_params=params(),
         name="solve",
-    )(*(near_core(a) for a in (target, *mats, *first, *second)))
+    )(*(near_core(a) for a in (target, *mats, *parts)))
 
 
 def place_kernel(ranks, *refs):
@@ -336,6 +383,7 @@
         out_specs=VMEM,
         scratch_shapes=[pltpu.VMEM((ranks, quarter, width), F32)],
         compiler_params=params(),
+        cost_estimate=cost(1, 1),
         name="place",
     )(*(near_core(a) for a in pieces))
 
@@ -351,28 +399,40 @@
         own = jnp.swapaxes(panels, 2, 3)
         own = own.reshape((2, 2 * own.shape[2], own.shape[3]))
 
-        share = own_share(inverse, inner_link, cross, groups, samples)
-        far = exchange(own, "samples", 2, samples)
-        near = exchange(own, "samples", 1, samples)
-        got = [exchange(share, "rows", k, ranks) for k in range(1, ranks)]
-        front = front_rows(row_map, ancestor)
-        target = targets(offsets, noise, 2 * block, ranks)
-
-        first = over_rows(terms(front, own, near, ranks))
+        share, fetched, moved = own_share(
+            inverse, inner_link, cross, (ancestor, own), groups, samples
+        )
+        share = share[None]
+        across = exchange(share, "rows", 3, ranks)
+        far = exchange(moved, "samples", 2, samples)
+        near = exchange(moved, "samples", 1, samples)
+        front = front_rows(row_map, fetched)
+        pair = gathered([share, across], front)
+        beside = exchange(pair, "rows", 1, ranks)
+        target = targets(offsets, noise, 2 * block, ranks, (pair,))
+        far = gathered([far], (pair,))
         far_near = exchange(far, "samples", 1, samples)
-        second = over_rows(terms(front, far, far_near, ranks))
-
-        here = jnp.stack(got)
+        kept, sent = terms(front, (moved, near, far, far_near), ranks, (target,))
+        got = exchange(sent, "rows", 1, ranks)
+        here = gathered([across, beside], (sent,))
         over_x = exchange(here, "samples", 2, samples)
         over_y = exchange(here, "groups", 1, groups)
-        over_xy = exchange(over_x, "groups", 1, groups)
-        masks = [(0, 0), (0, 2), (1, 0), (1, 2)]
-        shares = [here, over_x, over_y, over_xy]
-        shares = shares + [exchange(a, "samples", 1, samples) for a in shares]
-        masks = masks + [(g, s ^ 1) for g, s in masks]
-        mats = assemble(inverse, inner_link, cross, tuple(masks), shares, ranks, samples)
-
-        return place(over_rows(solve(target, mats, first, second, samples)))
+        over_xy = lax.ppermute(
+            here,
+            ("groups", "samples"),
+            [(i, i ^ (samples + 2)) for i in range(groups * samples)],
+        )
+        kept, sent = fold(kept, got, ())
+        came = exchange(sent, "rows", 3, ranks)
+        half = gathered([here, over_x], (kept,))
+        half_near = exchange(half, "samples", 1, samples)
+        rest = gathered([over_y, over_xy], (half, came))
+        rest_near = exchange(rest, "samples", 1, samples)
+        shares = (half, rest, half_near, rest_near)
+        masks = (((0, 0), (0, 2)), ((1, 0), (1, 2)), ((0, 1), (0, 3)), ((1, 1), (1, 3)))
+        mats = assemble(inverse, inner_link, cross, masks, shares, ranks, samples)
+
+        return place(over_rows(solve(target, mats, (kept, came), ranks, samples)))
 
     return local
 
@@ -395,7 +455,7 @@
         fits = (
             groups == 2
             and samples == 4
-            and ranks in (2, 4)
+            and ranks == 4
             and block % (ranks * groups * samples * 8) == 0
             and columns % (samples * ranks * 8) == 0
         )

time: 61 us -> 47.7 us (0.78)
  starting transfers between devices: 26.3 us -> 20.3 us
  waiting for transfers between devices: 24.2 us -> 18.5 us
  local copies, waits for them, and re-layouts: 3.52 us -> 0.01 us
  Pallas kernels: 6.52 us -> 8.59 us
    ppermute x22 -> x14, waiting for transfers between devices: 24.2 us -> 14 us  [exchange(): return lax.ppermute(array, axis, [(i, i ^ mask) for i in range(size)])]
    ppermute x22 -> x14, starting transfers between devices: 26.3 us -> 18.8 us  [exchange(): return lax.ppermute(array, axis, [(i, i ^ mask) for i in range(size)])]
    ppermute x0 -> x1, waiting for transfers between devices: none -> 4.48 us  [local(): lax.ppermute(here, ('groups', 'samples'), [(i, i ^ samples + 2) for i in...]
    unnamed x22 -> x8, local copies, waits for them, and re-layouts: 3.52 us -> 0.01 us
    pallas_call x4 -> x9, Pallas kernels: 1.8 us -> 3.76 us  [the longest x1 1.8 us: targets(): pl.pallas_call(with_after(target_kernel, 2, after), out_shape=pltpu.VMEM(...]
    ppermute x0 -> x1, starting transfers between devices: none -> 1.49 us  [local(): lax.ppermute(here, ('groups', 'samples'), [(i, i ^ samples + 2) for i in...]
  transfers between devices with their start and end apart: 22 -> 15, of which waited for: 8 -> 8; matrix products, arithmetic and copies ran while one was open for 0% -> 0% of each run, Pallas kernels for 7% -> 10%
where the time goes in v3:
time: 47.7 us; the launch traced here: 47.5 us
  starting transfers between devices  20.3 us (43%)
  waiting for transfers between devices  18.5 us (39%)
  Pallas kernels  8.59 us (18%)
    ppermute x14, starting transfers between devices, exchange(): return lax.ppermute(array, axis, [(i, i ^ mask) for i in range(size)])  18.8 us
    ppermute x14, waiting for transfers between devices, exchange(): return lax.ppermute(array, axis, [(i, i ^ mask) for i in range(size)])  14 us
    ppermute x1, waiting for transfers between devices, local(): lax.ppermute(here, ('groups', 'samples'), [(i, i ^ samples + 2) for i in...  4.48 us
    pallas_call x1, Pallas kernels, front_rows(): pl.pallas_call(front_kernel, out_shape=(out, out), in_specs=[SMEM, VMEM],...  1.95 us
    pallas_call x1, Pallas kernels, targets(): pl.pallas_call(with_after(target_kernel, 2, after), out_shape=pltpu.VMEM(...  1.8 us
    ppermute x1, starting transfers between devices, local(): lax.ppermute(here, ('groups', 'samples'), [(i, i ^ samples + 2) for i in...  1.49 us
    pallas_call x1, Pallas kernels, solve(): pl.pallas_call(functools.partial(solve_kernel, ranks, samples), out_shape...  1.35 us
    pallas_call x1, Pallas kernels, own_share(): pl.pallas_call(functools.partial(share_kernel, samples), out_shape=(pltpu...  1.14 us
  transfers between devices with their start and end apart: 15, of which 8 were waited for; matrix products, arithmetic and copies ran while one was open for 0% of the time, Pallas kernels for 10%

profile of v3, /device:TPU:0, one launch (start us, length us, event | category | flops | bytes accessed | tf_op | source)
XLA Modules:
  0.0 47.5 jit_solution(1815478503237717980)
XLA Ops:
  0.0 1.1 %own_share.1 = (f32[10,8,256]{2,1,0:T(8,128)S(1)}, f32[512,128]{1,0:T(8,128)S(1)}, f32[2,128,256]{2,1,0:T(8,128)S(1)}) custom-call(f32[4,64,256]{2,1,0:T(8,128)} %bitcast.6, f32[2,64,256]{2,1,0:T(8,128)} %inner_ref.1, f32[4,64,256]{2,1,0:T(8,128)} %bitcast.8, f32[512,128]{1,0:T(8,128)} %refs_3_.1, f32[2,128,256]{2,1,0:T(8,128)} %bitcast.12), custom_call_target="tpu_custom_call" | custom-call | flops 1 | bytes 1 | tf_op jit(solution)/shard_map/own_share/pallas_call | solution.py:121
  1.2 3.0 %collective-permute-start.3 = (f32[2,128,256]{2,1,0:T(8,128)S(1)}, f32[2,128,256]{2,1,0:T(8,128)S(1)}, u32[]{:S(2)}, u32[]{:S(2)}) collective-permute-start(f32[2,128,256]{2,1,0:T(8,128)S(1)} %get-tuple-element.24.refs_2_), channel_id=1, source_target_pairs={{0,2},{1,3},{2,0},{3,1},{4,6},{5,7},{6,4},{7,5},{8,10},{9,11},{10,... | collective-permute-start | bytes 786440 | tf_op jit(solution)/shard_map/ppermute | solution.py:52
  4.2 3.6 %collective-permute-start = (f32[1,10,8,256]{3,2,1,0:T(8,128)S(1)}, f32[1,10,8,256]{3,2,1,0:T(8,128)S(1)}, u32[]{:S(2)}, u32[]{:S(2)}) collective-permute-start(f32[1,10,8,256]{3,2,1,0:T(8,128)S(1)} %bitcast.10), channel_id=1, source_target_pairs={{0,12},{4,8},{8,4},{12,0},{1,13},{5,9},{9,5},{13,1},{2,14},{6,10},... | collective-permute-start | bytes 245768 | tf_op jit(solution)/shard_map/ppermute | solution.py:52
  7.8 1.9 %front_rows.1 = (bf16[2,128,256]{2,1,0:T(8,128)(2,1)S(1)}, bf16[2,128,256]{2,1,0:T(8,128)(2,1)S(1)}) custom-call(s32[2,256]{1,0:T(2,128)} %map_ref.1, f32[512,128]{1,0:T(8,128)S(1)} %get-tuple-element.21.ancestor_ref), custom_call_target="tpu_custom_call" | custom-call | flops 1 | bytes 1 | tf_op jit(solution)/shard_map/front_rows/pallas_call | solution.py:152
  9.7 0.7 %collective-permute-done.refs_1_.refs_0_ = f32[1,10,8,256]{3,2,1,0:T(8,128)S(1)} collective-permute-done((f32[1,10,8,256]{3,2,1,0:T(8,128)S(1)}, f32[1,10,8,256]{3,2,1,0:T(8,128)S(1)}, u32[]{:S(2)}, u32[]{:S(2)}) %collective-permute-start) | collective-permute-done | bytes 81952 | tf_op jit(solution)/shard_map/ppermute | solution.py:52
  10.5 0.0 collective-permute-done.3.refs_0_
  10.5 0.1 collective-permute-start.4
  10.6 1.9 %collective-permute-start.1 = (f32[2,10,8,256]{3,2,1,0:T(8,128)S(1)}, f32[2,10,8,256]{3,2,1,0:T(8,128)S(1)}, u32[]{:S(2)}, u32[]{:S(2)}) collective-permute-start(f32[2,10,8,256]{3,2,1,0:T(8,128)S(1)} %gathered.5.refs_2_.refs_1_), channel_id=1, source_target_pairs={{0,4},{4,0},{8,12},{12,8},{1,5},{5,1},{9,13},{13,9},{2,6},{6,2},{1... | collective-permute-start | bytes 491528 | tf_op jit(solution)/shard_map/ppermute | solution.py:52
  12.5 1.8 %targets.1.refs_6_.target_ref = f32[2,32,512]{2,1,0:T(8,128)S(1)} custom-call(s32[2]{0:T(128)S(1)} %copy-done.3, f32[2048,128]{1,0:T(8,128)} %refs_1_.3, f32[2,10,8,256]{3,2,1,0:T(8,128)S(1)} %gathered.5.refs_2_.refs_1_), custom_call_target="tpu_custom_call" | custom-call | flops 1 | bytes 1 | tf_op jit(solution)/shard_map/targets/pallas_call | solution.py:260
  14.3 0.0 collective-permute-done.4.refs_5_
  14.3 0.7 %terms.1 = (f32[2,4,2,32,128]{4,3,2,1,0:T(8,128)S(1)}, f32[2,4,2,32,128]{4,3,2,1,0:T(8,128)S(1)}) custom-call(bf16[2,128,256]{2,1,0:T(8,128)(2,1)S(1)} %get-tuple-element.22.refs_2_.refs_0_, bf16[2,128,256]{2,1,0:T(8,128)(2,1)S(1)} %get-tuple-element.23.refs_3_.refs_1_, f32[2,128,256]{2,1,0:T(8,128)S(1)} %get-tuple-element.24.refs_2_, ...), custom_call_target="tpu_custom_call" | custom-call | flops 1 | bytes 1 | tf_op jit(solution)/shard_map/terms/pallas_call | solution.py:205
  15.0 0.3 collective-permute-start.6
  15.3 2.0 %collective-permute-done.1.refs_1_ = f32[2,10,8,256]{3,2,1,0:T(8,128)S(1)} collective-permute-done((f32[2,10,8,256]{3,2,1,0:T(8,128)S(1)}, f32[2,10,8,256]{3,2,1,0:T(8,128)S(1)}, u32[]{:S(2)}, u32[]{:S(2)}) %collective-permute-start.1) | collective-permute-done | bytes 163872 | tf_op jit(solution)/shard_map/ppermute | solution.py:52
  17.3 1.7 %collective-permute-start.5 = (f32[3,10,8,256]{3,2,1,0:T(8,128)S(1)}, f32[3,10,8,256]{3,2,1,0:T(8,128)S(1)}, u32[]{:S(2)}, u32[]{:S(2)}) collective-permute-start(f32[3,10,8,256]{3,2,1,0:T(8,128)S(1)} %gathered.7.refs_0_), channel_id=1, source_target_pairs={{0,2},{1,3},{2,0},{3,1},{4,6},{5,7},{6,4},{7,5},{8,10},{9,11},{10,... | collective-permute-start | bytes 737288 | tf_op jit(solution)/shard_map/ppermute | solution.py:52
  19.0 1.5 %collective-permute-start.8 = (f32[3,10,8,256]{3,2,1,0:T(8,128)S(1)}, f32[3,10,8,256]{3,2,1,0:T(8,128)S(1)}, u32[]{:S(2)}, u32[]{:S(2)}) collective-permute-start(f32[3,10,8,256]{3,2,1,0:T(8,128)S(1)} %gathered.7.refs_0_), channel_id=1, source_target_pairs={{0,18},{1,19},{2,16},{3,17},{16,2},{17,3},{18,0},{19,1},{4,22},{5,... | collective-permute-start | bytes 737288 | tf_op jit(solution)/shard_map/ppermute | solution.py:420
  20.5 0.3 collective-permute-start.7
  20.8 2.6 %collective-permute-done.6.refs_1_ = f32[2,4,2,32,128]{4,3,2,1,0:T(8,128)S(1)} collective-permute-done((f32[2,4,2,32,128]{4,3,2,1,0:T(8,128)S(1)}, f32[2,4,2,32,128]{4,3,2,1,0:T(8,128)S(1)}, u32[]{:S(2)}, u32[]{:S(2)}) %collective-permute-start.6) | collective-permute-done | bytes 262176 | tf_op jit(solution)/shard_map/ppermute | solution.py:52
  23.4 3.3 %collective-permute-start.9 = (f32[4,2,32,128]{3,2,1,0:T(8,128)S(1)}, f32[4,2,32,128]{3,2,1,0:T(8,128)S(1)}, u32[]{:S(2)}, u32[]{:S(2)}) collective-permute-start(f32[4,2,32,128]{3,2,1,0:T(8,128)S(1)} %get-tuple-element.28), channel_id=1, source_target_pairs={{0,12},{4,8},{8,4},{12,0},{1,13},{5,9},{9,5},{13,1},{2,14},{6,10},... | collective-permute-start | bytes 393224 | tf_op jit(solution)/shard_map/ppermute | solution.py:52
  26.8 0.1 collective-permute-start.10
  26.9 4.5 %collective-permute-done.8.refs_1_ = f32[3,10,8,256]{3,2,1,0:T(8,128)S(1)} collective-permute-done((f32[3,10,8,256]{3,2,1,0:T(8,128)S(1)}, f32[3,10,8,256]{3,2,1,0:T(8,128)S(1)}, u32[]{:S(2)}, u32[]{:S(2)}) %collective-permute-start.8) | collective-permute-done | bytes 245792 | tf_op jit(solution)/shard_map/ppermute | solution.py:420
  31.4 1.4 %collective-permute-done.7.refs_0_ = f32[3,10,8,256]{3,2,1,0:T(8,128)S(1)} collective-permute-done((f32[3,10,8,256]{3,2,1,0:T(8,128)S(1)}, f32[3,10,8,256]{3,2,1,0:T(8,128)S(1)}, u32[]{:S(2)}, u32[]{:S(2)}) %collective-permute-start.7) | collective-permute-done | bytes 245792 | tf_op jit(solution)/shard_map/ppermute | solution.py:52
  32.8 0.1 collective-permute-start.11
  32.8 0.0 collective-permute-done.10.rest_2_
  32.9 1.8 %collective-permute-done.11.rest_3_ = f32[6,10,8,256]{3,2,1,0:T(8,128)S(1)} collective-permute-done((f32[6,10,8,256]{3,2,1,0:T(8,128)S(1)}, f32[6,10,8,256]{3,2,1,0:T(8,128)S(1)}, u32[]{:S(2)}, u32[]{:S(2)}) %collective-permute-start.11) | collective-permute-done | bytes 491552 | tf_op jit(solution)/shard_map/ppermute | solution.py:52
  34.7 0.8 %assemble.1 = (bf16[10,256,256]{2,1,0:T(8,128)(2,1)S(1)}, bf16[10,256,256]{2,1,0:T(8,128)(2,1)S(1)}) custom-call(f32[4,64,256]{2,1,0:T(8,128)S(1)} %bitcast.7, f32[2,64,256]{2,1,0:T(8,128)S(1)} %copy-done.2, f32[4,64,256]{2,1,0:T(8,128)S(1)} %bitcast.9, f32[6,10,8,256]{3,2,1,0:T(8,128)S(1)} %gathered.8.refs_2_.rest_0_, ...), custom_call_target="tpu_custom_call" | custom-call | flops 1 | bytes 1 | tf_op jit(solution)/shard_map/assemble/pallas_call | solution.py:298
  35.5 1.4 %solve.1 = (f32[32,256]{1,0:T(8,128)S(1)}, f32[32,256]{1,0:T(8,128)S(1)}, f32[32,256]{1,0:T(8,128)S(1)}, f32[32,256]{1,0:T(8,128)S(1)}) custom-call(f32[2,32,512]{2,1,0:T(8,128)S(1)} %targets.1.refs_6_.target_ref, bf16[10,256,256]{2,1,0:T(8,128)(2,1)S(1)} %get-tuple-element.29.high_ref, bf16[10,256,256]{2,1,0:T(8,128)(2,1)S(1)} %get-tuple-element.30.low_ref, ...), custom_call_target="tpu_custom_call" | custom-call | flops 1 | bytes 1 | tf_op jit(solution)/shard_map/solve/pallas_call | solution.py:348
  36.8 1.6 %collective-permute-start.12 = (f32[32,256]{1,0:T(8,128)S(1)}, f32[32,256]{1,0:T(8,128)S(1)}, u32[]{:S(2)}, u32[]{:S(2)}) collective-permute-start(f32[32,256]{1,0:T(8,128)S(1)} %get-tuple-element.32), channel_id=1, source_target_pairs={{0,4},{4,0},{8,12},{12,8},{1,5},{5,1},{9,13},{13,9},{2,6},{6,2},{1... | collective-permute-start | bytes 98312 | tf_op jit(solution)/shard_map/ppermute | solution.py:52
  38.5 2.6 %collective-permute-start.13 = (f32[32,256]{1,0:T(8,128)S(1)}, f32[32,256]{1,0:T(8,128)S(1)}, u32[]{:S(2)}, u32[]{:S(2)}) collective-permute-start(f32[32,256]{1,0:T(8,128)S(1)} %get-tuple-element.33), channel_id=1, source_target_pairs={{0,8},{4,12},{8,0},{12,4},{1,9},{5,13},{9,1},{13,5},{2,10},{6,14},... | collective-permute-start | bytes 98312 | tf_op jit(solution)/shard_map/ppermute | solution.py:52
  41.1 0.2 collective-permute-start.14
  41.3 2.6 %collective-permute-done.13.refs_2_ = f32[32,256]{1,0:T(8,128)S(1)} collective-permute-done((f32[32,256]{1,0:T(8,128)S(1)}, f32[32,256]{1,0:T(8,128)S(1)}, u32[]{:S(2)}, u32[]{:S(2)}) %collective-permute-start.13) | collective-permute-done | bytes 32800 | tf_op jit(solution)/shard_map/ppermute | solution.py:52
  43.9 2.9 %collective-permute-done.14.refs_3_ = f32[32,256]{1,0:T(8,128)S(1)} collective-permute-done((f32[32,256]{1,0:T(8,128)S(1)}, f32[32,256]{1,0:T(8,128)S(1)}, u32[]{:S(2)}, u32[]{:S(2)}) %collective-permute-start.14) | collective-permute-done | bytes 32800 | tf_op jit(solution)/shard_map/ppermute | solution.py:52
  46.8 0.8 %place.1 = f32[2,2,64,128]{3,2,1,0:T(8,128)} custom-call(f32[32,256]{1,0:T(8,128)S(1)} %get-tuple-element.31.refs_0_, f32[32,256]{1,0:T(8,128)S(1)} %collective-permute-done.12.refs_1_, f32[32,256]{1,0:T(8,128)S(1)} %collective-permute-done.13.refs_2_, f32[32,256]{1,0:T(8,128)S(1)} %collective-permute-done.14.refs_3_), custom_call_target="tpu_custom_call" | custom-call | flops 1 | bytes 1 | tf_op jit(solution)/shard_map/place/pallas_call | solution.py:379
  (19 shorter events, 0.2 us)
Async XLA Ops:
  0.0 12.5 %copy-start.3 = (s32[2]{0:T(128)S(1)}, s32[2]{0:T(128)}, u32[]{:S(2)}) copy-start(s32[2]{0:T(128)} %refs_0_.1) | copy-start | bytes 28
  1.2 9.3 %collective-permute-start.3 = (f32[2,128,256]{2,1,0:T(8,128)S(1)}, f32[2,128,256]{2,1,0:T(8,128)S(1)}, u32[]{:S(2)}, u32[]{:S(2)}) collective-permute-start(f32[2,128,256]{2,1,0:T(8,128)S(1)} %get-tuple-element.24.refs_2_), channel_id=1, source_target_pairs={{0,2},{1,3},{2,0},{3,1},{4,6},{5,7},{6,4},{7,5},{8,10},{9,11},{10,... | collective-permute-start | bytes 786440 | tf_op jit(solution)/shard_map/ppermute | solution.py:52
  4.2 6.3 %collective-permute-start = (f32[1,10,8,256]{3,2,1,0:T(8,128)S(1)}, f32[1,10,8,256]{3,2,1,0:T(8,128)S(1)}, u32[]{:S(2)}, u32[]{:S(2)}) collective-permute-start(f32[1,10,8,256]{3,2,1,0:T(8,128)S(1)} %bitcast.10), channel_id=1, source_target_pairs={{0,12},{4,8},{8,4},{12,0},{1,13},{5,9},{9,5},{13,1},{2,14},{6,10},... | collective-permute-start | bytes 245768 | tf_op jit(solution)/shard_map/ppermute | solution.py:52
  7.8 6.5 %collective-permute-start.2 = (f32[2,128,256]{2,1,0:T(8,128)S(1)}, f32[2,128,256]{2,1,0:T(8,128)S(1)}, u32[]{:S(2)}, u32[]{:S(2)}) collective-permute-start(f32[2,128,256]{2,1,0:T(8,128)S(1)} %get-tuple-element.24.refs_2_), channel_id=1, source_target_pairs={{0,1},{1,0},{2,3},{3,2},{4,5},{5,4},{6,7},{7,6},{8,9},{9,8},{10,11... | collective-permute-start | bytes 786440 | tf_op jit(solution)/shard_map/ppermute | solution.py:52
  10.5 3.8 %collective-permute-start.4 = (f32[2,128,256]{2,1,0:T(8,128)S(1)}, f32[2,128,256]{2,1,0:T(8,128)S(1)}, u32[]{:S(2)}, u32[]{:S(2)}) collective-permute-start(f32[2,128,256]{2,1,0:T(8,128)S(1)} %gathered.6.refs_4_), channel_id=1, source_target_pairs={{0,1},{1,0},{2,3},{3,2},{4,5},{5,4},{6,7},{7,6},{8,9},{9,8},{10,11... | collective-permute-start | bytes 786440 | tf_op jit(solution)/shard_map/ppermute | solution.py:52
  10.6 6.7 %collective-permute-start.1 = (f32[2,10,8,256]{3,2,1,0:T(8,128)S(1)}, f32[2,10,8,256]{3,2,1,0:T(8,128)S(1)}, u32[]{:S(2)}, u32[]{:S(2)}) collective-permute-start(f32[2,10,8,256]{3,2,1,0:T(8,128)S(1)} %gathered.5.refs_2_.refs_1_), channel_id=1, source_target_pairs={{0,4},{4,0},{8,12},{12,8},{1,5},{5,1},{9,13},{13,9},{2,6},{6,2},{1... | collective-permute-start | bytes 491528 | tf_op jit(solution)/shard_map/ppermute | solution.py:52
  15.0 8.4 %collective-permute-start.6 = (f32[2,4,2,32,128]{4,3,2,1,0:T(8,128)S(1)}, f32[2,4,2,32,128]{4,3,2,1,0:T(8,128)S(1)}, u32[]{:S(2)}, u32[]{:S(2)}) collective-permute-start(f32[2,4,2,32,128]{4,3,2,1,0:T(8,128)S(1)} %get-tuple-element.25.refs_2_), channel_id=1, source_target_pairs={{0,4},{4,0},{8,12},{12,8},{1,5},{5,1},{9,13},{13,9},{2,6},{6,2},{1... | collective-permute-start | bytes 786440 | tf_op jit(solution)/shard_map/ppermute | solution.py:52
  17.3 9.5 %collective-permute-start.5 = (f32[3,10,8,256]{3,2,1,0:T(8,128)S(1)}, f32[3,10,8,256]{3,2,1,0:T(8,128)S(1)}, u32[]{:S(2)}, u32[]{:S(2)}) collective-permute-start(f32[3,10,8,256]{3,2,1,0:T(8,128)S(1)} %gathered.7.refs_0_), channel_id=1, source_target_pairs={{0,2},{1,3},{2,0},{3,1},{4,6},{5,7},{6,4},{7,5},{8,10},{9,11},{10,... | collective-permute-start | bytes 737288 | tf_op jit(solution)/shard_map/ppermute | solution.py:52
  19.0 12.4 %collective-permute-start.8 = (f32[3,10,8,256]{3,2,1,0:T(8,128)S(1)}, f32[3,10,8,256]{3,2,1,0:T(8,128)S(1)}, u32[]{:S(2)}, u32[]{:S(2)}) collective-permute-start(f32[3,10,8,256]{3,2,1,0:T(8,128)S(1)} %gathered.7.refs_0_), channel_id=1, source_target_pairs={{0,18},{1,19},{2,16},{3,17},{16,2},{17,3},{18,0},{19,1},{4,22},{5,... | collective-permute-start | bytes 737288 | tf_op jit(solution)/shard_map/ppermute | solution.py:420
  20.5 12.2 %collective-permute-start.7 = (f32[3,10,8,256]{3,2,1,0:T(8,128)S(1)}, f32[3,10,8,256]{3,2,1,0:T(8,128)S(1)}, u32[]{:S(2)}, u32[]{:S(2)}) collective-permute-start(f32[3,10,8,256]{3,2,1,0:T(8,128)S(1)} %gathered.7.refs_0_), channel_id=1, source_target_pairs={{0,16},{16,0},{1,17},{17,1},{2,18},{18,2},{3,19},{19,3},{4,20},{20... | collective-permute-start | bytes 737288 | tf_op jit(solution)/shard_map/ppermute | solution.py:52
  23.4 9.3 %collective-permute-start.9 = (f32[4,2,32,128]{3,2,1,0:T(8,128)S(1)}, f32[4,2,32,128]{3,2,1,0:T(8,128)S(1)}, u32[]{:S(2)}, u32[]{:S(2)}) collective-permute-start(f32[4,2,32,128]{3,2,1,0:T(8,128)S(1)} %get-tuple-element.28), channel_id=1, source_target_pairs={{0,12},{4,8},{8,4},{12,0},{1,13},{5,9},{9,5},{13,1},{2,14},{6,10},... | collective-permute-start | bytes 393224 | tf_op jit(solution)/shard_map/ppermute | solution.py:52
  26.7 7.9 %copy-start = (f32[2,2,64,256]{3,2,1,0:T(8,128)S(1)}, f32[2,2,64,256]{3,2,1,0:T(8,128)}, u32[]{:S(2)}) copy-start(f32[2,2,64,256]{3,2,1,0:T(8,128)} %param.13) | copy-start | bytes 786436
  26.8 7.9 %copy-start.1 = (f32[2,2,64,256]{3,2,1,0:T(8,128)S(1)}, f32[2,2,64,256]{3,2,1,0:T(8,128)}, u32[]{:S(2)}) copy-start(f32[2,2,64,256]{3,2,1,0:T(8,128)} %param.15) | copy-start | bytes 786436
  26.8 7.9 %copy-start.2 = (f32[2,64,256]{2,1,0:T(8,128)S(1)}, f32[2,64,256]{2,1,0:T(8,128)}, u32[]{:S(2)}) copy-start(f32[2,64,256]{2,1,0:T(8,128)} %inner_ref.1) | copy-start | bytes 393220
  26.8 6.0 %collective-permute-start.10 = (f32[6,10,8,256]{3,2,1,0:T(8,128)S(1)}, f32[6,10,8,256]{3,2,1,0:T(8,128)S(1)}, u32[]{:S(2)}, u32[]{:S(2)}) collective-permute-start(f32[6,10,8,256]{3,2,1,0:T(8,128)S(1)} %gathered.8.refs_2_.rest_0_), channel_id=1, source_target_pairs={{0,1},{1,0},{2,3},{3,2},{4,5},{5,4},{6,7},{7,6},{8,9},{9,8},{10,11... | collective-permute-start | bytes 1474568 | tf_op jit(solution)/shard_map/ppermute | solution.py:52
  32.8 1.9 %collective-permute-start.11 = (f32[6,10,8,256]{3,2,1,0:T(8,128)S(1)}, f32[6,10,8,256]{3,2,1,0:T(8,128)S(1)}, u32[]{:S(2)}, u32[]{:S(2)}) collective-permute-start(f32[6,10,8,256]{3,2,1,0:T(8,128)S(1)} %gathered.9.rest_1_), channel_id=1, source_target_pairs={{0,1},{1,0},{2,3},{3,2},{4,5},{5,4},{6,7},{7,6},{8,9},{9,8},{10,11... | collective-permute-start | bytes 1474568 | tf_op jit(solution)/shard_map/ppermute | solution.py:52
  36.8 4.5 %collective-permute-start.12 = (f32[32,256]{1,0:T(8,128)S(1)}, f32[32,256]{1,0:T(8,128)S(1)}, u32[]{:S(2)}, u32[]{:S(2)}) collective-permute-start(f32[32,256]{1,0:T(8,128)S(1)} %get-tuple-element.32), channel_id=1, source_target_pairs={{0,4},{4,0},{8,12},{12,8},{1,5},{5,1},{9,13},{13,9},{2,6},{6,2},{1... | collective-permute-start | bytes 98312 | tf_op jit(solution)/shard_map/ppermute | solution.py:52
  38.5 5.4 %collective-permute-start.13 = (f32[32,256]{1,0:T(8,128)S(1)}, f32[32,256]{1,0:T(8,128)S(1)}, u32[]{:S(2)}, u32[]{:S(2)}) collective-permute-start(f32[32,256]{1,0:T(8,128)S(1)} %get-tuple-element.33), channel_id=1, source_target_pairs={{0,8},{4,12},{8,0},{12,4},{1,9},{5,13},{9,1},{13,5},{2,10},{6,14},... | collective-permute-start | bytes 98312 | tf_op jit(solution)/shard_map/ppermute | solution.py:52
  41.1 5.7 %collective-permute-start.14 = (f32[32,256]{1,0:T(8,128)S(1)}, f32[32,256]{1,0:T(8,128)S(1)}, u32[]{:S(2)}, u32[]{:S(2)}) collective-permute-start(f32[32,256]{1,0:T(8,128)S(1)} %get-tuple-element.34), channel_id=1, source_target_pairs={{0,12},{4,8},{8,4},{12,0},{1,13},{5,9},{9,5},{13,1},{2,14},{6,10},... | collective-permute-start | bytes 98312 | tf_op jit(solution)/shard_map/ppermute | solution.py:52

commit v4 on v3

--- a/solution.py
+++ b/solution.py
@@ -126,7 +126,7 @@
         out_specs=(VMEM,) * (1 + len(whole)),
         scratch_shapes=[pltpu.SemaphoreType.DMA((3 + len(whole),))],
         compiler_params=params(),
-        cost_estimate=cost(1, 1),
+        cost_estimate=cost(1265000000, 1),
         name="own_share",
     )(*(far_memory(a) for a in (inverse, inner, cross, *whole)))
 
@@ -155,7 +155,7 @@
         in_specs=[SMEM, VMEM],
         out_specs=(VMEM, VMEM),
         scratch_shapes=[pltpu.VMEM((2, k_rows, cols_here), F32)],
-        cost_estimate=cost(1, 1),
+        cost_estimate=cost(2300000000, 1),
         compiler_params=params(),
         name="front_rows",
     )(far_memory(row_map), near_core(ancestor))
@@ -177,7 +177,7 @@
         in_specs=[VMEM] * (len(pieces) + len(after)),
         out_specs=VMEM,
         compiler_params=params(),
-        cost_estimate=cost(1, 1),
+        cost_estimate=cost(115000000, 1),
         name="gathered",
     )(*(near_core(a) for a in (*pieces, *after)))
 
@@ -209,27 +209,31 @@
         out_specs=(VMEM,) * 2,
         scratch_shapes=[pltpu.VMEM((ranks, quarter, len(columns) * width), F32)],
         compiler_params=params(),
-        cost_estimate=cost(1, 1),
+        cost_estimate=cost(805000000, 1),
         name="terms",
     )(*(near_core(a) for a in (*front, *columns, *after)))
 
 
-def fold_kernel(keep_ref, got_ref, own_ref, send_ref):
-    own_ref[...] = keep_ref[0] + got_ref[0]
-    send_ref[...] = keep_ref[1] + got_ref[1]
-
-
-def fold(keep, got, after=()):
-    out = pltpu.VMEM(keep.shape[1:], F32)
-    return pl.pallas_call(
-        with_after(fold_kernel, 2, after),
+def fold_kernel(keep_1, got_1, keep_2, got_2, own_ref, send_ref):
+    groups = keep_1.shape[1]
+    for i, (keep_ref, got_ref) in enumerate(((keep_1, got_1), (keep_2, got_2))):
+        at = slice(i * groups, (i + 1) * groups)
+        own_ref[at] = keep_ref[0] + got_ref[0]
+        send_ref[at] = keep_ref[1] + got_ref[1]
+
+
+def fold(parts, after=()):
+    shape = parts[0].shape
+    out = pltpu.VMEM((2 * shape[1],) + shape[2:], F32)
+    return pl.pallas_call(
+        with_after(fold_kernel, 4, after),
         out_shape=(out, out),
-        in_specs=[VMEM] * (2 + len(after)),
+        in_specs=[VMEM] * (4 + len(after)),
         out_specs=(VMEM,) * 2,
         compiler_params=params(),
-        cost_estimate=cost(1, 1),
+        cost_estimate=cost(115000000, 1),
         name="fold",
-    )(*(near_core(a) for a in (keep, got, *after)))
+    )(*(near_core(a) for a in (*parts, *after)))
 
 
 def target_kernel(off_ref, noise_ref, out_ref, window, hold, sems):
@@ -267,7 +271,7 @@
             pltpu.VMEM((ranks, quarter, rows), F32),
             pltpu.SemaphoreType.DMA((2,)),
         ],
-        cost_estimate=cost(1, 1),
+        cost_estimate=cost(2070000000, 1),
         compiler_params=params(),
         name="targets",
     )(offsets, far_memory(noise), *(near_core(a) for a in after))
@@ -301,7 +305,7 @@
         in_specs=[VMEM] * (3 + len(shares)),
         out_specs=(VMEM, VMEM),
         scratch_shapes=[pltpu.VMEM((10, block, block), F32)],
-        cost_estimate=cost(1, 1),
+        cost_estimate=cost(920000000, 1),
         compiler_params=params(),
         name="assemble",
     )(*(near_core(a) for a in (inverse, inner, cross, *shares)))
@@ -354,7 +358,7 @@
             pltpu.VMEM((samples, 2, quarter, 2 * block // samples), F32),
             pltpu.VMEM((ranks, quarter, 4 * block // ranks), F32),
         ],
-        cost_estimate=cost(1, 1),
+        cost_estimate=cost(1610000000, 1),
         compiler_params=params(),
         name="solve",
     )(*(near_core(a) for a in (target, *mats, *parts)))
@@ -383,7 +387,7 @@
         out_specs=VMEM,
         scratch_shapes=[pltpu.VMEM((ranks, quarter, width), F32)],
         compiler_params=params(),
-        cost_estimate=cost(1, 1),
+        cost_estimate=cost(920000000, 1),
         name="place",
     )(*(near_core(a) for a in pieces))
 
@@ -403,18 +407,20 @@
             inverse, inner_link, cross, (ancestor, own), groups, samples
         )
         share = share[None]
+        far = exchange(own, "samples", 2, samples)
         across = exchange(share, "rows", 3, ranks)
-        far = exchange(moved, "samples", 2, samples)
         near = exchange(moved, "samples", 1, samples)
         front = front_rows(row_map, fetched)
         pair = gathered([share, across], front)
         beside = exchange(pair, "rows", 1, ranks)
+        kept_1, sent_1 = terms(front, (moved, near), ranks, ())
+        got_1 = exchange(sent_1, "rows", 1, ranks)
         target = targets(offsets, noise, 2 * block, ranks, (pair,))
         far = gathered([far], (pair,))
         far_near = exchange(far, "samples", 1, samples)
-        kept, sent = terms(front, (moved, near, far, far_near), ranks, (target,))
-        got = exchange(sent, "rows", 1, ranks)
-        here = gathered([across, beside], (sent,))
+        here = gathered([across, beside], (sent_1,))
+        kept_2, sent_2 = terms(front, (far, far_near), ranks, (target, here))
+        got_2 = exchange(sent_2, "rows", 1, ranks)
         over_x = exchange(here, "samples", 2, samples)
         over_y = exchange(here, "groups", 1, groups)
         over_xy = lax.ppermute(
@@ -422,14 +428,12 @@
             ("groups", "samples"),
             [(i, i ^ (samples + 2)) for i in range(groups * samples)],
         )
-        kept, sent = fold(kept, got, ())
+        kept, sent = fold((kept_1, got_1, kept_2, got_2), ())
         came = exchange(sent, "rows", 3, ranks)
-        half = gathered([here, over_x], (kept,))
+        half = gathered([here, over_x, over_y, over_xy], (came,))
         half_near = exchange(half, "samples", 1, samples)
-        rest = gathered([over_y, over_xy], (half, came))
-        rest_near = exchange(rest, "samples", 1, samples)
-        shares = (half, rest, half_near, rest_near)
-        masks = (((0, 0), (0, 2)), ((1, 0), (1, 2)), ((0, 1), (0, 3)), ((1, 1), (1, 3)))
+        shares = (half, half_near)
+        masks = (((0, 0), (0, 2), (1, 0), (1, 2)), ((0, 1), (0, 3), (1, 1), (1, 3)))
         mats = assemble(inverse, inner_link, cross, masks, shares, ranks, samples)
 
         return place(over_rows(solve(target, mats, (kept, came), ranks, samples)))

time: 47.7 us -> 45.6 us (0.956)
  waiting for transfers between devices: 18.5 us -> 15.9 us
    ppermute x1, waiting for transfers between devices: 4.48 us -> 1.6 us  [local(): lax.ppermute(here, ('groups', 'samples'), [(i, i ^ samples + 2) for i in...]
  transfers between devices with their start and end apart: 15 -> 15, of which waited for: 8 -> 9; matrix products, arithmetic and copies ran while one was open for 0% -> 0% of each run, Pallas kernels for 10% -> 13%
where the time goes in v4:
time: 45.6 us; the launch traced here: 45.4 us
  starting transfers between devices  20.5 us (45%)
  waiting for transfers between devices  15.9 us (35%)
  Pallas kernels  8.88 us (19%)
    ppermute x14, starting transfers between devices, exchange(): return lax.ppermute(array, axis, [(i, i ^ mask) for i in range(size)])  19 us
    ppermute x14, waiting for transfers between devices, exchange(): return lax.ppermute(array, axis, [(i, i ^ mask) for i in range(size)])  14.3 us
    pallas_call x1, Pallas kernels, front_rows(): pl.pallas_call(front_kernel, out_shape=(out, out), in_specs=[SMEM, VMEM],...  2.08 us
    pallas_call x1, Pallas kernels, targets(): pl.pallas_call(with_after(target_kernel, 2, after), out_shape=pltpu.VMEM(...  1.8 us
    ppermute x1, waiting for transfers between devices, local(): lax.ppermute(here, ('groups', 'samples'), [(i, i ^ samples + 2) for i in...  1.6 us
    ppermute x1, starting transfers between devices, local(): lax.ppermute(here, ('groups', 'samples'), [(i, i ^ samples + 2) for i in...  1.49 us
    pallas_call x1, Pallas kernels, solve(): pl.pallas_call(functools.partial(solve_kernel, ranks, samples), out_shape...  1.35 us
    pallas_call x1, Pallas kernels, own_share(): pl.pallas_call(functools.partial(share_kernel, samples), out_shape=(pltpu...  1.13 us
  transfers between devices with their start and end apart: 15, of which 9 were waited for; matrix products, arithmetic and copies ran while one was open for 0% of the time, Pallas kernels for 13%

profile of v4, /device:TPU:0, one launch (start us, length us, event | category | flops | bytes accessed | tf_op | source)
XLA Modules:
  0.0 45.4 jit_solution(1517124432599894552)
XLA Ops:
  0.0 2.9 %collective-permute-start.7 = (f32[2,128,256]{2,1,0:T(8,128)}, f32[2,128,256]{2,1,0:T(8,128)S(1)}, u32[]{:S(2)}, u32[]{:S(2)}) collective-permute-start(f32[2,128,256]{2,1,0:T(8,128)} %bitcast.12), channel_id=1, source_target_pairs={{0,2},{1,3},{2,0},{3,1},{4,6},{5,7},{6,4},{7,5},{8,10},{9,11},{10,... | collective-permute-start | bytes 786440 | tf_op jit(solution)/shard_map/ppermute | solution.py:52
  2.9 1.1 %own_share.1 = (f32[10,8,256]{2,1,0:T(8,128)S(1)}, f32[512,128]{1,0:T(8,128)S(1)}, f32[2,128,256]{2,1,0:T(8,128)S(1)}) custom-call(f32[4,64,256]{2,1,0:T(8,128)} %bitcast.8, f32[2,64,256]{2,1,0:T(8,128)} %inner_ref.1, f32[4,64,256]{2,1,0:T(8,128)} %bitcast.10, f32[512,128]{1,0:T(8,128)} %refs_3_.1, f32[2,128,256]{2,1,0:T(8,128)} %bitcast.13), custom_call_target="tpu_custom_call" | custom-call | flops 1264999936 | bytes 1 | tf_op jit(solution)/shard_map/own_share/pallas_call | solution.py:121
  4.1 3.7 %collective-permute-start = (f32[1,10,8,256]{3,2,1,0:T(8,128)S(1)}, f32[1,10,8,256]{3,2,1,0:T(8,128)S(1)}, u32[]{:S(2)}, u32[]{:S(2)}) collective-permute-start(f32[1,10,8,256]{3,2,1,0:T(8,128)S(1)} %bitcast.6), channel_id=1, source_target_pairs={{0,12},{4,8},{8,4},{12,0},{1,13},{5,9},{9,5},{13,1},{2,14},{6,10},... | collective-permute-start | bytes 245768 | tf_op jit(solution)/shard_map/ppermute | solution.py:52
  7.7 2.1 %front_rows.1 = (bf16[2,128,256]{2,1,0:T(8,128)(2,1)S(1)}, bf16[2,128,256]{2,1,0:T(8,128)(2,1)S(1)}) custom-call(s32[2,256]{1,0:T(2,128)} %map_ref.1, f32[512,128]{1,0:T(8,128)S(1)} %get-tuple-element.23.ancestor_ref), custom_call_target="tpu_custom_call" | custom-call | flops 2300000000 | bytes 1 | tf_op jit(solution)/shard_map/front_rows/pallas_call | solution.py:152
  9.8 0.6 %collective-permute-done.refs_1_.refs_0_ = f32[1,10,8,256]{3,2,1,0:T(8,128)S(1)} collective-permute-done((f32[1,10,8,256]{3,2,1,0:T(8,128)S(1)}, f32[1,10,8,256]{3,2,1,0:T(8,128)S(1)}, u32[]{:S(2)}, u32[]{:S(2)}) %collective-permute-start) | collective-permute-done | bytes 81952 | tf_op jit(solution)/shard_map/ppermute | solution.py:52
  10.5 1.0 %collective-permute-start.1 = (f32[2,10,8,256]{3,2,1,0:T(8,128)S(1)}, f32[2,10,8,256]{3,2,1,0:T(8,128)S(1)}, u32[]{:S(2)}, u32[]{:S(2)}) collective-permute-start(f32[2,10,8,256]{3,2,1,0:T(8,128)S(1)} %gathered.4.refs_2_.refs_1_), channel_id=1, source_target_pairs={{0,4},{4,0},{8,12},{12,8},{1,5},{5,1},{9,13},{13,9},{2,6},{6,2},{1... | collective-permute-start | bytes 491528 | tf_op jit(solution)/shard_map/ppermute | solution.py:52
  11.5 0.1 collective-permute-start.8
  11.6 1.8 %targets.1.refs_4_.target_ref = f32[2,32,512]{2,1,0:T(8,128)S(1)} custom-call(s32[2]{0:T(128)S(1)} %copy-done.3, f32[2048,128]{1,0:T(8,128)} %refs_1_.3, f32[2,10,8,256]{3,2,1,0:T(8,128)S(1)} %gathered.4.refs_2_.refs_1_), custom_call_target="tpu_custom_call" | custom-call | flops 2070000000 | bytes 1 | tf_op jit(solution)/shard_map/targets/pallas_call | solution.py:264
  13.4 0.4 terms.2
  13.8 1.2 %collective-permute-start.6 = (f32[2,2,2,32,128]{4,3,2,1,0:T(8,128)S(1)}, f32[2,2,2,32,128]{4,3,2,1,0:T(8,128)S(1)}, u32[]{:S(2)}, u32[]{:S(2)}) collective-permute-start(f32[2,2,2,32,128]{4,3,2,1,0:T(8,128)S(1)} %get-tuple-element.27.refs_2_), channel_id=1, source_target_pairs={{0,4},{4,0},{8,12},{12,8},{1,5},{5,1},{9,13},{13,9},{2,6},{6,2},{1... | collective-permute-start | bytes 393224 | tf_op jit(solution)/shard_map/ppermute | solution.py:52
  15.0 1.6 %collective-permute-done.1.refs_1_ = f32[2,10,8,256]{3,2,1,0:T(8,128)S(1)} collective-permute-done((f32[2,10,8,256]{3,2,1,0:T(8,128)S(1)}, f32[2,10,8,256]{3,2,1,0:T(8,128)S(1)}, u32[]{:S(2)}, u32[]{:S(2)}) %collective-permute-start.1) | collective-permute-done | bytes 163872 | tf_op jit(solution)/shard_map/ppermute | solution.py:52
  16.6 0.4 terms.3
  17.0 0.3 collective-permute-start.9
  17.4 1.5 %collective-permute-start.5 = (f32[3,10,8,256]{3,2,1,0:T(8,128)S(1)}, f32[3,10,8,256]{3,2,1,0:T(8,128)S(1)}, u32[]{:S(2)}, u32[]{:S(2)}) collective-permute-start(f32[3,10,8,256]{3,2,1,0:T(8,128)S(1)} %gathered.5.refs_5_.refs_0_), channel_id=1, source_target_pairs={{0,18},{1,19},{2,16},{3,17},{16,2},{17,3},{18,0},{19,1},{4,22},{5,... | collective-permute-start | bytes 737288 | tf_op jit(solution)/shard_map/ppermute | solution.py:426
  18.8 0.5 %collective-permute-start.4 = (f32[3,10,8,256]{3,2,1,0:T(8,128)S(1)}, f32[3,10,8,256]{3,2,1,0:T(8,128)S(1)}, u32[]{:S(2)}, u32[]{:S(2)}) collective-permute-start(f32[3,10,8,256]{3,2,1,0:T(8,128)S(1)} %gathered.5.refs_5_.refs_0_), channel_id=1, source_target_pairs={{0,16},{16,0},{1,17},{17,1},{2,18},{18,2},{3,19},{19,3},{4,20},{20... | collective-permute-start | bytes 737288 | tf_op jit(solution)/shard_map/ppermute | solution.py:52
  19.4 1.5 %collective-permute-start.3 = (f32[3,10,8,256]{3,2,1,0:T(8,128)S(1)}, f32[3,10,8,256]{3,2,1,0:T(8,128)S(1)}, u32[]{:S(2)}, u32[]{:S(2)}) collective-permute-start(f32[3,10,8,256]{3,2,1,0:T(8,128)S(1)} %gathered.5.refs_5_.refs_0_), channel_id=1, source_target_pairs={{0,2},{1,3},{2,0},{3,1},{4,6},{5,7},{6,4},{7,5},{8,10},{9,11},{10,... | collective-permute-start | bytes 737288 | tf_op jit(solution)/shard_map/ppermute | solution.py:52
  20.8 1.7 %collective-permute-done.9.refs_3_ = f32[2,2,2,32,128]{4,3,2,1,0:T(8,128)S(1)} collective-permute-done((f32[2,2,2,32,128]{4,3,2,1,0:T(8,128)S(1)}, f32[2,2,2,32,128]{4,3,2,1,0:T(8,128)S(1)}, u32[]{:S(2)}, u32[]{:S(2)}) %collective-permute-start.9) | collective-permute-done | bytes 131104 | tf_op jit(solution)/shard_map/ppermute | solution.py:52
  22.6 3.0 %collective-permute-start.10 = (f32[4,2,32,128]{3,2,1,0:T(8,128)S(1)}, f32[4,2,32,128]{3,2,1,0:T(8,128)S(1)}, u32[]{:S(2)}, u32[]{:S(2)}) collective-permute-start(f32[4,2,32,128]{3,2,1,0:T(8,128)S(1)} %get-tuple-element.31), channel_id=1, source_target_pairs={{0,12},{4,8},{8,4},{12,0},{1,13},{5,9},{9,5},{13,1},{2,14},{6,10},... | collective-permute-start | bytes 393224 | tf_op jit(solution)/shard_map/ppermute | solution.py:52
  25.6 1.6 %collective-permute-done.5.refs_3_ = f32[3,10,8,256]{3,2,1,0:T(8,128)S(1)} collective-permute-done((f32[3,10,8,256]{3,2,1,0:T(8,128)S(1)}, f32[3,10,8,256]{3,2,1,0:T(8,128)S(1)}, u32[]{:S(2)}, u32[]{:S(2)}) %collective-permute-start.5) | collective-permute-done | bytes 245792 | tf_op jit(solution)/shard_map/ppermute | solution.py:426
  27.2 3.2 %collective-permute-done.4.refs_2_ = f32[3,10,8,256]{3,2,1,0:T(8,128)S(1)} collective-permute-done((f32[3,10,8,256]{3,2,1,0:T(8,128)S(1)}, f32[3,10,8,256]{3,2,1,0:T(8,128)S(1)}, u32[]{:S(2)}, u32[]{:S(2)}) %collective-permute-start.4) | collective-permute-done | bytes 245792 | tf_op jit(solution)/shard_map/ppermute | solution.py:52
  30.4 0.1 collective-permute-done.3.refs_1_
  30.5 0.1 gathered.7.rest_0_
  30.6 0.1 collective-permute-start.11
  30.7 2.6 %collective-permute-done.11.rest_1_ = f32[12,10,8,256]{3,2,1,0:T(8,128)S(1)} collective-permute-done((f32[12,10,8,256]{3,2,1,0:T(8,128)S(1)}, f32[12,10,8,256]{3,2,1,0:T(8,128)S(1)}, u32[]{:S(2)}, u32[]{:S(2)}) %collective-permute-start.11) | collective-permute-done | bytes 983072 | tf_op jit(solution)/shard_map/ppermute | solution.py:52
  33.2 0.8 %assemble.1 = (bf16[10,256,256]{2,1,0:T(8,128)(2,1)S(1)}, bf16[10,256,256]{2,1,0:T(8,128)(2,1)S(1)}) custom-call(f32[4,64,256]{2,1,0:T(8,128)S(1)} %bitcast.9, f32[2,64,256]{2,1,0:T(8,128)S(1)} %copy-done.2, f32[4,64,256]{2,1,0:T(8,128)S(1)} %bitcast.11, f32[12,10,8,256]{3,2,1,0:T(8,128)S(1)} %gathered.7.rest_0_, ...), custom_call_target="tpu_custom_call" | custom-call | flops 920000000 | bytes 1 | tf_op jit(solution)/shard_map/assemble/pallas_call | solution.py:302
  34.0 1.4 %solve.1 = (f32[32,256]{1,0:T(8,128)S(1)}, f32[32,256]{1,0:T(8,128)S(1)}, f32[32,256]{1,0:T(8,128)S(1)}, f32[32,256]{1,0:T(8,128)S(1)}) custom-call(f32[2,32,512]{2,1,0:T(8,128)S(1)} %targets.1.refs_4_.target_ref, bf16[10,256,256]{2,1,0:T(8,128)(2,1)S(1)} %get-tuple-element.32.high_ref, bf16[10,256,256]{2,1,0:T(8,128)(2,1)S(1)} %get-tuple-element.33.low_ref, ...), custom_call_target="tpu_custom_call" | custom-call | flops 1610000000 | bytes 1 | tf_op jit(solution)/shard_map/solve/pallas_call | solution.py:352
  35.3 2.0 %collective-permute-start.12 = (f32[32,256]{1,0:T(8,128)S(1)}, f32[32,256]{1,0:T(8,128)S(1)}, u32[]{:S(2)}, u32[]{:S(2)}) collective-permute-start(f32[32,256]{1,0:T(8,128)S(1)} %get-tuple-element.36), channel_id=1, source_target_pairs={{0,4},{4,0},{8,12},{12,8},{1,5},{5,1},{9,13},{13,9},{2,6},{6,2},{1... | collective-permute-start | bytes 98312 | tf_op jit(solution)/shard_map/ppermute | solution.py:52
  37.4 1.6 %collective-permute-start.13 = (f32[32,256]{1,0:T(8,128)S(1)}, f32[32,256]{1,0:T(8,128)S(1)}, u32[]{:S(2)}, u32[]{:S(2)}) collective-permute-start(f32[32,256]{1,0:T(8,128)S(1)} %get-tuple-element.37), channel_id=1, source_target_pairs={{0,8},{4,12},{8,0},{12,4},{1,9},{5,13},{9,1},{13,5},{2,10},{6,14},... | collective-permute-start | bytes 98312 | tf_op jit(solution)/shard_map/ppermute | solution.py:52
  38.9 1.2 %collective-permute-start.14 = (f32[32,256]{1,0:T(8,128)S(1)}, f32[32,256]{1,0:T(8,128)S(1)}, u32[]{:S(2)}, u32[]{:S(2)}) collective-permute-start(f32[32,256]{1,0:T(8,128)S(1)} %get-tuple-element.38), channel_id=1, source_target_pairs={{0,12},{4,8},{8,4},{12,0},{1,13},{5,9},{9,5},{13,1},{2,14},{6,10},... | collective-permute-start | bytes 98312 | tf_op jit(solution)/shard_map/ppermute | solution.py:52
  40.1 2.4 %collective-permute-done.13.refs_2_ = f32[32,256]{1,0:T(8,128)S(1)} collective-permute-done((f32[32,256]{1,0:T(8,128)S(1)}, f32[32,256]{1,0:T(8,128)S(1)}, u32[]{:S(2)}, u32[]{:S(2)}) %collective-permute-start.13) | collective-permute-done | bytes 32800 | tf_op jit(solution)/shard_map/ppermute | solution.py:52
  42.6 2.1 %collective-permute-done.14.refs_3_ = f32[32,256]{1,0:T(8,128)S(1)} collective-permute-done((f32[32,256]{1,0:T(8,128)S(1)}, f32[32,256]{1,0:T(8,128)S(1)}, u32[]{:S(2)}, u32[]{:S(2)}) %collective-permute-start.14) | collective-permute-done | bytes 32800 | tf_op jit(solution)/shard_map/ppermute | solution.py:52
  44.7 0.8 %place.1 = f32[2,2,64,128]{3,2,1,0:T(8,128)} custom-call(f32[32,256]{1,0:T(8,128)S(1)} %get-tuple-element.35.refs_0_, f32[32,256]{1,0:T(8,128)S(1)} %collective-permute-done.12.refs_1_, f32[32,256]{1,0:T(8,128)S(1)} %collective-permute-done.13.refs_2_, f32[32,256]{1,0:T(8,128)S(1)} %collective-permute-done.14.refs_3_), custom_call_target="tpu_custom_call" | custom-call | flops 920000000 | bytes 1 | tf_op jit(solution)/shard_map/place/pallas_call | solution.py:383
  (19 shorter events, 0.1 us)
Async XLA Ops:
  0.0 11.5 %collective-permute-start.7 = (f32[2,128,256]{2,1,0:T(8,128)}, f32[2,128,256]{2,1,0:T(8,128)S(1)}, u32[]{:S(2)}, u32[]{:S(2)}) collective-permute-start(f32[2,128,256]{2,1,0:T(8,128)} %bitcast.12), channel_id=1, source_target_pairs={{0,2},{1,3},{2,0},{3,1},{4,6},{5,7},{6,4},{7,5},{8,10},{9,11},{10,... | collective-permute-start | bytes 786440 | tf_op jit(solution)/shard_map/ppermute | solution.py:52
  4.1 6.4 %collective-permute-start = (f32[1,10,8,256]{3,2,1,0:T(8,128)S(1)}, f32[1,10,8,256]{3,2,1,0:T(8,128)S(1)}, u32[]{:S(2)}, u32[]{:S(2)}) collective-permute-start(f32[1,10,8,256]{3,2,1,0:T(8,128)S(1)} %bitcast.6), channel_id=1, source_target_pairs={{0,12},{4,8},{8,4},{12,0},{1,13},{5,9},{9,5},{13,1},{2,14},{6,10},... | collective-permute-start | bytes 245768 | tf_op jit(solution)/shard_map/ppermute | solution.py:52
  7.7 5.6 %collective-permute-start.2 = (f32[2,128,256]{2,1,0:T(8,128)S(1)}, f32[2,128,256]{2,1,0:T(8,128)S(1)}, u32[]{:S(2)}, u32[]{:S(2)}) collective-permute-start(f32[2,128,256]{2,1,0:T(8,128)S(1)} %get-tuple-element.26.refs_2_), channel_id=1, source_target_pairs={{0,1},{1,0},{2,3},{3,2},{4,5},{5,4},{6,7},{7,6},{8,9},{9,8},{10,11... | collective-permute-start | bytes 786440 | tf_op jit(solution)/shard_map/ppermute | solution.py:52
  7.7 3.8 %copy-start.3 = (s32[2]{0:T(128)S(1)}, s32[2]{0:T(128)}, u32[]{:S(2)}) copy-start(s32[2]{0:T(128)} %refs_0_.1) | copy-start | bytes 28
  10.5 6.1 %collective-permute-start.1 = (f32[2,10,8,256]{3,2,1,0:T(8,128)S(1)}, f32[2,10,8,256]{3,2,1,0:T(8,128)S(1)}, u32[]{:S(2)}, u32[]{:S(2)}) collective-permute-start(f32[2,10,8,256]{3,2,1,0:T(8,128)S(1)} %gathered.4.refs_2_.refs_1_), channel_id=1, source_target_pairs={{0,4},{4,0},{8,12},{12,8},{1,5},{5,1},{9,13},{13,9},{2,6},{6,2},{1... | collective-permute-start | bytes 491528 | tf_op jit(solution)/shard_map/ppermute | solution.py:52
  11.5 5.1 %collective-permute-start.8 = (f32[2,128,256]{2,1,0:T(8,128)S(1)}, f32[2,128,256]{2,1,0:T(8,128)S(1)}, u32[]{:S(2)}, u32[]{:S(2)}) collective-permute-start(f32[2,128,256]{2,1,0:T(8,128)S(1)} %gathered.6.refs_2_), channel_id=1, source_target_pairs={{0,1},{1,0},{2,3},{3,2},{4,5},{5,4},{6,7},{7,6},{8,9},{9,8},{10,11... | collective-permute-start | bytes 786440 | tf_op jit(solution)/shard_map/ppermute | solution.py:52
  13.8 7.0 %collective-permute-start.6 = (f32[2,2,2,32,128]{4,3,2,1,0:T(8,128)S(1)}, f32[2,2,2,32,128]{4,3,2,1,0:T(8,128)S(1)}, u32[]{:S(2)}, u32[]{:S(2)}) collective-permute-start(f32[2,2,2,32,128]{4,3,2,1,0:T(8,128)S(1)} %get-tuple-element.27.refs_2_), channel_id=1, source_target_pairs={{0,4},{4,0},{8,12},{12,8},{1,5},{5,1},{9,13},{13,9},{2,6},{6,2},{1... | collective-permute-start | bytes 393224 | tf_op jit(solution)/shard_map/ppermute | solution.py:52
  17.0 5.6 %collective-permute-start.9 = (f32[2,2,2,32,128]{4,3,2,1,0:T(8,128)S(1)}, f32[2,2,2,32,128]{4,3,2,1,0:T(8,128)S(1)}, u32[]{:S(2)}, u32[]{:S(2)}) collective-permute-start(f32[2,2,2,32,128]{4,3,2,1,0:T(8,128)S(1)} %get-tuple-element.30), channel_id=1, source_target_pairs={{0,4},{4,0},{8,12},{12,8},{1,5},{5,1},{9,13},{13,9},{2,6},{6,2},{1... | collective-permute-start | bytes 393224 | tf_op jit(solution)/shard_map/ppermute | solution.py:52
  17.4 9.8 %collective-permute-start.5 = (f32[3,10,8,256]{3,2,1,0:T(8,128)S(1)}, f32[3,10,8,256]{3,2,1,0:T(8,128)S(1)}, u32[]{:S(2)}, u32[]{:S(2)}) collective-permute-start(f32[3,10,8,256]{3,2,1,0:T(8,128)S(1)} %gathered.5.refs_5_.refs_0_), channel_id=1, source_target_pairs={{0,18},{1,19},{2,16},{3,17},{16,2},{17,3},{18,0},{19,1},{4,22},{5,... | collective-permute-start | bytes 737288 | tf_op jit(solution)/shard_map/ppermute | solution.py:426
  18.8 11.6 %collective-permute-start.4 = (f32[3,10,8,256]{3,2,1,0:T(8,128)S(1)}, f32[3,10,8,256]{3,2,1,0:T(8,128)S(1)}, u32[]{:S(2)}, u32[]{:S(2)}) collective-permute-start(f32[3,10,8,256]{3,2,1,0:T(8,128)S(1)} %gathered.5.refs_5_.refs_0_), channel_id=1, source_target_pairs={{0,16},{16,0},{1,17},{17,1},{2,18},{18,2},{3,19},{19,3},{4,20},{20... | collective-permute-start | bytes 737288 | tf_op jit(solution)/shard_map/ppermute | solution.py:52
  19.4 11.1 %collective-permute-start.3 = (f32[3,10,8,256]{3,2,1,0:T(8,128)S(1)}, f32[3,10,8,256]{3,2,1,0:T(8,128)S(1)}, u32[]{:S(2)}, u32[]{:S(2)}) collective-permute-start(f32[3,10,8,256]{3,2,1,0:T(8,128)S(1)} %gathered.5.refs_5_.refs_0_), channel_id=1, source_target_pairs={{0,2},{1,3},{2,0},{3,1},{4,6},{5,7},{6,4},{7,5},{8,10},{9,11},{10,... | collective-permute-start | bytes 737288 | tf_op jit(solution)/shard_map/ppermute | solution.py:52
  22.6 10.6 %copy-start = (f32[2,2,64,256]{3,2,1,0:T(8,128)S(1)}, f32[2,2,64,256]{3,2,1,0:T(8,128)}, u32[]{:S(2)}) copy-start(f32[2,2,64,256]{3,2,1,0:T(8,128)} %param.13) | copy-start | bytes 786436
  22.6 10.6 %copy-start.1 = (f32[2,2,64,256]{3,2,1,0:T(8,128)S(1)}, f32[2,2,64,256]{3,2,1,0:T(8,128)}, u32[]{:S(2)}) copy-start(f32[2,2,64,256]{3,2,1,0:T(8,128)} %param.15) | copy-start | bytes 786436
  22.6 10.6 %copy-start.2 = (f32[2,64,256]{2,1,0:T(8,128)S(1)}, f32[2,64,256]{2,1,0:T(8,128)}, u32[]{:S(2)}) copy-start(f32[2,64,256]{2,1,0:T(8,128)} %inner_ref.1) | copy-start | bytes 393220
  22.6 7.9 %collective-permute-start.10 = (f32[4,2,32,128]{3,2,1,0:T(8,128)S(1)}, f32[4,2,32,128]{3,2,1,0:T(8,128)S(1)}, u32[]{:S(2)}, u32[]{:S(2)}) collective-permute-start(f32[4,2,32,128]{3,2,1,0:T(8,128)S(1)} %get-tuple-element.31), channel_id=1, source_target_pairs={{0,12},{4,8},{8,4},{12,0},{1,13},{5,9},{9,5},{13,1},{2,14},{6,10},... | collective-permute-start | bytes 393224 | tf_op jit(solution)/shard_map/ppermute | solution.py:52
  30.6 2.6 %collective-permute-start.11 = (f32[12,10,8,256]{3,2,1,0:T(8,128)S(1)}, f32[12,10,8,256]{3,2,1,0:T(8,128)S(1)}, u32[]{:S(2)}, u32[]{:S(2)}) collective-permute-start(f32[12,10,8,256]{3,2,1,0:T(8,128)S(1)} %gathered.7.rest_0_), channel_id=1, source_target_pairs={{0,1},{1,0},{2,3},{3,2},{4,5},{5,4},{6,7},{7,6},{8,9},{9,8},{10,11... | collective-permute-start | bytes 2949128 | tf_op jit(solution)/shard_map/ppermute | solution.py:52
  35.3 4.8 %collective-permute-start.12 = (f32[32,256]{1,0:T(8,128)S(1)}, f32[32,256]{1,0:T(8,128)S(1)}, u32[]{:S(2)}, u32[]{:S(2)}) collective-permute-start(f32[32,256]{1,0:T(8,128)S(1)} %get-tuple-element.36), channel_id=1, source_target_pairs={{0,4},{4,0},{8,12},{12,8},{1,5},{5,1},{9,13},{13,9},{2,6},{6,2},{1... | collective-permute-start | bytes 98312 | tf_op jit(solution)/shard_map/ppermute | solution.py:52
  37.4 5.2 %collective-permute-start.13 = (f32[32,256]{1,0:T(8,128)S(1)}, f32[32,256]{1,0:T(8,128)S(1)}, u32[]{:S(2)}, u32[]{:S(2)}) collective-permute-start(f32[32,256]{1,0:T(8,128)S(1)} %get-tuple-element.37), channel_id=1, source_target_pairs={{0,8},{4,12},{8,0},{12,4},{1,9},{5,13},{9,1},{13,5},{2,10},{6,14},... | collective-permute-start | bytes 98312 | tf_op jit(solution)/shard_map/ppermute | solution.py:52
  38.9 5.7 %collective-permute-start.14 = (f32[32,256]{1,0:T(8,128)S(1)}, f32[32,256]{1,0:T(8,128)S(1)}, u32[]{:S(2)}, u32[]{:S(2)}) collective-permute-start(f32[32,256]{1,0:T(8,128)S(1)} %get-tuple-element.38), channel_id=1, source_target_pairs={{0,12},{4,8},{8,4},{12,0},{1,13},{5,9},{9,5},{13,1},{2,14},{6,10},... | collective-permute-start | bytes 98312 | tf_op jit(solution)/shard_map/ppermute | solution.py:52

commit v5 on v4

--- a/solution.py
+++ b/solution.py
@@ -277,44 +277,35 @@
     )(offsets, far_memory(noise), *(near_core(a) for a in after))
 
 
-def assemble_kernel(ranks, samples, masks, inv_ref, inner_ref, cross_ref, *rest):
-    shares, (high_ref, low_ref, mats) = rest[: len(masks)], rest[len(masks) :]
+def fill(mats, masks, shares):
     row, sample, group = (lax.axis_index(a) for a in ("rows", "samples", "groups"))
-    rows_here = inv_ref.shape[1]
+    ranks, samples = lax.axis_size("rows"), lax.axis_size("samples")
+    rows_here = mats.shape[1] // ranks
     piece = shares[0].shape[2]
-    own = pl.ds(pl.multiple_of(row * rows_here, rows_here), rows_here)
-    mats[0:4, own, :] = inv_ref[...]
-    mats[4:6, own, :] = inner_ref[...]
-    mats[6:10, own, :] = cross_ref[...]
-    for pair, ref in zip(masks, shares):
-        for j, (group_mask, sample_mask) in enumerate(pair):
+    for pairs, ref in zip(masks, shares):
+        for j, (group_mask, sample_mask) in enumerate(pairs):
             part = (group ^ group_mask) * samples + (sample ^ sample_mask)
             for i, k in enumerate((3, 1, 2)):
                 start = (row ^ k) * rows_here + part * piece
                 mats[:, pl.ds(pl.multiple_of(start, piece), piece), :] = ref[3 * j + i]
-    for m in range(10):
-        high_ref[m], low_ref[m] = halves(mats[m])
-
-
-def assemble(inverse, inner, cross, masks, shares, ranks, samples):
-    block = inverse.shape[2]
-    out = pltpu.VMEM((10, block, block), B16)
-    return pl.pallas_call(
-        functools.partial(assemble_kernel, ranks, samples, masks),
-        out_shape=(out, out),
-        in_specs=[VMEM] * (3 + len(shares)),
-        out_specs=(VMEM, VMEM),
-        scratch_shapes=[pltpu.VMEM((10, block, block), F32)],
-        cost_estimate=cost(920000000, 1),
-        compiler_params=params(),
-        name="assemble",
-    )(*(near_core(a) for a in (inverse, inner, cross, *shares)))
-
-
-def solve_kernel(ranks, samples, target_ref, high_ref, low_ref, *refs):
-    (kept_ref, got_ref), outs, (sums, ordered) = refs[:2], refs[2 : 2 + ranks], refs[2 + ranks :]
+
+
+def fill_own(mats, inv_ref, inner_ref, cross_ref):
+    rows_here = inv_ref.shape[1]
+    start = lax.axis_index("rows") * rows_here
+    own = pl.ds(pl.multiple_of(start, rows_here), rows_here)
+    mats[0:4, own, :] = inv_ref[...]
+    mats[4:6, own, :] = inner_ref[...]
+    mats[6:10, own, :] = cross_ref[...]
+
+
+def solve_kernel(ranks, samples, masks, target_ref, *refs):
+    sources, shares, (kept_ref, got_ref) = refs[:3], refs[3:5], refs[5:7]
+    outs, (sums, ordered, mats) = refs[7 : 7 + ranks], refs[7 + ranks :]
+    fill_own(mats, *sources)
+    fill(mats, masks, shares)
     row, sample = lax.axis_index("rows"), lax.axis_index("samples")
-    block = high_ref.shape[1]
+    block = mats.shape[1]
     rows_here = block // ranks
     for i in range(samples):
         sums[sample ^ i] = kept_ref[i] + got_ref[i]
@@ -328,10 +319,10 @@
             rest[p][b] = target_ref[p, :, b * block : (b + 1) * block] - value
 
     def apply(value, m):
-        return stacked(dot_t, value, high_ref[m], low_ref[m])
+        return stacked(dot_t, value, *halves(mats[m]))
 
     def link(value, m):
-        return stacked(dot_n, value, high_ref[m], low_ref[m])
+        return stacked(dot_n, value, *halves(mats[m]))
 
     x11 = apply(rest[1][1], 3)
     x10 = apply(rest[1][0] - link(x11, 5), 2)
@@ -345,23 +336,24 @@
         out[...] = ordered[row ^ k]
 
 
-def solve(target, mats, parts, ranks, samples):
+def solve(target, matrices, masks, shares, parts, ranks, samples):
     quarter = target.shape[1]
-    block = mats[0].shape[1]
+    block = matrices[0].shape[2]
     out = pltpu.VMEM((quarter, 4 * block // ranks), F32)
     return pl.pallas_call(
-        functools.partial(solve_kernel, ranks, samples),
+        functools.partial(solve_kernel, ranks, samples, masks),
         out_shape=(out,) * ranks,
-        in_specs=[VMEM] * 5,
+        in_specs=[VMEM] * 8,
         out_specs=(VMEM,) * ranks,
         scratch_shapes=[
             pltpu.VMEM((samples, 2, quarter, 2 * block // samples), F32),
             pltpu.VMEM((ranks, quarter, 4 * block // ranks), F32),
+            pltpu.VMEM((10, block, block), F32),
         ],
-        cost_estimate=cost(1610000000, 1),
-        compiler_params=params(),
+        compiler_params=params(),
+        cost_estimate=cost(2000000000, 1),
         name="solve",
-    )(*(near_core(a) for a in (target, *mats, *parts)))
+    )(*(near_core(a) for a in (target, *matrices, *shares, *parts)))
 
 
 def place_kernel(ranks, *refs):
@@ -434,9 +426,9 @@
         half_near = exchange(half, "samples", 1, samples)
         shares = (half, half_near)
         masks = (((0, 0), (0, 2), (1, 0), (1, 2)), ((0, 1), (0, 3), (1, 1), (1, 3)))
-        mats = assemble(inverse, inner_link, cross, masks, shares, ranks, samples)
-
-        return place(over_rows(solve(target, mats, (kept, came), ranks, samples)))
+        matrices = (inverse, inner_link, cross)
+        pieces = solve(target, matrices, masks, shares, (kept, came), ranks, samples)
+        return place(over_rows(pieces))
 
     return local
 

time: 45.6 us -> 45 us (0.987)
  Pallas kernels: 8.88 us -> 8.16 us
    pallas_call x2 -> x1, Pallas kernels: 2.11 us -> 1.54 us  [solve(): pl.pallas_call(functools.partial(solve_kernel, ranks, samples, masks), ou...]
where the time goes in v5:
time: 45 us; the launch traced here: 44.9 us
  starting transfers between devices  20.6 us (46%)
  waiting for transfers between devices  15.9 us (35%)
  Pallas kernels  8.16 us (18%)
    ppermute x14, starting transfers between devices, exchange(): return lax.ppermute(array, axis, [(i, i ^ mask) for i in range(size)])  19.1 us
    ppermute x14, waiting for transfers between devices, exchange(): return lax.ppermute(array, axis, [(i, i ^ mask) for i in range(size)])  14.4 us
    pallas_call x1, Pallas kernels, front_rows(): pl.pallas_call(front_kernel, out_shape=(out, out), in_specs=[SMEM, VMEM],...  1.95 us
    pallas_call x1, Pallas kernels, targets(): pl.pallas_call(with_after(target_kernel, 2, after), out_shape=pltpu.VMEM(...  1.8 us
    pallas_call x1, Pallas kernels, solve(): pl.pallas_call(functools.partial(solve_kernel, ranks, samples, masks), ou...  1.54 us
    ppermute x1, waiting for transfers between devices, local(): lax.ppermute(here, ('groups', 'samples'), [(i, i ^ samples + 2) for i in...  1.51 us
    ppermute x1, starting transfers between devices, local(): lax.ppermute(here, ('groups', 'samples'), [(i, i ^ samples + 2) for i in...  1.49 us
    pallas_call x1, Pallas kernels, own_share(): pl.pallas_call(functools.partial(share_kernel, samples), out_shape=(pltpu...  1.13 us
  transfers between devices with their start and end apart: 15, of which 9 were waited for; matrix products, arithmetic and copies ran while one was open for 0% of the time, Pallas kernels for 13%

profile of v5, /device:TPU:0, one launch (start us, length us, event | category | flops | bytes accessed | tf_op | source)
XLA Modules:
  0.0 44.9 jit_solution(15282814742278895198)
XLA Ops:
  0.0 2.9 %collective-permute-start.7 = (f32[2,128,256]{2,1,0:T(8,128)}, f32[2,128,256]{2,1,0:T(8,128)S(1)}, u32[]{:S(2)}, u32[]{:S(2)}) collective-permute-start(f32[2,128,256]{2,1,0:T(8,128)} %bitcast.12), channel_id=1, source_target_pairs={{0,2},{1,3},{2,0},{3,1},{4,6},{5,7},{6,4},{7,5},{8,10},{9,11},{10,... | collective-permute-start | bytes 786440 | tf_op jit(solution)/shard_map/ppermute | solution.py:52
  2.9 1.1 %own_share.1 = (f32[10,8,256]{2,1,0:T(8,128)S(1)}, f32[512,128]{1,0:T(8,128)S(1)}, f32[2,128,256]{2,1,0:T(8,128)S(1)}) custom-call(f32[4,64,256]{2,1,0:T(8,128)} %bitcast.8, f32[2,64,256]{2,1,0:T(8,128)} %refs_1_.5, f32[4,64,256]{2,1,0:T(8,128)} %bitcast.10, f32[512,128]{1,0:T(8,128)} %refs_3_.1, f32[2,128,256]{2,1,0:T(8,128)} %bitcast.13), custom_call_target="tpu_custom_call" | custom-call | flops 1264999936 | bytes 1 | tf_op jit(solution)/shard_map/own_share/pallas_call | solution.py:121
  4.1 3.7 %collective-permute-start = (f32[1,10,8,256]{3,2,1,0:T(8,128)S(1)}, f32[1,10,8,256]{3,2,1,0:T(8,128)S(1)}, u32[]{:S(2)}, u32[]{:S(2)}) collective-permute-start(f32[1,10,8,256]{3,2,1,0:T(8,128)S(1)} %bitcast.6), channel_id=1, source_target_pairs={{0,12},{4,8},{8,4},{12,0},{1,13},{5,9},{9,5},{13,1},{2,14},{6,10},... | collective-permute-start | bytes 245768 | tf_op jit(solution)/shard_map/ppermute | solution.py:52
  7.7 1.9 %front_rows.1 = (bf16[2,128,256]{2,1,0:T(8,128)(2,1)S(1)}, bf16[2,128,256]{2,1,0:T(8,128)(2,1)S(1)}) custom-call(s32[2,256]{1,0:T(2,128)} %map_ref.1, f32[512,128]{1,0:T(8,128)S(1)} %get-tuple-element.21.ancestor_ref), custom_call_target="tpu_custom_call" | custom-call | flops 2300000000 | bytes 1 | tf_op jit(solution)/shard_map/front_rows/pallas_call | solution.py:152
  9.7 0.7 %collective-permute-done.refs_1_.refs_0_ = f32[1,10,8,256]{3,2,1,0:T(8,128)S(1)} collective-permute-done((f32[1,10,8,256]{3,2,1,0:T(8,128)S(1)}, f32[1,10,8,256]{3,2,1,0:T(8,128)S(1)}, u32[]{:S(2)}, u32[]{:S(2)}) %collective-permute-start) | collective-permute-done | bytes 81952 | tf_op jit(solution)/shard_map/ppermute | solution.py:52
  10.5 0.0 copy-start.3
  10.5 1.0 %collective-permute-start.1 = (f32[2,10,8,256]{3,2,1,0:T(8,128)S(1)}, f32[2,10,8,256]{3,2,1,0:T(8,128)S(1)}, u32[]{:S(2)}, u32[]{:S(2)}) collective-permute-start(f32[2,10,8,256]{3,2,1,0:T(8,128)S(1)} %gathered.4.refs_2_.refs_1_), channel_id=1, source_target_pairs={{0,4},{4,0},{8,12},{12,8},{1,5},{5,1},{9,13},{13,9},{2,6},{6,2},{1... | collective-permute-start | bytes 491528 | tf_op jit(solution)/shard_map/ppermute | solution.py:52
  11.5 0.1 collective-permute-start.8
  11.6 1.8 %targets.1.refs_4_.target_ref = f32[2,32,512]{2,1,0:T(8,128)S(1)} custom-call(s32[2]{0:T(128)S(1)} %copy-done.3, f32[2048,128]{1,0:T(8,128)} %refs_1_.4, f32[2,10,8,256]{3,2,1,0:T(8,128)S(1)} %gathered.4.refs_2_.refs_1_), custom_call_target="tpu_custom_call" | custom-call | flops 2070000000 | bytes 1 | tf_op jit(solution)/shard_map/targets/pallas_call | solution.py:264
  13.4 0.4 terms.2
  13.8 1.2 %collective-permute-start.6 = (f32[2,2,2,32,128]{4,3,2,1,0:T(8,128)S(1)}, f32[2,2,2,32,128]{4,3,2,1,0:T(8,128)S(1)}, u32[]{:S(2)}, u32[]{:S(2)}) collective-permute-start(f32[2,2,2,32,128]{4,3,2,1,0:T(8,128)S(1)} %get-tuple-element.25.refs_2_), channel_id=1, source_target_pairs={{0,4},{4,0},{8,12},{12,8},{1,5},{5,1},{9,13},{13,9},{2,6},{6,2},{1... | collective-permute-start | bytes 393224 | tf_op jit(solution)/shard_map/ppermute | solution.py:52
  15.0 1.4 %collective-permute-done.1.refs_1_ = f32[2,10,8,256]{3,2,1,0:T(8,128)S(1)} collective-permute-done((f32[2,10,8,256]{3,2,1,0:T(8,128)S(1)}, f32[2,10,8,256]{3,2,1,0:T(8,128)S(1)}, u32[]{:S(2)}, u32[]{:S(2)}) %collective-permute-start.1) | collective-permute-done | bytes 163872 | tf_op jit(solution)/shard_map/ppermute | solution.py:52
  16.5 0.4 terms.3
  16.9 0.4 collective-permute-start.9
  17.3 1.5 %collective-permute-start.5 = (f32[3,10,8,256]{3,2,1,0:T(8,128)S(1)}, f32[3,10,8,256]{3,2,1,0:T(8,128)S(1)}, u32[]{:S(2)}, u32[]{:S(2)}) collective-permute-start(f32[3,10,8,256]{3,2,1,0:T(8,128)S(1)} %gathered.5.refs_5_.refs_0_), channel_id=1, source_target_pairs={{0,18},{1,19},{2,16},{3,17},{16,2},{17,3},{18,0},{19,1},{4,22},{5,... | collective-permute-start | bytes 737288 | tf_op jit(solution)/shard_map/ppermute | solution.py:418
  18.8 0.5 %collective-permute-start.4 = (f32[3,10,8,256]{3,2,1,0:T(8,128)S(1)}, f32[3,10,8,256]{3,2,1,0:T(8,128)S(1)}, u32[]{:S(2)}, u32[]{:S(2)}) collective-permute-start(f32[3,10,8,256]{3,2,1,0:T(8,128)S(1)} %gathered.5.refs_5_.refs_0_), channel_id=1, source_target_pairs={{0,16},{16,0},{1,17},{17,1},{2,18},{18,2},{3,19},{19,3},{4,20},{20... | collective-permute-start | bytes 737288 | tf_op jit(solution)/shard_map/ppermute | solution.py:52
  19.3 1.5 %collective-permute-start.3 = (f32[3,10,8,256]{3,2,1,0:T(8,128)S(1)}, f32[3,10,8,256]{3,2,1,0:T(8,128)S(1)}, u32[]{:S(2)}, u32[]{:S(2)}) collective-permute-start(f32[3,10,8,256]{3,2,1,0:T(8,128)S(1)} %gathered.5.refs_5_.refs_0_), channel_id=1, source_target_pairs={{0,2},{1,3},{2,0},{3,1},{4,6},{5,7},{6,4},{7,5},{8,10},{9,11},{10,... | collective-permute-start | bytes 737288 | tf_op jit(solution)/shard_map/ppermute | solution.py:52
  20.8 1.8 %collective-permute-done.9.refs_3_ = f32[2,2,2,32,128]{4,3,2,1,0:T(8,128)S(1)} collective-permute-done((f32[2,2,2,32,128]{4,3,2,1,0:T(8,128)S(1)}, f32[2,2,2,32,128]{4,3,2,1,0:T(8,128)S(1)}, u32[]{:S(2)}, u32[]{:S(2)}) %collective-permute-start.9) | collective-permute-done | bytes 131104 | tf_op jit(solution)/shard_map/ppermute | solution.py:52
  22.7 3.0 %collective-permute-start.10 = (f32[4,2,32,128]{3,2,1,0:T(8,128)S(1)}, f32[4,2,32,128]{3,2,1,0:T(8,128)S(1)}, u32[]{:S(2)}, u32[]{:S(2)}) collective-permute-start(f32[4,2,32,128]{3,2,1,0:T(8,128)S(1)} %get-tuple-element.29), channel_id=1, source_target_pairs={{0,12},{4,8},{8,4},{12,0},{1,13},{5,9},{9,5},{13,1},{2,14},{6,10},... | collective-permute-start | bytes 393224 | tf_op jit(solution)/shard_map/ppermute | solution.py:52
  25.6 1.5 %collective-permute-done.5.refs_3_ = f32[3,10,8,256]{3,2,1,0:T(8,128)S(1)} collective-permute-done((f32[3,10,8,256]{3,2,1,0:T(8,128)S(1)}, f32[3,10,8,256]{3,2,1,0:T(8,128)S(1)}, u32[]{:S(2)}, u32[]{:S(2)}) %collective-permute-start.5) | collective-permute-done | bytes 245792 | tf_op jit(solution)/shard_map/ppermute | solution.py:418
  27.1 3.3 %collective-permute-done.4.refs_2_ = f32[3,10,8,256]{3,2,1,0:T(8,128)S(1)} collective-permute-done((f32[3,10,8,256]{3,2,1,0:T(8,128)S(1)}, f32[3,10,8,256]{3,2,1,0:T(8,128)S(1)}, u32[]{:S(2)}, u32[]{:S(2)}) %collective-permute-start.4) | collective-permute-done | bytes 245792 | tf_op jit(solution)/shard_map/ppermute | solution.py:52
  30.4 0.1 collective-permute-done.3.refs_1_
  30.5 0.1 gathered.7.refs_3_
  30.6 0.1 collective-permute-start.11
  30.7 2.6 %collective-permute-done.11.refs_4_ = f32[12,10,8,256]{3,2,1,0:T(8,128)S(1)} collective-permute-done((f32[12,10,8,256]{3,2,1,0:T(8,128)S(1)}, f32[12,10,8,256]{3,2,1,0:T(8,128)S(1)}, u32[]{:S(2)}, u32[]{:S(2)}) %collective-permute-start.11) | collective-permute-done | bytes 983072 | tf_op jit(solution)/shard_map/ppermute | solution.py:52
  33.2 1.5 %solve.1 = (f32[32,256]{1,0:T(8,128)S(1)}, f32[32,256]{1,0:T(8,128)S(1)}, f32[32,256]{1,0:T(8,128)S(1)}, f32[32,256]{1,0:T(8,128)S(1)}) custom-call(f32[2,32,512]{2,1,0:T(8,128)S(1)} %targets.1.refs_4_.target_ref, f32[4,64,256]{2,1,0:T(8,128)S(1)} %bitcast.9, f32[2,64,256]{2,1,0:T(8,128)S(1)} %copy-done.2, f32[4,64,256]{2,1,0:T(8,128)S(1)} %bitcast.11, ...), custom_call_target="tpu_custom_call" | custom-call | flops 2000000000 | bytes 1 | tf_op jit(solution)/shard_map/solve/pallas_call | solution.py:343
  34.8 2.2 %collective-permute-start.12 = (f32[32,256]{1,0:T(8,128)S(1)}, f32[32,256]{1,0:T(8,128)S(1)}, u32[]{:S(2)}, u32[]{:S(2)}) collective-permute-start(f32[32,256]{1,0:T(8,128)S(1)} %get-tuple-element.32), channel_id=1, source_target_pairs={{0,4},{4,0},{8,12},{12,8},{1,5},{5,1},{9,13},{13,9},{2,6},{6,2},{1... | collective-permute-start | bytes 98312 | tf_op jit(solution)/shard_map/ppermute | solution.py:52
  36.9 1.4 %collective-permute-start.13 = (f32[32,256]{1,0:T(8,128)S(1)}, f32[32,256]{1,0:T(8,128)S(1)}, u32[]{:S(2)}, u32[]{:S(2)}) collective-permute-start(f32[32,256]{1,0:T(8,128)S(1)} %get-tuple-element.33), channel_id=1, source_target_pairs={{0,8},{4,12},{8,0},{12,4},{1,9},{5,13},{9,1},{13,5},{2,10},{6,14},... | collective-permute-start | bytes 98312 | tf_op jit(solution)/shard_map/ppermute | solution.py:52
  38.4 1.2 %collective-permute-start.14 = (f32[32,256]{1,0:T(8,128)S(1)}, f32[32,256]{1,0:T(8,128)S(1)}, u32[]{:S(2)}, u32[]{:S(2)}) collective-permute-start(f32[32,256]{1,0:T(8,128)S(1)} %get-tuple-element.34), channel_id=1, source_target_pairs={{0,12},{4,8},{8,4},{12,0},{1,13},{5,9},{9,5},{13,1},{2,14},{6,10},... | collective-permute-start | bytes 98312 | tf_op jit(solution)/shard_map/ppermute | solution.py:52
  39.6 2.7 %collective-permute-done.13.refs_2_ = f32[32,256]{1,0:T(8,128)S(1)} collective-permute-done((f32[32,256]{1,0:T(8,128)S(1)}, f32[32,256]{1,0:T(8,128)S(1)}, u32[]{:S(2)}, u32[]{:S(2)}) %collective-permute-start.13) | collective-permute-done | bytes 32800 | tf_op jit(solution)/shard_map/ppermute | solution.py:52
  42.3 1.8 %collective-permute-done.14.refs_3_ = f32[32,256]{1,0:T(8,128)S(1)} collective-permute-done((f32[32,256]{1,0:T(8,128)S(1)}, f32[32,256]{1,0:T(8,128)S(1)}, u32[]{:S(2)}, u32[]{:S(2)}) %collective-permute-start.14) | collective-permute-done | bytes 32800 | tf_op jit(solution)/shard_map/ppermute | solution.py:52
  44.1 0.8 %place.1 = f32[2,2,64,128]{3,2,1,0:T(8,128)} custom-call(f32[32,256]{1,0:T(8,128)S(1)} %get-tuple-element.31.refs_0_, f32[32,256]{1,0:T(8,128)S(1)} %collective-permute-done.12.refs_1_, f32[32,256]{1,0:T(8,128)S(1)} %collective-permute-done.13.refs_2_, f32[32,256]{1,0:T(8,128)S(1)} %collective-permute-done.14.refs_3_), custom_call_target="tpu_custom_call" | custom-call | flops 920000000 | bytes 1 | tf_op jit(solution)/shard_map/place/pallas_call | solution.py:375
  (18 shorter events, 0.1 us)
Async XLA Ops:
  0.0 11.5 %collective-permute-start.7 = (f32[2,128,256]{2,1,0:T(8,128)}, f32[2,128,256]{2,1,0:T(8,128)S(1)}, u32[]{:S(2)}, u32[]{:S(2)}) collective-permute-start(f32[2,128,256]{2,1,0:T(8,128)} %bitcast.12), channel_id=1, source_target_pairs={{0,2},{1,3},{2,0},{3,1},{4,6},{5,7},{6,4},{7,5},{8,10},{9,11},{10,... | collective-permute-start | bytes 786440 | tf_op jit(solution)/shard_map/ppermute | solution.py:52
  4.1 6.4 %collective-permute-start = (f32[1,10,8,256]{3,2,1,0:T(8,128)S(1)}, f32[1,10,8,256]{3,2,1,0:T(8,128)S(1)}, u32[]{:S(2)}, u32[]{:S(2)}) collective-permute-start(f32[1,10,8,256]{3,2,1,0:T(8,128)S(1)} %bitcast.6), channel_id=1, source_target_pairs={{0,12},{4,8},{8,4},{12,0},{1,13},{5,9},{9,5},{13,1},{2,14},{6,10},... | collective-permute-start | bytes 245768 | tf_op jit(solution)/shard_map/ppermute | solution.py:52
  7.7 5.7 %collective-permute-start.2 = (f32[2,128,256]{2,1,0:T(8,128)S(1)}, f32[2,128,256]{2,1,0:T(8,128)S(1)}, u32[]{:S(2)}, u32[]{:S(2)}) collective-permute-start(f32[2,128,256]{2,1,0:T(8,128)S(1)} %get-tuple-element.24.refs_2_), channel_id=1, source_target_pairs={{0,1},{1,0},{2,3},{3,2},{4,5},{5,4},{6,7},{7,6},{8,9},{9,8},{10,11... | collective-permute-start | bytes 786440 | tf_op jit(solution)/shard_map/ppermute | solution.py:52
  10.5 1.1 %copy-start.3 = (s32[2]{0:T(128)S(1)}, s32[2]{0:T(128)}, u32[]{:S(2)}) copy-start(s32[2]{0:T(128)} %refs_0_.1) | copy-start | bytes 28
  10.5 6.0 %collective-permute-start.1 = (f32[2,10,8,256]{3,2,1,0:T(8,128)S(1)}, f32[2,10,8,256]{3,2,1,0:T(8,128)S(1)}, u32[]{:S(2)}, u32[]{:S(2)}) collective-permute-start(f32[2,10,8,256]{3,2,1,0:T(8,128)S(1)} %gathered.4.refs_2_.refs_1_), channel_id=1, source_target_pairs={{0,4},{4,0},{8,12},{12,8},{1,5},{5,1},{9,13},{13,9},{2,6},{6,2},{1... | collective-permute-start | bytes 491528 | tf_op jit(solution)/shard_map/ppermute | solution.py:52
  11.5 5.0 %collective-permute-start.8 = (f32[2,128,256]{2,1,0:T(8,128)S(1)}, f32[2,128,256]{2,1,0:T(8,128)S(1)}, u32[]{:S(2)}, u32[]{:S(2)}) collective-permute-start(f32[2,128,256]{2,1,0:T(8,128)S(1)} %gathered.6.refs_2_), channel_id=1, source_target_pairs={{0,1},{1,0},{2,3},{3,2},{4,5},{5,4},{6,7},{7,6},{8,9},{9,8},{10,11... | collective-permute-start | bytes 786440 | tf_op jit(solution)/shard_map/ppermute | solution.py:52
  13.8 7.0 %collective-permute-start.6 = (f32[2,2,2,32,128]{4,3,2,1,0:T(8,128)S(1)}, f32[2,2,2,32,128]{4,3,2,1,0:T(8,128)S(1)}, u32[]{:S(2)}, u32[]{:S(2)}) collective-permute-start(f32[2,2,2,32,128]{4,3,2,1,0:T(8,128)S(1)} %get-tuple-element.25.refs_2_), channel_id=1, source_target_pairs={{0,4},{4,0},{8,12},{12,8},{1,5},{5,1},{9,13},{13,9},{2,6},{6,2},{1... | collective-permute-start | bytes 393224 | tf_op jit(solution)/shard_map/ppermute | solution.py:52
  16.9 5.7 %collective-permute-start.9 = (f32[2,2,2,32,128]{4,3,2,1,0:T(8,128)S(1)}, f32[2,2,2,32,128]{4,3,2,1,0:T(8,128)S(1)}, u32[]{:S(2)}, u32[]{:S(2)}) collective-permute-start(f32[2,2,2,32,128]{4,3,2,1,0:T(8,128)S(1)} %get-tuple-element.28), channel_id=1, source_target_pairs={{0,4},{4,0},{8,12},{12,8},{1,5},{5,1},{9,13},{13,9},{2,6},{6,2},{1... | collective-permute-start | bytes 393224 | tf_op jit(solution)/shard_map/ppermute | solution.py:52
  17.3 9.8 %collective-permute-start.5 = (f32[3,10,8,256]{3,2,1,0:T(8,128)S(1)}, f32[3,10,8,256]{3,2,1,0:T(8,128)S(1)}, u32[]{:S(2)}, u32[]{:S(2)}) collective-permute-start(f32[3,10,8,256]{3,2,1,0:T(8,128)S(1)} %gathered.5.refs_5_.refs_0_), channel_id=1, source_target_pairs={{0,18},{1,19},{2,16},{3,17},{16,2},{17,3},{18,0},{19,1},{4,22},{5,... | collective-permute-start | bytes 737288 | tf_op jit(solution)/shard_map/ppermute | solution.py:418
  18.8 11.6 %collective-permute-start.4 = (f32[3,10,8,256]{3,2,1,0:T(8,128)S(1)}, f32[3,10,8,256]{3,2,1,0:T(8,128)S(1)}, u32[]{:S(2)}, u32[]{:S(2)}) collective-permute-start(f32[3,10,8,256]{3,2,1,0:T(8,128)S(1)} %gathered.5.refs_5_.refs_0_), channel_id=1, source_target_pairs={{0,16},{16,0},{1,17},{17,1},{2,18},{18,2},{3,19},{19,3},{4,20},{20... | collective-permute-start | bytes 737288 | tf_op jit(solution)/shard_map/ppermute | solution.py:52
  19.3 11.2 %collective-permute-start.3 = (f32[3,10,8,256]{3,2,1,0:T(8,128)S(1)}, f32[3,10,8,256]{3,2,1,0:T(8,128)S(1)}, u32[]{:S(2)}, u32[]{:S(2)}) collective-permute-start(f32[3,10,8,256]{3,2,1,0:T(8,128)S(1)} %gathered.5.refs_5_.refs_0_), channel_id=1, source_target_pairs={{0,2},{1,3},{2,0},{3,1},{4,6},{5,7},{6,4},{7,5},{8,10},{9,11},{10,... | collective-permute-start | bytes 737288 | tf_op jit(solution)/shard_map/ppermute | solution.py:52
  22.6 10.6 %copy-start = (f32[2,2,64,256]{3,2,1,0:T(8,128)S(1)}, f32[2,2,64,256]{3,2,1,0:T(8,128)}, u32[]{:S(2)}) copy-start(f32[2,2,64,256]{3,2,1,0:T(8,128)} %param.13) | copy-start | bytes 786436
  22.6 10.6 %copy-start.1 = (f32[2,2,64,256]{3,2,1,0:T(8,128)S(1)}, f32[2,2,64,256]{3,2,1,0:T(8,128)}, u32[]{:S(2)}) copy-start(f32[2,2,64,256]{3,2,1,0:T(8,128)} %param.15) | copy-start | bytes 786436
  22.7 10.6 %copy-start.2 = (f32[2,64,256]{2,1,0:T(8,128)S(1)}, f32[2,64,256]{2,1,0:T(8,128)}, u32[]{:S(2)}) copy-start(f32[2,64,256]{2,1,0:T(8,128)} %refs_1_.5) | copy-start | bytes 393220
  22.7 7.8 %collective-permute-start.10 = (f32[4,2,32,128]{3,2,1,0:T(8,128)S(1)}, f32[4,2,32,128]{3,2,1,0:T(8,128)S(1)}, u32[]{:S(2)}, u32[]{:S(2)}) collective-permute-start(f32[4,2,32,128]{3,2,1,0:T(8,128)S(1)} %get-tuple-element.29), channel_id=1, source_target_pairs={{0,12},{4,8},{8,4},{12,0},{1,13},{5,9},{9,5},{13,1},{2,14},{6,10},... | collective-permute-start | bytes 393224 | tf_op jit(solution)/shard_map/ppermute | solution.py:52
  30.6 2.6 %collective-permute-start.11 = (f32[12,10,8,256]{3,2,1,0:T(8,128)S(1)}, f32[12,10,8,256]{3,2,1,0:T(8,128)S(1)}, u32[]{:S(2)}, u32[]{:S(2)}) collective-permute-start(f32[12,10,8,256]{3,2,1,0:T(8,128)S(1)} %gathered.7.refs_3_), channel_id=1, source_target_pairs={{0,1},{1,0},{2,3},{3,2},{4,5},{5,4},{6,7},{7,6},{8,9},{9,8},{10,11... | collective-permute-start | bytes 2949128 | tf_op jit(solution)/shard_map/ppermute | solution.py:52
  34.8 4.8 %collective-permute-start.12 = (f32[32,256]{1,0:T(8,128)S(1)}, f32[32,256]{1,0:T(8,128)S(1)}, u32[]{:S(2)}, u32[]{:S(2)}) collective-permute-start(f32[32,256]{1,0:T(8,128)S(1)} %get-tuple-element.32), channel_id=1, source_target_pairs={{0,4},{4,0},{8,12},{12,8},{1,5},{5,1},{9,13},{13,9},{2,6},{6,2},{1... | collective-permute-start | bytes 98312 | tf_op jit(solution)/shard_map/ppermute | solution.py:52
  36.9 5.3 %collective-permute-start.13 = (f32[32,256]{1,0:T(8,128)S(1)}, f32[32,256]{1,0:T(8,128)S(1)}, u32[]{:S(2)}, u32[]{:S(2)}) collective-permute-start(f32[32,256]{1,0:T(8,128)S(1)} %get-tuple-element.33), channel_id=1, source_target_pairs={{0,8},{4,12},{8,0},{12,4},{1,9},{5,13},{9,1},{13,5},{2,10},{6,14},... | collective-permute-start | bytes 98312 | tf_op jit(solution)/shard_map/ppermute | solution.py:52
  38.4 5.7 %collective-permute-start.14 = (f32[32,256]{1,0:T(8,128)S(1)}, f32[32,256]{1,0:T(8,128)S(1)}, u32[]{:S(2)}, u32[]{:S(2)}) collective-permute-start(f32[32,256]{1,0:T(8,128)S(1)} %get-tuple-element.34), channel_id=1, source_target_pairs={{0,12},{4,8},{8,4},{12,0},{1,13},{5,9},{9,5},{13,1},{2,14},{6,10},... | collective-permute-start | bytes 98312 | tf_op jit(solution)/shard_map/ppermute | solution.py:52

commit v6 on v5

--- a/solution.py
+++ b/solution.py
@@ -299,11 +299,27 @@
     mats[6:10, own, :] = cross_ref[...]
 
 
-def solve_kernel(ranks, samples, masks, target_ref, *refs):
-    sources, shares, (kept_ref, got_ref) = refs[:3], refs[3:5], refs[5:7]
-    outs, (sums, ordered, mats) = refs[7 : 7 + ranks], refs[7 + ranks :]
-    fill_own(mats, *sources)
-    fill(mats, masks, shares)
+def assemble_kernel(masks, inv_ref, inner_ref, cross_ref, share_ref, mats):
+    fill_own(mats, inv_ref, inner_ref, cross_ref)
+    fill(mats, masks, (share_ref,))
+
+
+def assemble(inverse, inner, cross, masks, share):
+    block = inverse.shape[2]
+    return pl.pallas_call(
+        functools.partial(assemble_kernel, masks),
+        out_shape=pltpu.VMEM((10, block, block), F32),
+        in_specs=[VMEM] * 4,
+        out_specs=VMEM,
+        compiler_params=params(),
+        cost_estimate=cost(575000000, 1),
+        name="assemble",
+    )(*(near_core(a) for a in (inverse, inner, cross, share)))
+
+
+def solve_kernel(ranks, samples, masks, target_ref, mats, share_ref, kept_ref, got_ref, *refs):
+    outs, (sums, ordered) = refs[:ranks], refs[ranks + 1 :]
+    fill(mats, masks, (share_ref,))
     row, sample = lax.axis_index("rows"), lax.axis_index("samples")
     block = mats.shape[1]
     rows_here = block // ranks
@@ -336,24 +352,24 @@
         out[...] = ordered[row ^ k]
 
 
-def solve(target, matrices, masks, shares, parts, ranks, samples):
+def solve(target, mats, masks, share, parts, ranks, samples):
     quarter = target.shape[1]
-    block = matrices[0].shape[2]
+    block = mats.shape[1]
     out = pltpu.VMEM((quarter, 4 * block // ranks), F32)
     return pl.pallas_call(
         functools.partial(solve_kernel, ranks, samples, masks),
-        out_shape=(out,) * ranks,
-        in_specs=[VMEM] * 8,
-        out_specs=(VMEM,) * ranks,
+        out_shape=(out,) * ranks + (pltpu.VMEM(mats.shape, F32),),
+        in_specs=[VMEM] * 5,
+        out_specs=(VMEM,) * (ranks + 1),
         scratch_shapes=[
             pltpu.VMEM((samples, 2, quarter, 2 * block // samples), F32),
             pltpu.VMEM((ranks, quarter, 4 * block // ranks), F32),
-            pltpu.VMEM((10, block, block), F32),
         ],
-        compiler_params=params(),
-        cost_estimate=cost(2000000000, 1),
+        input_output_aliases={1: ranks},
+        compiler_params=params(),
+        cost_estimate=cost(1700000000, 1),
         name="solve",
-    )(*(near_core(a) for a in (target, *matrices, *shares, *parts)))
+    )(*(near_core(a) for a in (target, mats, share, *parts)))[:ranks]
 
 
 def place_kernel(ranks, *refs):
@@ -424,10 +440,9 @@
         came = exchange(sent, "rows", 3, ranks)
         half = gathered([here, over_x, over_y, over_xy], (came,))
         half_near = exchange(half, "samples", 1, samples)
-        shares = (half, half_near)
         masks = (((0, 0), (0, 2), (1, 0), (1, 2)), ((0, 1), (0, 3), (1, 1), (1, 3)))
-        matrices = (inverse, inner_link, cross)
-        pieces = solve(target, matrices, masks, shares, (kept, came), ranks, samples)
+        mats = assemble(inverse, inner_link, cross, masks[:1], half)
+        pieces = solve(target, mats, masks[1:], half_near, (kept, came), ranks, samples)
         return place(over_rows(pieces))
 
     return local

time: 45 us -> 44.9 us (level)
  transfers between devices with their start and end apart: 15 -> 15, of which waited for: 9 -> 9; matrix products, arithmetic and copies ran while one was open for 0% -> 0% of each run, Pallas kernels for 13% -> 14%
where the time goes in v6:
time: 44.9 us; the launch traced here: 44.8 us
  starting transfers between devices  20.5 us (46%)
  waiting for transfers between devices  15.8 us (35%)
  Pallas kernels  8.31 us (19%)
    ppermute x14, starting transfers between devices, exchange(): return lax.ppermute(array, axis, [(i, i ^ mask) for i in range(size)])  19 us
    ppermute x14, waiting for transfers between devices, exchange(): return lax.ppermute(array, axis, [(i, i ^ mask) for i in range(size)])  14.2 us
    pallas_call x1, Pallas kernels, front_rows(): pl.pallas_call(front_kernel, out_shape=(out, out), in_specs=[SMEM, VMEM],...  2.08 us
    pallas_call x1, Pallas kernels, targets(): pl.pallas_call(with_after(target_kernel, 2, after), out_shape=pltpu.VMEM(...  1.8 us
    ppermute x1, waiting for transfers between devices, local(): lax.ppermute(here, ('groups', 'samples'), [(i, i ^ samples + 2) for i in...  1.64 us
    ppermute x1, starting transfers between devices, local(): lax.ppermute(here, ('groups', 'samples'), [(i, i ^ samples + 2) for i in...  1.49 us
    pallas_call x1, Pallas kernels, solve(): pl.pallas_call(functools.partial(solve_kernel, ranks, samples, masks), ou...  1.42 us
    pallas_call x1, Pallas kernels, own_share(): pl.pallas_call(functools.partial(share_kernel, samples), out_shape=(pltpu...  1.13 us
  transfers between devices with their start and end apart: 15, of which 9 were waited for; matrix products, arithmetic and copies ran while one was open for 0% of the time, Pallas kernels for 14%

profile of v6, /device:TPU:0, one launch (start us, length us, event | category | flops | bytes accessed | tf_op | source)
XLA Modules:
  0.0 44.8 jit_solution(10700558968827272363)
XLA Ops:
  0.0 2.9 %collective-permute-start.7 = (f32[2,128,256]{2,1,0:T(8,128)}, f32[2,128,256]{2,1,0:T(8,128)S(1)}, u32[]{:S(2)}, u32[]{:S(2)}) collective-permute-start(f32[2,128,256]{2,1,0:T(8,128)} %bitcast.12), channel_id=1, source_target_pairs={{0,2},{1,3},{2,0},{3,1},{4,6},{5,7},{6,4},{7,5},{8,10},{9,11},{10,... | collective-permute-start | bytes 786440 | tf_op jit(solution)/shard_map/ppermute | solution.py:52
  2.9 1.1 %own_share.1 = (f32[10,8,256]{2,1,0:T(8,128)S(1)}, f32[512,128]{1,0:T(8,128)S(1)}, f32[2,128,256]{2,1,0:T(8,128)S(1)}) custom-call(f32[4,64,256]{2,1,0:T(8,128)} %bitcast.6, f32[2,64,256]{2,1,0:T(8,128)} %inner_ref.1, f32[4,64,256]{2,1,0:T(8,128)} %bitcast.8, f32[512,128]{1,0:T(8,128)} %refs_3_.1, f32[2,128,256]{2,1,0:T(8,128)} %bitcast.13), custom_call_target="tpu_custom_call" | custom-call | flops 1264999936 | bytes 1 | tf_op jit(solution)/shard_map/own_share/pallas_call | solution.py:121
  4.1 3.7 %collective-permute-start = (f32[1,10,8,256]{3,2,1,0:T(8,128)S(1)}, f32[1,10,8,256]{3,2,1,0:T(8,128)S(1)}, u32[]{:S(2)}, u32[]{:S(2)}) collective-permute-start(f32[1,10,8,256]{3,2,1,0:T(8,128)S(1)} %bitcast.10), channel_id=1, source_target_pairs={{0,12},{4,8},{8,4},{12,0},{1,13},{5,9},{9,5},{13,1},{2,14},{6,10},... | collective-permute-start | bytes 245768 | tf_op jit(solution)/shard_map/ppermute | solution.py:52
  7.7 2.1 %front_rows.1 = (bf16[2,128,256]{2,1,0:T(8,128)(2,1)S(1)}, bf16[2,128,256]{2,1,0:T(8,128)(2,1)S(1)}) custom-call(s32[2,256]{1,0:T(2,128)} %map_ref.1, f32[512,128]{1,0:T(8,128)S(1)} %get-tuple-element.21.ancestor_ref), custom_call_target="tpu_custom_call" | custom-call | flops 2300000000 | bytes 1 | tf_op jit(solution)/shard_map/front_rows/pallas_call | solution.py:152
  9.8 0.6 %collective-permute-done.refs_1_.refs_0_ = f32[1,10,8,256]{3,2,1,0:T(8,128)S(1)} collective-permute-done((f32[1,10,8,256]{3,2,1,0:T(8,128)S(1)}, f32[1,10,8,256]{3,2,1,0:T(8,128)S(1)}, u32[]{:S(2)}, u32[]{:S(2)}) %collective-permute-start) | collective-permute-done | bytes 81952 | tf_op jit(solution)/shard_map/ppermute | solution.py:52
  10.5 1.0 %collective-permute-start.1 = (f32[2,10,8,256]{3,2,1,0:T(8,128)S(1)}, f32[2,10,8,256]{3,2,1,0:T(8,128)S(1)}, u32[]{:S(2)}, u32[]{:S(2)}) collective-permute-start(f32[2,10,8,256]{3,2,1,0:T(8,128)S(1)} %gathered.4.refs_2_.refs_1_), channel_id=1, source_target_pairs={{0,4},{4,0},{8,12},{12,8},{1,5},{5,1},{9,13},{13,9},{2,6},{6,2},{1... | collective-permute-start | bytes 491528 | tf_op jit(solution)/shard_map/ppermute | solution.py:52
  11.5 0.1 collective-permute-start.8
  11.6 1.8 %targets.1.refs_4_.target_ref = f32[2,32,512]{2,1,0:T(8,128)S(1)} custom-call(s32[2]{0:T(128)S(1)} %copy-done.3, f32[2048,128]{1,0:T(8,128)} %refs_1_.3, f32[2,10,8,256]{3,2,1,0:T(8,128)S(1)} %gathered.4.refs_2_.refs_1_), custom_call_target="tpu_custom_call" | custom-call | flops 2070000000 | bytes 1 | tf_op jit(solution)/shard_map/targets/pallas_call | solution.py:264
  13.4 0.4 terms.2
  13.8 1.2 %collective-permute-start.6 = (f32[2,2,2,32,128]{4,3,2,1,0:T(8,128)S(1)}, f32[2,2,2,32,128]{4,3,2,1,0:T(8,128)S(1)}, u32[]{:S(2)}, u32[]{:S(2)}) collective-permute-start(f32[2,2,2,32,128]{4,3,2,1,0:T(8,128)S(1)} %get-tuple-element.25.refs_2_), channel_id=1, source_target_pairs={{0,4},{4,0},{8,12},{12,8},{1,5},{5,1},{9,13},{13,9},{2,6},{6,2},{1... | collective-permute-start | bytes 393224 | tf_op jit(solution)/shard_map/ppermute | solution.py:52
  15.0 1.6 %collective-permute-done.1.refs_1_ = f32[2,10,8,256]{3,2,1,0:T(8,128)S(1)} collective-permute-done((f32[2,10,8,256]{3,2,1,0:T(8,128)S(1)}, f32[2,10,8,256]{3,2,1,0:T(8,128)S(1)}, u32[]{:S(2)}, u32[]{:S(2)}) %collective-permute-start.1) | collective-permute-done | bytes 163872 | tf_op jit(solution)/shard_map/ppermute | solution.py:52
  16.6 0.4 terms.3
  17.0 0.3 collective-permute-start.9
  17.4 1.5 %collective-permute-start.5 = (f32[3,10,8,256]{3,2,1,0:T(8,128)S(1)}, f32[3,10,8,256]{3,2,1,0:T(8,128)S(1)}, u32[]{:S(2)}, u32[]{:S(2)}) collective-permute-start(f32[3,10,8,256]{3,2,1,0:T(8,128)S(1)} %gathered.5.refs_5_.refs_0_), channel_id=1, source_target_pairs={{0,18},{1,19},{2,16},{3,17},{16,2},{17,3},{18,0},{19,1},{4,22},{5,... | collective-permute-start | bytes 737288 | tf_op jit(solution)/shard_map/ppermute | solution.py:434
  18.9 0.5 %collective-permute-start.4 = (f32[3,10,8,256]{3,2,1,0:T(8,128)S(1)}, f32[3,10,8,256]{3,2,1,0:T(8,128)S(1)}, u32[]{:S(2)}, u32[]{:S(2)}) collective-permute-start(f32[3,10,8,256]{3,2,1,0:T(8,128)S(1)} %gathered.5.refs_5_.refs_0_), channel_id=1, source_target_pairs={{0,16},{16,0},{1,17},{17,1},{2,18},{18,2},{3,19},{19,3},{4,20},{20... | collective-permute-start | bytes 737288 | tf_op jit(solution)/shard_map/ppermute | solution.py:52
  19.4 1.5 %collective-permute-start.3 = (f32[3,10,8,256]{3,2,1,0:T(8,128)S(1)}, f32[3,10,8,256]{3,2,1,0:T(8,128)S(1)}, u32[]{:S(2)}, u32[]{:S(2)}) collective-permute-start(f32[3,10,8,256]{3,2,1,0:T(8,128)S(1)} %gathered.5.refs_5_.refs_0_), channel_id=1, source_target_pairs={{0,2},{1,3},{2,0},{3,1},{4,6},{5,7},{6,4},{7,5},{8,10},{9,11},{10,... | collective-permute-start | bytes 737288 | tf_op jit(solution)/shard_map/ppermute | solution.py:52
  20.9 1.7 %collective-permute-done.9.refs_3_ = f32[2,2,2,32,128]{4,3,2,1,0:T(8,128)S(1)} collective-permute-done((f32[2,2,2,32,128]{4,3,2,1,0:T(8,128)S(1)}, f32[2,2,2,32,128]{4,3,2,1,0:T(8,128)S(1)}, u32[]{:S(2)}, u32[]{:S(2)}) %collective-permute-start.9) | collective-permute-done | bytes 131104 | tf_op jit(solution)/shard_map/ppermute | solution.py:52
  22.6 3.0 %collective-permute-start.10 = (f32[4,2,32,128]{3,2,1,0:T(8,128)S(1)}, f32[4,2,32,128]{3,2,1,0:T(8,128)S(1)}, u32[]{:S(2)}, u32[]{:S(2)}) collective-permute-start(f32[4,2,32,128]{3,2,1,0:T(8,128)S(1)} %get-tuple-element.29), channel_id=1, source_target_pairs={{0,12},{4,8},{8,4},{12,0},{1,13},{5,9},{9,5},{13,1},{2,14},{6,10},... | collective-permute-start | bytes 393224 | tf_op jit(solution)/shard_map/ppermute | solution.py:52
  25.6 1.6 %collective-permute-done.5.refs_3_ = f32[3,10,8,256]{3,2,1,0:T(8,128)S(1)} collective-permute-done((f32[3,10,8,256]{3,2,1,0:T(8,128)S(1)}, f32[3,10,8,256]{3,2,1,0:T(8,128)S(1)}, u32[]{:S(2)}, u32[]{:S(2)}) %collective-permute-start.5) | collective-permute-done | bytes 245792 | tf_op jit(solution)/shard_map/ppermute | solution.py:434
  27.2 3.2 %collective-permute-done.4.refs_2_ = f32[3,10,8,256]{3,2,1,0:T(8,128)S(1)} collective-permute-done((f32[3,10,8,256]{3,2,1,0:T(8,128)S(1)}, f32[3,10,8,256]{3,2,1,0:T(8,128)S(1)}, u32[]{:S(2)}, u32[]{:S(2)}) %collective-permute-start.4) | collective-permute-done | bytes 245792 | tf_op jit(solution)/shard_map/ppermute | solution.py:52
  30.4 0.1 collective-permute-done.3.refs_1_
  30.5 0.1 gathered.7.share_ref
  30.6 0.1 collective-permute-start.11
  30.7 0.1 assemble.1.mats
  30.9 2.4 %collective-permute-done.11.share_ref = f32[12,10,8,256]{3,2,1,0:T(8,128)S(1)} collective-permute-done((f32[12,10,8,256]{3,2,1,0:T(8,128)S(1)}, f32[12,10,8,256]{3,2,1,0:T(8,128)S(1)}, u32[]{:S(2)}, u32[]{:S(2)}) %collective-permute-start.11) | collective-permute-done | bytes 983072 | tf_op jit(solution)/shard_map/ppermute | solution.py:52
  33.2 1.4 %solve.1 = (f32[32,256]{1,0:T(8,128)S(1)}, f32[32,256]{1,0:T(8,128)S(1)}, f32[32,256]{1,0:T(8,128)S(1)}, f32[32,256]{1,0:T(8,128)S(1)}, f32[10,256,256]{2,1,0:T(8,128)S(1)}) custom-call(f32[2,32,512]{2,1,0:T(8,128)S(1)} %targets.1.refs_4_.target_ref, f32[10,256,256]{2,1,0:T(8,128)S(1)} %assemble.1.mats, ...), custom_call_target="tpu_custom_call", output_to_operand_aliasing={{4}: (1, {})} | custom-call | flops 1700000000 | bytes 1 | tf_op jit(solution)/shard_map/solve/pallas_call | solution.py:359
  34.7 1.9 %collective-permute-start.12 = (f32[32,256]{1,0:T(8,128)S(1)}, f32[32,256]{1,0:T(8,128)S(1)}, u32[]{:S(2)}, u32[]{:S(2)}) collective-permute-start(f32[32,256]{1,0:T(8,128)S(1)} %get-tuple-element.32), channel_id=1, source_target_pairs={{0,4},{4,0},{8,12},{12,8},{1,5},{5,1},{9,13},{13,9},{2,6},{6,2},{1... | collective-permute-start | bytes 98312 | tf_op jit(solution)/shard_map/ppermute | solution.py:52
  36.6 1.7 %collective-permute-start.13 = (f32[32,256]{1,0:T(8,128)S(1)}, f32[32,256]{1,0:T(8,128)S(1)}, u32[]{:S(2)}, u32[]{:S(2)}) collective-permute-start(f32[32,256]{1,0:T(8,128)S(1)} %get-tuple-element.33), channel_id=1, source_target_pairs={{0,8},{4,12},{8,0},{12,4},{1,9},{5,13},{9,1},{13,5},{2,10},{6,14},... | collective-permute-start | bytes 98312 | tf_op jit(solution)/shard_map/ppermute | solution.py:52
  38.3 1.2 %collective-permute-start.14 = (f32[32,256]{1,0:T(8,128)S(1)}, f32[32,256]{1,0:T(8,128)S(1)}, u32[]{:S(2)}, u32[]{:S(2)}) collective-permute-start(f32[32,256]{1,0:T(8,128)S(1)} %get-tuple-element.34), channel_id=1, source_target_pairs={{0,12},{4,8},{8,4},{12,0},{1,13},{5,9},{9,5},{13,1},{2,14},{6,10},... | collective-permute-start | bytes 98312 | tf_op jit(solution)/shard_map/ppermute | solution.py:52
  39.4 2.3 %collective-permute-done.13.refs_2_ = f32[32,256]{1,0:T(8,128)S(1)} collective-permute-done((f32[32,256]{1,0:T(8,128)S(1)}, f32[32,256]{1,0:T(8,128)S(1)}, u32[]{:S(2)}, u32[]{:S(2)}) %collective-permute-start.13) | collective-permute-done | bytes 32800 | tf_op jit(solution)/shard_map/ppermute | solution.py:52
  41.8 2.2 %collective-permute-done.14.refs_3_ = f32[32,256]{1,0:T(8,128)S(1)} collective-permute-done((f32[32,256]{1,0:T(8,128)S(1)}, f32[32,256]{1,0:T(8,128)S(1)}, u32[]{:S(2)}, u32[]{:S(2)}) %collective-permute-start.14) | collective-permute-done | bytes 32800 | tf_op jit(solution)/shard_map/ppermute | solution.py:52
  44.0 0.8 %place.1 = f32[2,2,64,128]{3,2,1,0:T(8,128)} custom-call(f32[32,256]{1,0:T(8,128)S(1)} %get-tuple-element.31.refs_0_, f32[32,256]{1,0:T(8,128)S(1)} %collective-permute-done.12.refs_1_, f32[32,256]{1,0:T(8,128)S(1)} %collective-permute-done.13.refs_2_, f32[32,256]{1,0:T(8,128)S(1)} %collective-permute-done.14.refs_3_), custom_call_target="tpu_custom_call" | custom-call | flops 920000000 | bytes 1 | tf_op jit(solution)/shard_map/place/pallas_call | solution.py:391
  (19 shorter events, 0.1 us)
Async XLA Ops:
  0.0 11.5 %collective-permute-start.7 = (f32[2,128,256]{2,1,0:T(8,128)}, f32[2,128,256]{2,1,0:T(8,128)S(1)}, u32[]{:S(2)}, u32[]{:S(2)}) collective-permute-start(f32[2,128,256]{2,1,0:T(8,128)} %bitcast.12), channel_id=1, source_target_pairs={{0,2},{1,3},{2,0},{3,1},{4,6},{5,7},{6,4},{7,5},{8,10},{9,11},{10,... | collective-permute-start | bytes 786440 | tf_op jit(solution)/shard_map/ppermute | solution.py:52
  4.1 6.4 %collective-permute-start = (f32[1,10,8,256]{3,2,1,0:T(8,128)S(1)}, f32[1,10,8,256]{3,2,1,0:T(8,128)S(1)}, u32[]{:S(2)}, u32[]{:S(2)}) collective-permute-start(f32[1,10,8,256]{3,2,1,0:T(8,128)S(1)} %bitcast.10), channel_id=1, source_target_pairs={{0,12},{4,8},{8,4},{12,0},{1,13},{5,9},{9,5},{13,1},{2,14},{6,10},... | collective-permute-start | bytes 245768 | tf_op jit(solution)/shard_map/ppermute | solution.py:52
  7.7 5.6 %collective-permute-start.2 = (f32[2,128,256]{2,1,0:T(8,128)S(1)}, f32[2,128,256]{2,1,0:T(8,128)S(1)}, u32[]{:S(2)}, u32[]{:S(2)}) collective-permute-start(f32[2,128,256]{2,1,0:T(8,128)S(1)} %get-tuple-element.24.refs_2_), channel_id=1, source_target_pairs={{0,1},{1,0},{2,3},{3,2},{4,5},{5,4},{6,7},{7,6},{8,9},{9,8},{10,11... | collective-permute-start | bytes 786440 | tf_op jit(solution)/shard_map/ppermute | solution.py:52
  7.7 3.8 %copy-start.3 = (s32[2]{0:T(128)S(1)}, s32[2]{0:T(128)}, u32[]{:S(2)}) copy-start(s32[2]{0:T(128)} %refs_0_.1) | copy-start | bytes 28
  10.5 6.1 %collective-permute-start.1 = (f32[2,10,8,256]{3,2,1,0:T(8,128)S(1)}, f32[2,10,8,256]{3,2,1,0:T(8,128)S(1)}, u32[]{:S(2)}, u32[]{:S(2)}) collective-permute-start(f32[2,10,8,256]{3,2,1,0:T(8,128)S(1)} %gathered.4.refs_2_.refs_1_), channel_id=1, source_target_pairs={{0,4},{4,0},{8,12},{12,8},{1,5},{5,1},{9,13},{13,9},{2,6},{6,2},{1... | collective-permute-start | bytes 491528 | tf_op jit(solution)/shard_map/ppermute | solution.py:52
  11.5 5.1 %collective-permute-start.8 = (f32[2,128,256]{2,1,0:T(8,128)S(1)}, f32[2,128,256]{2,1,0:T(8,128)S(1)}, u32[]{:S(2)}, u32[]{:S(2)}) collective-permute-start(f32[2,128,256]{2,1,0:T(8,128)S(1)} %gathered.6.refs_2_), channel_id=1, source_target_pairs={{0,1},{1,0},{2,3},{3,2},{4,5},{5,4},{6,7},{7,6},{8,9},{9,8},{10,11... | collective-permute-start | bytes 786440 | tf_op jit(solution)/shard_map/ppermute | solution.py:52
  13.8 7.1 %collective-permute-start.6 = (f32[2,2,2,32,128]{4,3,2,1,0:T(8,128)S(1)}, f32[2,2,2,32,128]{4,3,2,1,0:T(8,128)S(1)}, u32[]{:S(2)}, u32[]{:S(2)}) collective-permute-start(f32[2,2,2,32,128]{4,3,2,1,0:T(8,128)S(1)} %get-tuple-element.25.refs_2_), channel_id=1, source_target_pairs={{0,4},{4,0},{8,12},{12,8},{1,5},{5,1},{9,13},{13,9},{2,6},{6,2},{1... | collective-permute-start | bytes 393224 | tf_op jit(solution)/shard_map/ppermute | solution.py:52
  16.6 14.1 %copy-start = (f32[2,2,64,256]{3,2,1,0:T(8,128)S(1)}, f32[2,2,64,256]{3,2,1,0:T(8,128)}, u32[]{:S(2)}) copy-start(f32[2,2,64,256]{3,2,1,0:T(8,128)} %param.13) | copy-start | bytes 786436
  16.6 14.1 %copy-start.1 = (f32[2,2,64,256]{3,2,1,0:T(8,128)S(1)}, f32[2,2,64,256]{3,2,1,0:T(8,128)}, u32[]{:S(2)}) copy-start(f32[2,2,64,256]{3,2,1,0:T(8,128)} %param.15) | copy-start | bytes 786436
  16.6 14.1 %copy-start.2 = (f32[2,64,256]{2,1,0:T(8,128)S(1)}, f32[2,64,256]{2,1,0:T(8,128)}, u32[]{:S(2)}) copy-start(f32[2,64,256]{2,1,0:T(8,128)} %inner_ref.1) | copy-start | bytes 393220
  17.0 5.5 %collective-permute-start.9 = (f32[2,2,2,32,128]{4,3,2,1,0:T(8,128)S(1)}, f32[2,2,2,32,128]{4,3,2,1,0:T(8,128)S(1)}, u32[]{:S(2)}, u32[]{:S(2)}) collective-permute-start(f32[2,2,2,32,128]{4,3,2,1,0:T(8,128)S(1)} %get-tuple-element.28), channel_id=1, source_target_pairs={{0,4},{4,0},{8,12},{12,8},{1,5},{5,1},{9,13},{13,9},{2,6},{6,2},{1... | collective-permute-start | bytes 393224 | tf_op jit(solution)/shard_map/ppermute | solution.py:52
  17.4 9.8 %collective-permute-start.5 = (f32[3,10,8,256]{3,2,1,0:T(8,128)S(1)}, f32[3,10,8,256]{3,2,1,0:T(8,128)S(1)}, u32[]{:S(2)}, u32[]{:S(2)}) collective-permute-start(f32[3,10,8,256]{3,2,1,0:T(8,128)S(1)} %gathered.5.refs_5_.refs_0_), channel_id=1, source_target_pairs={{0,18},{1,19},{2,16},{3,17},{16,2},{17,3},{18,0},{19,1},{4,22},{5,... | collective-permute-start | bytes 737288 | tf_op jit(solution)/shard_map/ppermute | solution.py:434
  18.9 11.6 %collective-permute-start.4 = (f32[3,10,8,256]{3,2,1,0:T(8,128)S(1)}, f32[3,10,8,256]{3,2,1,0:T(8,128)S(1)}, u32[]{:S(2)}, u32[]{:S(2)}) collective-permute-start(f32[3,10,8,256]{3,2,1,0:T(8,128)S(1)} %gathered.5.refs_5_.refs_0_), channel_id=1, source_target_pairs={{0,16},{16,0},{1,17},{17,1},{2,18},{18,2},{3,19},{19,3},{4,20},{20... | collective-permute-start | bytes 737288 | tf_op jit(solution)/shard_map/ppermute | solution.py:52
  19.4 11.1 %collective-permute-start.3 = (f32[3,10,8,256]{3,2,1,0:T(8,128)S(1)}, f32[3,10,8,256]{3,2,1,0:T(8,128)S(1)}, u32[]{:S(2)}, u32[]{:S(2)}) collective-permute-start(f32[3,10,8,256]{3,2,1,0:T(8,128)S(1)} %gathered.5.refs_5_.refs_0_), channel_id=1, source_target_pairs={{0,2},{1,3},{2,0},{3,1},{4,6},{5,7},{6,4},{7,5},{8,10},{9,11},{10,... | collective-permute-start | bytes 737288 | tf_op jit(solution)/shard_map/ppermute | solution.py:52
  22.6 7.9 %collective-permute-start.10 = (f32[4,2,32,128]{3,2,1,0:T(8,128)S(1)}, f32[4,2,32,128]{3,2,1,0:T(8,128)S(1)}, u32[]{:S(2)}, u32[]{:S(2)}) collective-permute-start(f32[4,2,32,128]{3,2,1,0:T(8,128)S(1)} %get-tuple-element.29), channel_id=1, source_target_pairs={{0,12},{4,8},{8,4},{12,0},{1,13},{5,9},{9,5},{13,1},{2,14},{6,10},... | collective-permute-start | bytes 393224 | tf_op jit(solution)/shard_map/ppermute | solution.py:52
  30.6 2.6 %collective-permute-start.11 = (f32[12,10,8,256]{3,2,1,0:T(8,128)S(1)}, f32[12,10,8,256]{3,2,1,0:T(8,128)S(1)}, u32[]{:S(2)}, u32[]{:S(2)}) collective-permute-start(f32[12,10,8,256]{3,2,1,0:T(8,128)S(1)} %gathered.7.share_ref), channel_id=1, source_target_pairs={{0,1},{1,0},{2,3},{3,2},{4,5},{5,4},{6,7},{7,6},{8,9},{9,8},{10,11... | collective-permute-start | bytes 2949128 | tf_op jit(solution)/shard_map/ppermute | solution.py:52
  34.7 4.8 %collective-permute-start.12 = (f32[32,256]{1,0:T(8,128)S(1)}, f32[32,256]{1,0:T(8,128)S(1)}, u32[]{:S(2)}, u32[]{:S(2)}) collective-permute-start(f32[32,256]{1,0:T(8,128)S(1)} %get-tuple-element.32), channel_id=1, source_target_pairs={{0,4},{4,0},{8,12},{12,8},{1,5},{5,1},{9,13},{13,9},{2,6},{6,2},{1... | collective-permute-start | bytes 98312 | tf_op jit(solution)/shard_map/ppermute | solution.py:52
  36.6 5.2 %collective-permute-start.13 = (f32[32,256]{1,0:T(8,128)S(1)}, f32[32,256]{1,0:T(8,128)S(1)}, u32[]{:S(2)}, u32[]{:S(2)}) collective-permute-start(f32[32,256]{1,0:T(8,128)S(1)} %get-tuple-element.33), channel_id=1, source_target_pairs={{0,8},{4,12},{8,0},{12,4},{1,9},{5,13},{9,1},{13,5},{2,10},{6,14},... | collective-permute-start | bytes 98312 | tf_op jit(solution)/shard_map/ppermute | solution.py:52
  38.3 5.7 %collective-permute-start.14 = (f32[32,256]{1,0:T(8,128)S(1)}, f32[32,256]{1,0:T(8,128)S(1)}, u32[]{:S(2)}, u32[]{:S(2)}) collective-permute-start(f32[32,256]{1,0:T(8,128)S(1)} %get-tuple-element.34), channel_id=1, source_target_pairs={{0,12},{4,8},{8,4},{12,0},{1,13},{5,9},{9,5},{13,1},{2,14},{6,10},... | collective-permute-start | bytes 98312 | tf_op jit(solution)/shard_map/ppermute | solution.py:52
